TPU v7x, 32 devices: a whole 2x2x4 slice. The times are simulated.
32 devices in a mesh: gx: 8 (over y, x, core), gy: 4 (over z).
Axes of the slice: x: 2, y: 2, z: 4, core: 2. Of those that a mesh axis runs over, the one named last changes fastest.
Arguments:
- estimate: float32 [32, 128, 512], P(None, 'gx', 'gy'), may hold values from 0.5 to 2
- stored: bfloat16 [4096, 16, 128], P(('gx', 'gy')), may hold values from 0.19921875 to 5
- placement: int32 [4096], replicated, may hold values from 0 to 4095, as said below
- psf_taps: float32 [48, 31], replicated, may hold values from 0.05 to 1
- kernel_index: int32 [8, 4, 4, 3], replicated, may hold values from 0 to 47
Outputs:
- refined: float32 [32, 128, 512], P(None, 'gx', 'gy')
Inputs may be any that keep to these rules, and one draw needn't show every extreme that they name: `placement`: each value occurs once; the value b * 128 + v * 32 + z marks plane z of view v of brick b. Entries d * 128 to (d + 1) * 128 - 1 are the slots of device d of gx+gy; among them at most 8 name any one brick, every device has exactly 8 naming some brick, and every brick has exactly 8 on some device.
All inputs are finite; a program needn't handle non-finite values.
Results may differ from a plain program's by a relative error of at most 0.0003.
Values may be sent and summed in bfloat16 or wider, within the bound.
No kernel may reach another device: no remote copies, remote signals or barrier semaphores. Data moves between devices by JAX's collectives and lax.ppermute only.
A program may use at most 128 MiB of HBM per device.

v0:
```python
import functools

import jax
import jax.numpy as jnp
from jax import lax
from jax.experimental import pallas as pl
from jax.experimental.pallas import tpu as pltpu
from jax.sharding import PartitionSpec as P

f32 = jnp.float32
bf16 = jnp.bfloat16
i32 = jnp.int32

NZ = 32
BX = 16
BY = 128
V = 4
TAPS = 31
RADIUS = 15
FIELD = BX * NZ
STRIP = 16
LANES = 128
ROLES = 3


def iota(shape, axis):
    return lax.broadcasted_iota(i32, shape, axis)


def one_hot(mask):
    return jnp.where(mask, 1.0, 0.0).astype(bf16)


def split(a):
    hi = a.astype(bf16)
    return hi, (a - hi.astype(f32)).astype(bf16)


def dot(a, b):
    return jnp.dot(a, b, preferred_element_type=f32)


def earlier(count):
    return one_hot(iota((count, count), 0) < iota((count, count), 1))


def route_kernel(cap, target_ref, stored_ref, out_ref):
    rows, slots = out_ref.shape[0], stored_ref.shape[0]
    place = iota((rows, slots), 0) - target_ref[...] * cap
    marked = jnp.logical_and(place >= 0, place < cap)
    rank = dot(one_hot(marked), earlier(slots))
    chosen = one_hot(jnp.logical_and(marked, rank == place.astype(f32)))
    out_ref[...] = dot(chosen, stored_ref[...]).astype(bf16)


def arrival_kernel(cap, me_ref, slots_ref, out_ref):
    rows, slots = slots_ref.shape
    item = slots_ref[...] - me_ref[0] * slots
    wanted = jnp.logical_and(item >= 0, item < slots)
    rank = dot(one_hot(wanted), earlier(slots))
    order = jnp.bitwise_and(iota((rows, slots), 0), cap - 1)
    found = jnp.logical_and(wanted, rank == order.astype(f32))
    item_of = jnp.sum(jnp.where(found, item + 1, 0).astype(f32), axis=1, keepdims=True) - 1.0
    table = jnp.where(item_of == iota((rows, slots), 1).astype(f32), 1.0, 0.0)
    out_ref[...] = table.T.astype(bf16)


def toeplitz(row, count):
    spread = jnp.broadcast_to(row, (count, LANES))
    return pltpu.roll(spread, LANES - RADIUS, 1, stride=1, stride_axis=0)


def expand(table, selector):
    first = table.astype(bf16)
    rest = table - first.astype(f32)
    second = rest.astype(bf16)
    third = (rest - second.astype(f32)).astype(bf16)
    return dot(first, selector) + dot(second, selector) + dot(third, selector)


def selectors(width, count):
    lane = iota((LANES, width * count), 1)
    row = iota((LANES, width * count), 0)
    each = one_hot(row == jnp.right_shift(lane, width.bit_length() - 1))
    tiled = one_hot(row == jnp.bitwise_and(lane, width - 1))
    return each, tiled


def row_of(xr, yr, view, axis):
    return ((xr * ROLES + yr) * V + view) * 3 + axis


def kron_rows(out, outer, inner, count, width):
    for i in range(count):
        out[i * width : (i + 1) * width, :] = (inner * outer[i : i + 1, :]).astype(bf16)


def stack3(table):
    hi, lo = split(table)
    return jnp.concatenate([hi, hi, lo], axis=0)


def lanes3(table, width):
    inside = iota(table.shape, 1) < width
    kept = jnp.where(inside, table, 0.0)
    hi, lo = split(kept)
    hi, lo = hi.astype(f32), lo.astype(f32)
    return (hi + pltpu.roll(lo, width, 1) + pltpu.roll(hi, 2 * width, 1)).astype(bf16)


def banded_y(row):
    table = toeplitz(row, BY)
    off = iota((BY, BY), 0) - iota((BY, BY), 1)
    return jnp.where(jnp.abs(off) <= RADIUS, table, 0.0)


def build_forward_kernel(taps_ref, back_ref, k_ref, y_ref, xy_ref, z_ref):
    each, tiled = selectors(NZ, BX)
    each16, tiled16 = selectors(STRIP, BX)
    for xr in range(ROLES):
        for v in range(V):
            def fwd(yr, e):
                r = row_of(xr, yr, v, e)
                return taps_ref[r : r + 1, :]

            def bwd(yr, e):
                r = row_of(xr, yr, v, e)
                return back_ref[r : r + 1, :]

            outer = expand(toeplitz(fwd(0, 0), BX), each)
            inner = expand(toeplitz(fwd(0, 2), NZ), tiled)
            kron_rows(k_ref.at[xr, v], outer, inner, BX, NZ)
            y_ref[xr, :, v * BY : (v + 1) * BY] = stack3(banded_y(bwd(0, 1)))
            for yr in (1, 2):
                outer = expand(toeplitz(bwd(yr, 0), BX), each16)
                inner = expand(toeplitz(bwd(yr, 1), STRIP), tiled16)
                kron_rows(xy_ref.at[xr, yr - 1, v], outer, inner, BX, STRIP)
                z_ref[xr, yr - 1, v * NZ : (v + 1) * NZ, :] = lanes3(toeplitz(fwd(yr, 2), NZ), NZ)


def build_adjoint_kernel(taps_ref, back_ref, k_ref, y_ref, xy_ref, z_ref):
    each, tiled = selectors(NZ, BX)
    each16, tiled16 = selectors(STRIP, BX)
    for xr in range(ROLES):
        for v in range(V):
            def fwd(yr, e):
                r = row_of(xr, yr, v, e)
                return taps_ref[r : r + 1, :]

            def bwd(yr, e):
                r = row_of(xr, yr, v, e)
                return back_ref[r : r + 1, :]

            outer = expand(toeplitz(bwd(0, 0), BX), each)
            inner = expand(toeplitz(bwd(0, 2), NZ), tiled) * (1.0 / V)
            kron_rows(k_ref.at[xr, v], outer, inner, BX, NZ)
            y_ref[v, :, xr * BY : (xr + 1) * BY] = stack3(banded_y(fwd(0, 1)))
            for yr in (1, 2):
                outer = expand(toeplitz(fwd(yr, 0), BX), each16)
                inner = expand(toeplitz(fwd(yr, 1), STRIP), tiled16)
                kron_rows(xy_ref.at[xr, yr - 1, v], outer, inner, BX, STRIP)
                z_ref[xr, yr - 1, :, v * LANES : (v + 1) * LANES] = lanes3(
                    toeplitz(bwd(yr, 2), NZ) * (1.0 / V), NZ
                )


def pack_strip(field, shift):
    lane = iota((NZ, LANES), 1)
    halves = []
    for half in range(2):
        total = jnp.zeros((NZ, LANES), f32)
        for j in range(8):
            x = half * 8 + j
            moved = pltpu.roll(field[x * NZ : (x + 1) * NZ, :], shift + STRIP * j, 1)
            inside = jnp.logical_and(lane >= STRIP * j, lane < STRIP * (j + 1))
            total = jnp.where(inside, moved, total)
        halves.append(total)
    return jnp.concatenate(halves, axis=0)


def unpack_strip(halves, shift):
    lane = iota((NZ, LANES), 1)
    first = jnp.where(shift > 0, BY - STRIP, 0)
    inside = jnp.logical_and(lane >= first, lane < first + STRIP)
    rows = []
    for x in range(BX):
        half, j = x // 8, x % 8
        moved = pltpu.roll(halves[half * NZ : (half + 1) * NZ, :], 2 * LANES - shift - STRIP * j, 1)
        rows.append(jnp.where(inside, moved, 0.0))
    return jnp.concatenate(rows, axis=0)


def wide(halves):
    return jnp.concatenate([halves[:NZ], halves[NZ:]], axis=1)


def tall(strip):
    return jnp.concatenate([strip[:, :LANES], strip[:, LANES:]], axis=0)


def column3(a):
    hi, lo = split(a)
    return jnp.concatenate([hi, hi, lo, jnp.zeros_like(hi)], axis=0)


def two_rows(a, matrix):
    hi, lo = split(a)
    both = dot(jnp.concatenate([hi, lo], axis=0), matrix)
    return both[: a.shape[0]] + both[a.shape[0] :]


def two_lanes(matrix, a):
    hi, lo = split(a)
    both = dot(matrix, jnp.concatenate([hi, lo], axis=1))
    return both[:, :LANES] + both[:, LANES:]


def three_lanes(a, stacked):
    hi, lo = split(a)
    return dot(jnp.concatenate([hi, lo, hi], axis=1), stacked)


def forward_parts(sources, k_ref, y_ref, xy_ref, z_ref, shifts, add):
    for xr, field, _ in sources:
        spread = three_lanes(field, y_ref[xr])
        for v in range(V):
            add(v, two_lanes(k_ref[xr, v], spread[:, v * BY : (v + 1) * BY]))
    for yr in (1, 2):
        totals = [jnp.zeros((NZ, 2 * LANES), f32) for _ in range(V)]
        for xr, _, strips in sources:
            along = dot(z_ref[xr, yr - 1], column3(wide(strips[yr - 1])))
            for v in range(V):
                totals[v] += two_rows(along[v * NZ : (v + 1) * NZ], xy_ref[xr, yr - 1, v])
        for v in range(V):
            add(v, unpack_strip(tall(totals[v]), shifts[yr - 1]))


def adjoint_parts(roles, quotient, edges, k_ref, y_ref, xy_ref, z_ref):
    first, last = roles[0], roles[-1] + 1
    totals = [jnp.zeros((FIELD, LANES), f32) for _ in roles]
    for v in range(V):
        spread = three_lanes(quotient(v), y_ref[v, :, first * BY : last * BY])
        for n, xr in enumerate(roles):
            totals[n] += two_lanes(k_ref[xr, v], spread[:, n * BY : (n + 1) * BY])
    strips = [[], []]
    for yr in (1, 2):
        packed = [wide(edges(v, yr)) for v in range(V)]
        for xr in roles:
            parts = [column3(two_rows(packed[v], xy_ref[xr, yr - 1, v])) for v in range(V)]
            strips[yr - 1].append(tall(dot(z_ref[xr, yr - 1], jnp.concatenate(parts, axis=0))))
    return totals, strips


def message_parts(message):
    return message[:FIELD], [message[FIELD : FIELD + 2 * NZ], message[FIELD + 2 * NZ :]]


def start_kernel(info_ref, estimate_ref, field_ref, first_ref, second_ref):
    for x in range(BX):
        field_ref[x * NZ : (x + 1) * NZ, :] = estimate_ref[:, x, :]
    field = field_ref[...]
    first_ref[...] = pack_strip(field, info_ref[0])
    second_ref[...] = pack_strip(field, info_ref[1])


def forward_first_kernel(info_ref, own_ref, first_ref, second_ref, k_ref, y_ref, xy_ref, z_ref, out_ref):
    shifts = (info_ref[0], info_ref[1])
    out_ref[...] = jnp.zeros_like(out_ref)

    def add(v, part):
        out_ref[v] += part

    sources = [(n, *message_parts(ref[...])) for n, ref in enumerate((own_ref, first_ref, second_ref))]
    forward_parts(sources, k_ref, y_ref, xy_ref, z_ref, shifts, add)
    for v in range(V):
        out_ref[v] = 1.0 / out_ref[v]


def adjoint_sides(quotient_ref, edge_ref, shifts, k_ref, y_ref, xy_ref, z_ref, first_ref, second_ref):
    for v in range(V):
        for yr in (1, 2):
            edge_ref[v, yr - 1] = pack_strip(quotient_ref[v], shifts[yr - 1])
    totals, strips = adjoint_parts(
        (1, 2), lambda v: quotient_ref[v], lambda v, yr: edge_ref[v, yr - 1], k_ref, y_ref, xy_ref, z_ref
    )
    for n, ref in enumerate((first_ref, second_ref)):
        ref[:FIELD] = totals[n]
        ref[FIELD : FIELD + 2 * NZ] = strips[0][n]
        ref[FIELD + 2 * NZ :] = strips[1][n]


def quotient_first_kernel(
    info_ref, table_ref, arrived_ref, inverse_ref, k_ref, y_ref, xy_ref, z_ref,
    data_ref, quotient_ref, edge_ref, first_ref, second_ref,
):
    shifts = (info_ref[0], info_ref[1])
    planes = dot(table_ref[...], arrived_ref[...])
    for v in range(V):
        for x in range(BX):
            rows = slice(x * NZ, (x + 1) * NZ)
            piece = planes[v * NZ : (v + 1) * NZ, x * BY : (x + 1) * BY]
            data_ref[v, rows, :] = piece.astype(bf16)
            quotient_ref[v, rows, :] = piece * inverse_ref[v, rows, :]
    adjoint_sides(quotient_ref, edge_ref, shifts, k_ref, y_ref, xy_ref, z_ref, first_ref, second_ref)


def adjoint_center_kernel(quotient_ref, edge_ref, k_ref, y_ref, xy_ref, z_ref, field_ref, strips_ref):
    totals, strips = adjoint_parts(
        (0,), lambda v: quotient_ref[v], lambda v, yr: edge_ref[v, yr - 1], k_ref, y_ref, xy_ref, z_ref
    )
    field_ref[...] = totals[0]
    strips_ref[0] = strips[0][0]
    strips_ref[1] = strips[1][0]


def gather_kernel(info_ref, field_ref, strips_ref, first_ref, second_ref, total_ref, up_ref, down_ref):
    total = field_ref[...] + first_ref[:FIELD] + second_ref[:FIELD]
    total_ref[...] = total
    for n, ref in enumerate((up_ref, down_ref)):
        rows = slice(FIELD + n * 2 * NZ, FIELD + (n + 1) * 2 * NZ)
        ref[: 2 * NZ] = strips_ref[n] + first_ref[rows] + second_ref[rows]
        ref[2 * NZ :] = pack_strip(total, info_ref[n])


def gather_last_kernel(field_ref, strips_ref, first_ref, second_ref, total_ref, up_ref, down_ref):
    total_ref[...] = field_ref[...] + first_ref[:FIELD] + second_ref[:FIELD]
    for n, ref in enumerate((up_ref, down_ref)):
        rows = slice(FIELD + n * 2 * NZ, FIELD + (n + 1) * 2 * NZ)
        ref[...] = strips_ref[n] + first_ref[rows] + second_ref[rows]


def update_kernel(info_ref, old_ref, total_ref, up_ref, down_ref, up_in_ref, down_in_ref, new_ref):
    half = 2 * NZ
    correction = total_ref[...]
    for n, ref in enumerate((up_in_ref, down_in_ref)):
        correction += unpack_strip(ref[:half], info_ref[n])
    new_ref[:FIELD] = old_ref[:FIELD] * correction
    for n, (ref, own) in enumerate(((up_in_ref, up_ref), (down_in_ref, down_ref))):
        rows = slice(FIELD + n * half, FIELD + (n + 1) * half)
        new_ref[rows] = old_ref[rows] * (ref[half:] + own[:half])


def forward_center_kernel(info_ref, own_ref, k_ref, y_ref, xy_ref, z_ref, out_ref):
    shifts = (info_ref[0], info_ref[1])
    out_ref[...] = jnp.zeros_like(out_ref)

    def add(v, part):
        out_ref[v] += part

    forward_parts([(0, *message_parts(own_ref[...]))], k_ref, y_ref, xy_ref, z_ref, shifts, add)


def middle_kernel(
    info_ref, data_ref, blurred_ref, from_first_ref, from_second_ref,
    k_ref, y_ref, xy_ref, z_ref, ka_ref, ya_ref, xya_ref, za_ref,
    quotient_ref, edge_ref, first_ref, second_ref,
):
    shifts = (info_ref[0], info_ref[1])
    quotient_ref[...] = blurred_ref[...]

    def add(v, part):
        quotient_ref[v] += part

    sources = [(1, *message_parts(from_first_ref[...])), (2, *message_parts(from_second_ref[...]))]
    forward_parts(sources, k_ref, y_ref, xy_ref, z_ref, shifts, add)
    for v in range(V):
        quotient_ref[v] = data_ref[v].astype(f32) / quotient_ref[v]
    adjoint_sides(quotient_ref, edge_ref, shifts, ka_ref, ya_ref, xya_ref, za_ref, first_ref, second_ref)


def final_kernel(info_ref, old_ref, total_ref, up_in_ref, down_in_ref, out_ref):
    correction = total_ref[...]
    for n, ref in enumerate((up_in_ref, down_in_ref)):
        correction += unpack_strip(ref[...], info_ref[n])
    result = old_ref[:FIELD] * correction
    for x in range(BX):
        out_ref[:, x, :] = result[x * NZ : (x + 1) * NZ]


def call(kernel, outs, *args, scalars=0):
    specs = [pl.BlockSpec(memory_space=pltpu.SMEM)] * scalars
    specs += [pl.BlockSpec(memory_space=pltpu.VMEM)] * (len(args) - scalars)
    return pl.pallas_call(
        kernel,
        out_shape=[jax.ShapeDtypeStruct(s, d) for s, d in outs],
        in_specs=specs,
        out_specs=[pl.BlockSpec(memory_space=pltpu.VMEM)] * len(outs),
        compiler_params=pltpu.CompilerParams(vmem_limit_bytes=60 * 2**20),
    )(*args)


def partner_swaps(axis):
    count = lax.axis_size(axis)
    near = [(i, i ^ 1) for i in range(count)]
    far = [(i, (i - 1 if i % 2 == 0 else i + 1) % count) for i in range(count)]
    return near, far


def swap(axis, near_value, far_value):
    near, far = partner_swaps(axis)
    far_in = lax.ppermute(far_value, axis, far)
    near_in = lax.ppermute(near_value, axis, near)
    return near_in, far_in


def tap_tables(psf_taps, kernel_index):
    gx, gy = lax.axis_index("gx"), lax.axis_index("gy")
    even_x, even_y = gx % 2 == 0, gy % 2 == 0
    anchor = jnp.zeros((), i32)
    bordered = jnp.pad(kernel_index, ((1, 1), (1, 1), (0, 0), (0, 0)), constant_values=-1)
    around = lax.dynamic_slice(
        bordered, (gx.astype(i32), gy.astype(i32), anchor, anchor), (ROLES, ROLES, V, 3)
    )
    up, down = jnp.array([1, 2, 0]), jnp.array([1, 0, 2])
    around = jnp.where(even_x, around[up], around[down])
    around = jnp.where(even_y, around[:, up], around[:, down])
    normal = psf_taps / jnp.sum(psf_taps, axis=-1, keepdims=True)
    chosen = (around.reshape(-1)[:, None] == jnp.arange(psf_taps.shape[0], dtype=i32)).astype(f32)
    kernels = jnp.dot(chosen, normal, precision=lax.Precision.HIGHEST)
    kernels = jnp.pad(kernels, ((0, 0), (0, LANES - TAPS)))
    backward = jnp.pad(kernels[:, :TAPS][:, ::-1], ((0, 0), (0, LANES - TAPS)))
    role = jnp.arange(kernels.shape[0])
    axis, yr, xr = role % 3, role // (3 * V) % ROLES, role // (3 * V * ROLES)
    step = jnp.where(axis == 0, jnp.where(xr == 1, 1, jnp.where(xr == 2, -1, 0)), 0)
    step = step * jnp.where(even_x, 1, -1)
    step_y = jnp.where(axis == 1, jnp.where(yr == 1, 1, jnp.where(yr == 2, -1, 0)), 0)
    step = (step + step_y * jnp.where(even_y, 1, -1))[:, None]

    def moved(a, sign):
        return jnp.where(
            step * sign > 0, jnp.roll(a, -STRIP, 1), jnp.where(step * sign < 0, jnp.roll(a, STRIP, 1), a)
        )

    shifts = jnp.stack([jnp.where(even_y, STRIP, 0), jnp.where(even_y, 0, STRIP)]).astype(i32)
    return moved(kernels, 1), moved(backward, -1), shifts


def shards(estimate, stored, placement, psf_taps, kernel_index):
    devices_y = lax.axis_size("gy")
    devices = lax.axis_size("gx") * devices_y
    slots = stored.shape[0]
    cap = 2 * slots // devices
    rows = devices * cap
    plane = BX * BY
    me = (lax.axis_index("gx") * devices_y + lax.axis_index("gy")).astype(i32)

    own = lax.dynamic_slice_in_dim(placement, me * slots, slots)
    (outgoing,) = call(
        functools.partial(route_kernel, cap),
        [((rows, plane), bf16)],
        (own // slots).reshape(1, slots),
        stored.reshape(slots, plane),
    )
    arrived = lax.all_to_all(
        outgoing.reshape(devices, cap, plane), ("gx", "gy"), split_axis=0, concat_axis=0, tiled=True
    ).reshape(rows, plane)

    taps, backward, info = tap_tables(psf_taps, kernel_index)
    half, message = (2 * NZ, LANES), (FIELD + 4 * NZ, LANES)
    field, up, down = call(
        start_kernel, [((FIELD, LANES), f32), (half, f32), (half, f32)], info, estimate, scalars=1
    )
    up_in, down_in = swap("gy", up, down)
    old = jnp.concatenate([field, up_in, down_in], axis=0)
    first, second = swap("gx", old, old)

    def shapes(y_shape, z_shape):
        return [
            ((ROLES, V, FIELD, FIELD), bf16),
            (y_shape, bf16),
            ((ROLES, 2, V, 2 * LANES, 2 * LANES), bf16),
            (z_shape, bf16),
        ]

    forward = call(build_forward_kernel, shapes((ROLES, 3 * BY, V * BY), (ROLES, 2, V * NZ, LANES)), taps, backward)
    adjoint = call(build_adjoint_kernel, shapes((V, 3 * BY, ROLES * BY), (ROLES, 2, NZ, V * LANES)), taps, backward)
    every = (V, FIELD, LANES)
    (inverse,) = call(forward_first_kernel, [(every, f32)], info, old, first, second, *forward, scalars=1)
    repeated = jnp.repeat(placement.reshape(devices, slots), cap, axis=0)
    (table,) = call(
        functools.partial(arrival_kernel, cap), [((slots, rows), bf16)], me.reshape(1), repeated, scalars=1
    )

    edges = ((V, 2) + half, f32)
    data, quotient, edge, first, second = call(
        quotient_first_kernel,
        [(every, bf16), (every, f32), edges, (message, f32), (message, f32)],
        info, table, arrived, inverse, *adjoint, scalars=1,
    )
    first, second = swap("gx", first, second)
    field, strips = call(
        adjoint_center_kernel, [((FIELD, LANES), f32), ((2,) + half, f32)], quotient, edge, *adjoint
    )
    both = (4 * NZ, LANES)
    total, up, down = call(
        gather_kernel, [((FIELD, LANES), f32), (both, f32), (both, f32)],
        info, field, strips, first, second, scalars=1,
    )
    up_in, down_in = swap("gy", up, down)
    (new,) = call(update_kernel, [(message, f32)], info, old, total, up, down, up_in, down_in, scalars=1)
    first, second = swap("gx", new, new)
    (blurred,) = call(forward_center_kernel, [(every, f32)], info, new, *forward, scalars=1)
    quotient, edge, first, second = call(
        middle_kernel, [(every, f32), edges, (message, f32), (message, f32)],
        info, data, blurred, first, second, *forward, *adjoint, scalars=1,
    )
    first, second = swap("gx", first, second)
    field, strips = call(
        adjoint_center_kernel, [((FIELD, LANES), f32), ((2,) + half, f32)], quotient, edge, *adjoint
    )
    total, up, down = call(
        gather_last_kernel, [((FIELD, LANES), f32), (half, f32), (half, f32)], field, strips, first, second
    )
    up_in, down_in = swap("gy", up, down)
    (refined,) = call(final_kernel, [(estimate.shape, f32)], info, new, total, up_in, down_in, scalars=1)
    return refined


def solution(mesh):
    return jax.shard_map(
        shards,
        mesh=mesh,
        in_specs=(P(None, "gx", "gy"), P(("gx", "gy"), None, None), P(), P(), P()),
        out_specs=P(None, "gx", "gy"),
        check_vma=False,
    )
```

profile of v0, /device:TPU:0, one launch (start us, length us, event | category | flops | bytes accessed | tf_op | source)
XLA Modules:
  0.0 134.3 jit_solution(3619150256936100546)
XLA Ops:
  0.7 1.8 %shard_map.73 = (f32[512,128]{1,0:T(8,128)}, f32[64,128]{1,0:T(8,128)}, f32[64,128]{1,0:T(8,128)}) custom-call(s32[2]{0:T(128)} %pad_add_fusion.info_ref, f32[32,16,128]{2,1,0:T(8,128)} %estimate_ref.1), custom_call_target="tpu_custom_call" | custom-call | tf_op jit(solution)/shard_map/pallas_call | solution.py:383
  2.5 3.1 %collective-permute-start = (f32[64,128]{1,0:T(8,128)}, f32[64,128]{1,0:T(8,128)S(1)}, u32[]{:S(2)}, u32[]{:S(2)}) collective-permute-start(f32[64,128]{1,0:T(8,128)} %get-tuple-element.36), channel_id=1, source_target_pairs={{0,1},{1,0},{2,3},{3,2},{4,5},{5,4},{6,7},{7,6},{8,9},{9,8},{10,11... | collective-permute-start | bytes 98312 | tf_op jit(solution)/shard_map/ppermute | solution.py:402
  5.6 2.5 %collective-permute-start.1 = (f32[64,128]{1,0:T(8,128)}, f32[64,128]{1,0:T(8,128)S(1)}, u32[]{:S(2)}, u32[]{:S(2)}) collective-permute-start(f32[64,128]{1,0:T(8,128)} %get-tuple-element.37), channel_id=1, source_target_pairs={{0,3},{1,2},{2,1},{3,0},{4,7},{5,6},{6,5},{7,4},{8,11},{9,10},{10,... | collective-permute-start | bytes 98312 | tf_op jit(solution)/shard_map/ppermute | solution.py:401
  8.1 2.0 %copy.22 = bf16[16,8,16,128]{3,1,2,0:T(8,128)(2,1)} copy(bf16[16,8,16,128]{3,2,1,0:T(8,128)(2,1)} %bitcast.19) | data formatting | bytes 1048576
  10.0 1.4 %fusion.8.target_ref = s32[1,128]{1,0:T(1,128)} fusion(s32[4096]{0:T(1024)} %param.9, s32[]{:T(128)S(6)} %select_n.254), kind=kLoop, calls=%fused_computation.50 | loop fusion | flops 1920 | bytes 1028 | tf_op jit(solution)/shard_map/reshape | solution.py:451
  11.4 2.6 %shard_map.75 = bf16[256,2048]{1,0:T(8,128)(2,1)} custom-call(s32[1,128]{1,0:T(1,128)} %fusion.8.target_ref, bf16[128,2048]{1,0:T(8,128)(2,1)} %bitcast.18), custom_call_target="tpu_custom_call" | custom-call | tf_op jit(solution)/shard_map/pallas_call | solution.py:383
  14.0 3.6 %all-to-all-start = ((bf16[32,8,2048]{2,1,0:T(8,128)(2,1)}), bf16[32,8,2048]{2,1,0:T(8,128)(2,1)S(1)}, u32[]{:S(2)}, u32[]{:S(2)}) async-start(bf16[32,8,2048]{2,1,0:T(8,128)(2,1)} %bitcast.17), calls=%async_computation | async-start | bytes 2097152 | tf_op jit(solution)/shard_map/all_to_all | solution.py:454
  21.9 2.5 %collective-permute-start.3 = (f32[640,128]{1,0:T(8,128)S(1)}, f32[640,128]{1,0:T(8,128)S(1)}, u32[]{:S(2)}, u32[]{:S(2)}) collective-permute-start(f32[640,128]{1,0:T(8,128)S(1)} %constant_dynamic-update-slice_fusion.own_ref.old_ref), channel_id=1, source_target_pairs={{0,28},{4,8},{8,4},{12,16},{16,12},{20,24},{24,20},{28,0},{1,29},{... | collective-permute-start | bytes 983048 | tf_op jit(solution)/shard_map/ppermute | solution.py:401
  25.1 7.4 %shard_map.78 = (bf16[3,4,512,512]{3,2,1,0:T(8,128)(2,1)}, bf16[4,384,384]{2,1,0:T(8,128)(2,1)}, bf16[3,2,4,256,256]{4,3,2,1,0:T(8,128)(2,1)}, bf16[3,2,32,512]{3,2,1,0:T(8,128)(2,1)}) custom-call(f32[108,128]{1,0:T(8,128)} %maximum_select_fusion.taps_ref, f32[108,128]{1,0:T(8,128)} %maximum_select_fusion.1.back_ref), custom_call_target="tpu_custom_call" | custom-call | tf_op jit(solution)/shard_map/pallas_call | solution.py:383
  32.5 7.1 %shard_map.76 = (bf16[3,4,512,512]{3,2,1,0:T(8,128)(2,1)}, bf16[3,384,512]{2,1,0:T(8,128)(2,1)}, bf16[3,2,4,256,256]{4,3,2,1,0:T(8,128)(2,1)}, bf16[3,2,128,128]{3,2,1,0:T(8,128)(2,1)}) custom-call(f32[108,128]{1,0:T(8,128)} %maximum_select_fusion.taps_ref, f32[108,128]{1,0:T(8,128)} %maximum_select_fusion.1.back_ref), custom_call_target="tpu_custom_call" | custom-call | tf_op jit(solution)/shard_map/pallas_call | solution.py:383
  40.3 1.9 %shard_map.74.table_ref = bf16[128,256]{1,0:T(8,128)(2,1)} custom-call(s32[1]{0:T(128)} %bitcast.2.me_ref, s32[256,128]{1,0:T(8,128)} %broadcast_bitcast_fusion.slots_ref), custom_call_target="tpu_custom_call" | custom-call | tf_op jit(solution)/shard_map/pallas_call | solution.py:383
  43.0 9.6 %shard_map.77.inverse_ref = f32[4,512,128]{2,1,0:T(8,128)} custom-call(s32[2]{0:T(128)} %pad_add_fusion.info_ref, f32[640,128]{1,0:T(8,128)} %copy-done.1, f32[640,128]{1,0:T(8,128)} %copy-done.3, f32[640,128]{1,0:T(8,128)} %copy-done.2, bf16[3,4,512,512]{3,2,1,0:T(8,128)(2,1)} %get-tuple-element.38.k_ref, bf16[3,384,512]{2,1,0:T(8,128)(2,1)} %get-tuple-element.39.y_ref, ...), custom_call_target="tpu_custom_call" | custom-call | tf_op jit(solution)/shard_map/pallas_call | solution.py:383
  52.6 1.0 copy-done
  53.6 9.0 %shard_map.79 = (bf16[4,512,128]{2,1,0:T(8,128)(2,1)}, f32[4,512,128]{2,1,0:T(8,128)}, f32[4,2,64,128]{3,2,1,0:T(8,128)}, f32[640,128]{1,0:T(8,128)}, f32[640,128]{1,0:T(8,128)}) custom-call(s32[2]{0:T(128)} %pad_add_fusion.info_ref, bf16[128,256]{1,0:T(8,128)(2,1)} %shard_map.74.table_ref, bf16[256,2048]{1,0:T(8,128)(2,1)} %bitcast.16, ...), custom_call_target="tpu_custom_call" | custom-call | tf_op jit(solution)/shard_map/pallas_call | solution.py:383
  63.3 6.7 %shard_map.80 = (f32[512,128]{1,0:T(8,128)}, f32[2,64,128]{2,1,0:T(8,128)}) custom-call(f32[4,512,128]{2,1,0:T(8,128)} %get-tuple-element.46.quotient_ref, f32[4,2,64,128]{3,2,1,0:T(8,128)} %get-tuple-element.47.edge_ref, bf16[3,4,512,512]{3,2,1,0:T(8,128)(2,1)} %get-tuple-element.42.k_ref.ka_ref, bf16[4,384,384]{2,1,0:T(8,128)(2,1)} %get-tuple-element.43.y_ref.ya_ref, ...), custom_call_target="tpu_custom_call" | custom-call | tf_op jit(solution)/shard_map/pallas_call | solution.py:383
  70.0 3.8 %collective-permute-done.5.second_ref = f32[640,128]{1,0:T(8,128)S(1)} collective-permute-done((f32[640,128]{1,0:T(8,128)}, f32[640,128]{1,0:T(8,128)S(1)}, u32[]{:S(2)}, u32[]{:S(2)}) %collective-permute-start.5) | collective-permute-done | bytes 327712 | tf_op jit(solution)/shard_map/ppermute | solution.py:401
  74.6 2.0 %shard_map.81 = (f32[512,128]{1,0:T(8,128)}, f32[128,128]{1,0:T(8,128)}, f32[128,128]{1,0:T(8,128)}) custom-call(s32[2]{0:T(128)} %pad_add_fusion.info_ref, f32[512,128]{1,0:T(8,128)} %get-tuple-element.48.field_ref, f32[2,64,128]{2,1,0:T(8,128)} %get-tuple-element.49.strips_ref, f32[640,128]{1,0:T(8,128)} %copy-done.4, f32[640,128]{1,0:T(8,128)} %copy-done.5), custom_call_target="tpu_custom_call" | custom-call | tf_op jit(solution)/shard_map/pallas_call | solution.py:383
  76.6 1.5 %collective-permute-start.6 = (f32[128,128]{1,0:T(8,128)}, f32[128,128]{1,0:T(8,128)S(1)}, u32[]{:S(2)}, u32[]{:S(2)}) collective-permute-start(f32[128,128]{1,0:T(8,128)} %get-tuple-element.53.up_ref), channel_id=1, source_target_pairs={{0,1},{1,0},{2,3},{3,2},{4,5},{5,4},{6,7},{7,6},{8,9},{9,8},{10,11... | collective-permute-start | bytes 196616 | tf_op jit(solution)/shard_map/ppermute | solution.py:402
  78.1 2.4 %collective-permute-start.7 = (f32[128,128]{1,0:T(8,128)}, f32[128,128]{1,0:T(8,128)S(1)}, u32[]{:S(2)}, u32[]{:S(2)}) collective-permute-start(f32[128,128]{1,0:T(8,128)} %get-tuple-element.54.down_ref), channel_id=1, source_target_pairs={{0,3},{1,2},{2,1},{3,0},{4,7},{5,6},{6,5},{7,4},{8,11},{9,10},{10,... | collective-permute-start | bytes 196616 | tf_op jit(solution)/shard_map/ppermute | solution.py:401
  81.1 3.3 %collective-permute-done.7.down_in_ref = f32[128,128]{1,0:T(8,128)S(1)} collective-permute-done((f32[128,128]{1,0:T(8,128)}, f32[128,128]{1,0:T(8,128)S(1)}, u32[]{:S(2)}, u32[]{:S(2)}) %collective-permute-start.7) | collective-permute-done | bytes 65568 | tf_op jit(solution)/shard_map/ppermute | solution.py:401
  85.0 2.0 %shard_map.82.own_ref.old_ref = f32[640,128]{1,0:T(8,128)} custom-call(s32[2]{0:T(128)} %pad_add_fusion.info_ref, f32[640,128]{1,0:T(8,128)} %copy-done.1, f32[512,128]{1,0:T(8,128)} %get-tuple-element.52.total_ref, f32[128,128]{1,0:T(8,128)} %get-tuple-element.53.up_ref, f32[128,128]{1,0:T(8,128)} %get-tuple-element.54.down_ref, f32[128,128]{1,0:T(8,128)} %copy-done.11, ...), custom_call_target="tpu_custom_call" | custom-call | tf_op jit(solution)/shard_map/pallas_call | solution.py:383
  87.0 6.9 %shard_map.83.blurred_ref = f32[4,512,128]{2,1,0:T(8,128)} custom-call(s32[2]{0:T(128)} %pad_add_fusion.info_ref, f32[640,128]{1,0:T(8,128)} %shard_map.82.own_ref.old_ref, bf16[3,4,512,512]{3,2,1,0:T(8,128)(2,1)} %get-tuple-element.38.k_ref, bf16[3,384,512]{2,1,0:T(8,128)(2,1)} %get-tuple-element.39.y_ref, ...), custom_call_target="tpu_custom_call" | custom-call | tf_op jit(solution)/shard_map/pallas_call | solution.py:383
  94.0 2.5 %collective-permute-done.9.from_second_ref = f32[640,128]{1,0:T(8,128)S(1)} collective-permute-done((f32[640,128]{1,0:T(8,128)}, f32[640,128]{1,0:T(8,128)S(1)}, u32[]{:S(2)}, u32[]{:S(2)}) %collective-permute-start.9) | collective-permute-done | bytes 327712 | tf_op jit(solution)/shard_map/ppermute | solution.py:401
  97.4 14.7 %shard_map.84 = (f32[4,512,128]{2,1,0:T(8,128)}, f32[4,2,64,128]{3,2,1,0:T(8,128)}, f32[640,128]{1,0:T(8,128)}, f32[640,128]{1,0:T(8,128)}) custom-call(s32[2]{0:T(128)} %pad_add_fusion.info_ref, bf16[4,512,128]{2,1,0:T(8,128)(2,1)} %get-tuple-element.55.data_ref, f32[4,512,128]{2,1,0:T(8,128)} %shard_map.83.blurred_ref, f32[640,128]{1,0:T(8,128)} %copy-done.9, ...), custom_call_target="tpu_custom_call" | custom-call | tf_op jit(solution)/shard_map/pallas_call | solution.py:383
  112.0 0.8 collective-permute-start.11
  112.8 6.7 %shard_map.85 = (f32[512,128]{1,0:T(8,128)}, f32[2,64,128]{2,1,0:T(8,128)}) custom-call(f32[4,512,128]{2,1,0:T(8,128)} %get-tuple-element.56.quotient_ref, f32[4,2,64,128]{3,2,1,0:T(8,128)} %get-tuple-element.57.edge_ref, bf16[3,4,512,512]{3,2,1,0:T(8,128)(2,1)} %get-tuple-element.42.k_ref.ka_ref, bf16[4,384,384]{2,1,0:T(8,128)(2,1)} %get-tuple-element.43.y_ref.ya_ref, ...), custom_call_target="tpu_custom_call" | custom-call | tf_op jit(solution)/shard_map/pallas_call | solution.py:383
  119.6 3.5 %collective-permute-done.11.second_ref = f32[640,128]{1,0:T(8,128)S(1)} collective-permute-done((f32[640,128]{1,0:T(8,128)}, f32[640,128]{1,0:T(8,128)S(1)}, u32[]{:S(2)}, u32[]{:S(2)}) %collective-permute-start.11) | collective-permute-done | bytes 327712 | tf_op jit(solution)/shard_map/ppermute | solution.py:401
  123.7 1.9 %shard_map.86 = (f32[512,128]{1,0:T(8,128)}, f32[64,128]{1,0:T(8,128)}, f32[64,128]{1,0:T(8,128)}) custom-call(f32[512,128]{1,0:T(8,128)} %get-tuple-element.58.field_ref, f32[2,64,128]{2,1,0:T(8,128)} %get-tuple-element.59.strips_ref, f32[640,128]{1,0:T(8,128)} %copy-done.6, f32[640,128]{1,0:T(8,128)} %copy-done.7), custom_call_target="tpu_custom_call" | custom-call | tf_op jit(solution)/shard_map/pallas_call | solution.py:383
  125.7 3.0 %collective-permute-start.13 = (f32[64,128]{1,0:T(8,128)}, f32[64,128]{1,0:T(8,128)S(1)}, u32[]{:S(2)}, u32[]{:S(2)}) collective-permute-start(f32[64,128]{1,0:T(8,128)} %get-tuple-element.64), channel_id=1, source_target_pairs={{0,3},{1,2},{2,1},{3,0},{4,7},{5,6},{6,5},{7,4},{8,11},{9,10},{10,... | collective-permute-start | bytes 98312 | tf_op jit(solution)/shard_map/ppermute | solution.py:401
  128.7 1.1 collective-permute-done.12.up_in_ref
  129.8 1.8 %collective-permute-done.13.down_in_ref = f32[64,128]{1,0:T(8,128)S(1)} collective-permute-done((f32[64,128]{1,0:T(8,128)}, f32[64,128]{1,0:T(8,128)S(1)}, u32[]{:S(2)}, u32[]{:S(2)}) %collective-permute-start.13) | collective-permute-done | bytes 32800 | tf_op jit(solution)/shard_map/ppermute | solution.py:401
  132.2 2.1 %shard_map.87 = f32[32,16,128]{2,1,0:T(8,128)} custom-call(s32[2]{0:T(128)} %pad_add_fusion.info_ref, f32[640,128]{1,0:T(8,128)} %shard_map.82.own_ref.old_ref, f32[512,128]{1,0:T(8,128)} %get-tuple-element.62.total_ref, f32[64,128]{1,0:T(8,128)} %copy-done.13, f32[64,128]{1,0:T(8,128)} %copy-done.14), custom_call_target="tpu_custom_call" | custom-call | tf_op jit(solution)/shard_map/pallas_call | solution.py:383
  (82 shorter events, 12.1 us)
Async XLA Ops:
  0.0 17.8 %copy-start.18 = (s32[3]{0:T(128)S(1)}, s32[3]{0:T(128)}, u32[]{:S(2)}) copy-start(s32[3]{0:T(128)} %constant.117) | copy-start | bytes 40
  0.0 17.8 %copy-start.19 = (s32[3]{0:T(128)S(1)}, s32[3]{0:T(128)}, u32[]{:S(2)}) copy-start(s32[3]{0:T(128)} %constant.116) | copy-start | bytes 40
  0.0 17.6 %copy-start.15 = (s32[8,4,4,3]{0,2,3,1:T(4,128)S(1)}, s32[8,4,4,3]{0,2,3,1:T(4,128)}, u32[]{:S(2)}) copy-start(s32[8,4,4,3]{0,2,3,1:T(4,128)} %param.11) | copy-start | bytes 4612
  0.0 20.3 %copy-start.17 = (f32[48,31]{0,1:T(8,128)S(1)}, f32[48,31]{0,1:T(8,128)}, u32[]{:S(2)}) copy-start(f32[48,31]{0,1:T(8,128)} %param.10) | copy-start | bytes 17860
  2.5 18.3 %copy-start.10 = (f32[512,128]{1,0:T(8,128)S(1)}, f32[512,128]{1,0:T(8,128)}, u32[]{:S(2)}) copy-start(f32[512,128]{1,0:T(8,128)} %get-tuple-element.35) | copy-start | bytes 786436
  2.5 19.3 %collective-permute-start = (f32[64,128]{1,0:T(8,128)}, f32[64,128]{1,0:T(8,128)S(1)}, u32[]{:S(2)}, u32[]{:S(2)}) collective-permute-start(f32[64,128]{1,0:T(8,128)} %get-tuple-element.36), channel_id=1, source_target_pairs={{0,1},{1,0},{2,3},{3,2},{4,5},{5,4},{6,7},{7,6},{8,9},{9,8},{10,11... | collective-permute-start | bytes 98312 | tf_op jit(solution)/shard_map/ppermute | solution.py:402
  5.6 16.3 %collective-permute-start.1 = (f32[64,128]{1,0:T(8,128)}, f32[64,128]{1,0:T(8,128)S(1)}, u32[]{:S(2)}, u32[]{:S(2)}) collective-permute-start(f32[64,128]{1,0:T(8,128)} %get-tuple-element.37), channel_id=1, source_target_pairs={{0,3},{1,2},{2,1},{3,0},{4,7},{5,6},{6,5},{7,4},{8,11},{9,10},{10,... | collective-permute-start | bytes 98312 | tf_op jit(solution)/shard_map/ppermute | solution.py:401
  11.4 28.2 %copy-start.16 = (s32[4096]{0:T(1024)S(1)}, s32[4096]{0:T(1024)}, u32[]{:S(2)}) copy-start(s32[4096]{0:T(1024)} %param.9) | copy-start | bytes 49156
  14.0 38.6 %all-to-all-start = ((bf16[32,8,2048]{2,1,0:T(8,128)(2,1)}), bf16[32,8,2048]{2,1,0:T(8,128)(2,1)S(1)}, u32[]{:S(2)}, u32[]{:S(2)}) async-start(bf16[32,8,2048]{2,1,0:T(8,128)(2,1)} %bitcast.17), calls=%async_computation | async-start | bytes 2097152 | tf_op jit(solution)/shard_map/all_to_all | solution.py:454
  21.9 20.3 %copy-start.1 = (f32[640,128]{1,0:T(8,128)}, f32[640,128]{1,0:T(8,128)S(1)}, u32[]{:S(2)}) copy-start(f32[640,128]{1,0:T(8,128)S(1)} %constant_dynamic-update-slice_fusion.own_ref.old_ref) | copy-start | bytes 983044
  21.9 20.3 %collective-permute-start.3 = (f32[640,128]{1,0:T(8,128)S(1)}, f32[640,128]{1,0:T(8,128)S(1)}, u32[]{:S(2)}, u32[]{:S(2)}) collective-permute-start(f32[640,128]{1,0:T(8,128)S(1)} %constant_dynamic-update-slice_fusion.own_ref.old_ref), channel_id=1, source_target_pairs={{0,28},{4,8},{8,4},{12,16},{16,12},{20,24},{24,20},{28,0},{1,29},{... | collective-permute-start | bytes 983048 | tf_op jit(solution)/shard_map/ppermute | solution.py:401
  24.4 17.8 %collective-permute-start.2 = (f32[640,128]{1,0:T(8,128)S(1)}, f32[640,128]{1,0:T(8,128)S(1)}, u32[]{:S(2)}, u32[]{:S(2)}) collective-permute-start(f32[640,128]{1,0:T(8,128)S(1)} %constant_dynamic-update-slice_fusion.own_ref.old_ref), channel_id=1, source_target_pairs={{0,4},{4,0},{8,12},{12,8},{16,20},{20,16},{24,28},{28,24},{1,5},{5... | collective-permute-start | bytes 983048 | tf_op jit(solution)/shard_map/ppermute | solution.py:402
  42.1 0.8 copy-start.3
  52.6 1.0 copy-start
  62.6 7.5 %collective-permute-start.4 = (f32[640,128]{1,0:T(8,128)}, f32[640,128]{1,0:T(8,128)S(1)}, u32[]{:S(2)}, u32[]{:S(2)}) collective-permute-start(f32[640,128]{1,0:T(8,128)} %get-tuple-element.50), channel_id=1, source_target_pairs={{0,4},{4,0},{8,12},{12,8},{16,20},{20,16},{24,28},{28,24},{1,5},{5... | collective-permute-start | bytes 983048 | tf_op jit(solution)/shard_map/ppermute | solution.py:402
  63.1 10.8 %collective-permute-start.5 = (f32[640,128]{1,0:T(8,128)}, f32[640,128]{1,0:T(8,128)S(1)}, u32[]{:S(2)}, u32[]{:S(2)}) collective-permute-start(f32[640,128]{1,0:T(8,128)} %get-tuple-element.51), channel_id=1, source_target_pairs={{0,28},{4,8},{8,4},{12,16},{16,12},{20,24},{24,20},{28,0},{1,29},{... | collective-permute-start | bytes 983048 | tf_op jit(solution)/shard_map/ppermute | solution.py:401
  70.0 3.8 %copy-start.4 = (f32[640,128]{1,0:T(8,128)}, f32[640,128]{1,0:T(8,128)S(1)}, u32[]{:S(2)}) copy-start(f32[640,128]{1,0:T(8,128)S(1)} %collective-permute-done.4.first_ref) | copy-start | bytes 983044
  73.8 0.7 copy-start.5
  76.6 4.5 %collective-permute-start.6 = (f32[128,128]{1,0:T(8,128)}, f32[128,128]{1,0:T(8,128)S(1)}, u32[]{:S(2)}, u32[]{:S(2)}) collective-permute-start(f32[128,128]{1,0:T(8,128)} %get-tuple-element.53.up_ref), channel_id=1, source_target_pairs={{0,1},{1,0},{2,3},{3,2},{4,5},{5,4},{6,7},{7,6},{8,9},{9,8},{10,11... | collective-permute-start | bytes 196616 | tf_op jit(solution)/shard_map/ppermute | solution.py:402
  78.1 6.3 %collective-permute-start.7 = (f32[128,128]{1,0:T(8,128)}, f32[128,128]{1,0:T(8,128)S(1)}, u32[]{:S(2)}, u32[]{:S(2)}) collective-permute-start(f32[128,128]{1,0:T(8,128)} %get-tuple-element.54.down_ref), channel_id=1, source_target_pairs={{0,3},{1,2},{2,1},{3,0},{4,7},{5,6},{6,5},{7,4},{8,11},{9,10},{10,... | collective-permute-start | bytes 196616 | tf_op jit(solution)/shard_map/ppermute | solution.py:401
  81.1 3.3 %copy-start.11 = (f32[128,128]{1,0:T(8,128)}, f32[128,128]{1,0:T(8,128)S(1)}, u32[]{:S(2)}) copy-start(f32[128,128]{1,0:T(8,128)S(1)} %collective-permute-done.6.up_in_ref) | copy-start | bytes 196612
  87.0 9.4 %collective-permute-start.9 = (f32[640,128]{1,0:T(8,128)}, f32[640,128]{1,0:T(8,128)S(1)}, u32[]{:S(2)}, u32[]{:S(2)}) collective-permute-start(f32[640,128]{1,0:T(8,128)} %shard_map.82.own_ref.old_ref), channel_id=1, source_target_pairs={{0,28},{4,8},{8,4},{12,16},{16,12},{20,24},{24,20},{28,0},{1,29},{... | collective-permute-start | bytes 983048 | tf_op jit(solution)/shard_map/ppermute | solution.py:401
  87.0 9.4 %collective-permute-start.8 = (f32[640,128]{1,0:T(8,128)}, f32[640,128]{1,0:T(8,128)S(1)}, u32[]{:S(2)}, u32[]{:S(2)}) collective-permute-start(f32[640,128]{1,0:T(8,128)} %shard_map.82.own_ref.old_ref), channel_id=1, source_target_pairs={{0,4},{4,0},{8,12},{12,8},{16,20},{20,16},{24,28},{28,24},{1,5},{5... | collective-permute-start | bytes 983048 | tf_op jit(solution)/shard_map/ppermute | solution.py:402
  96.4 0.7 copy-start.8
  96.4 0.9 copy-start.9
  112.0 7.5 %collective-permute-start.10 = (f32[640,128]{1,0:T(8,128)}, f32[640,128]{1,0:T(8,128)S(1)}, u32[]{:S(2)}, u32[]{:S(2)}) collective-permute-start(f32[640,128]{1,0:T(8,128)} %get-tuple-element.60), channel_id=1, source_target_pairs={{0,4},{4,0},{8,12},{12,8},{16,20},{20,16},{24,28},{28,24},{1,5},{5... | collective-permute-start | bytes 983048 | tf_op jit(solution)/shard_map/ppermute | solution.py:402
  112.0 11.0 %collective-permute-start.11 = (f32[640,128]{1,0:T(8,128)}, f32[640,128]{1,0:T(8,128)S(1)}, u32[]{:S(2)}, u32[]{:S(2)}) collective-permute-start(f32[640,128]{1,0:T(8,128)} %get-tuple-element.61), channel_id=1, source_target_pairs={{0,28},{4,8},{8,4},{12,16},{16,12},{20,24},{24,20},{28,0},{1,29},{... | collective-permute-start | bytes 983048 | tf_op jit(solution)/shard_map/ppermute | solution.py:401
  119.6 3.5 %copy-start.6 = (f32[640,128]{1,0:T(8,128)}, f32[640,128]{1,0:T(8,128)S(1)}, u32[]{:S(2)}) copy-start(f32[640,128]{1,0:T(8,128)S(1)} %collective-permute-done.10.first_ref) | copy-start | bytes 983044
  123.0 0.7 copy-start.7
  125.7 4.1 %collective-permute-start.12 = (f32[64,128]{1,0:T(8,128)}, f32[64,128]{1,0:T(8,128)S(1)}, u32[]{:S(2)}, u32[]{:S(2)}) collective-permute-start(f32[64,128]{1,0:T(8,128)} %get-tuple-element.63), channel_id=1, source_target_pairs={{0,1},{1,0},{2,3},{3,2},{4,5},{5,4},{6,7},{7,6},{8,9},{9,8},{10,11... | collective-permute-start | bytes 98312 | tf_op jit(solution)/shard_map/ppermute | solution.py:402
  125.7 5.9 %collective-permute-start.13 = (f32[64,128]{1,0:T(8,128)}, f32[64,128]{1,0:T(8,128)S(1)}, u32[]{:S(2)}, u32[]{:S(2)}) collective-permute-start(f32[64,128]{1,0:T(8,128)} %get-tuple-element.64), channel_id=1, source_target_pairs={{0,3},{1,2},{2,1},{3,0},{4,7},{5,6},{6,5},{7,4},{8,11},{9,10},{10,... | collective-permute-start | bytes 98312 | tf_op jit(solution)/shard_map/ppermute | solution.py:401
  129.8 1.8 %copy-start.13 = (f32[64,128]{1,0:T(8,128)}, f32[64,128]{1,0:T(8,128)S(1)}, u32[]{:S(2)}) copy-start(f32[64,128]{1,0:T(8,128)S(1)} %collective-permute-done.12.up_in_ref) | copy-start | bytes 98308
  (3 other events, 2.0 us)
where the time goes:
time: 135 us; the launch traced here: 134 us
  Pallas kernels  82.5 us (61%)
  starting transfers between devices  20 us (15%)
  waiting for transfers between devices  16.6 us (12%)
  local copies, waits for them, and re-layouts  11.2 us (8%)
  other arithmetic  3.61 us (3%)
    pallas_call x15, Pallas kernels, call(): pl.pallas_call(kernel, out_shape=[jax.ShapeDtypeStruct(s, d) for s, d in...  82.5 us
    ppermute x7, waiting for transfers between devices, swap(): far_in = lax.ppermute(far_value, axis, far)  14.8 us
    ppermute x7, starting transfers between devices, swap(): far_in = lax.ppermute(far_value, axis, far)  11.4 us
    unnamed x44, local copies, waits for them, and re-layouts  7.67 us
    ppermute x7, starting transfers between devices, swap(): near_in = lax.ppermute(near_value, axis, near)  5.05 us
    all_to_all x1, starting transfers between devices, shards(): lax.all_to_all(outgoing.reshape(devices, cap, plane), ('gx', 'gy'), split...  3.59 us
  transfers between devices with their start and end apart: 15, of which 7 were waited for; matrix products, arithmetic and copies ran while one was open for 7% of the time, Pallas kernels for 36%

commit v1 on v0

v1 whole, which is shorter than its diff:
```python
import functools
import math

import jax
import jax.numpy as jnp
from jax import lax
from jax.experimental import pallas as pl
from jax.experimental.pallas import tpu as pltpu
from jax.sharding import PartitionSpec as P

f32 = jnp.float32
bf16 = jnp.bfloat16
i32 = jnp.int32

NZ = 32
BX = 16
BY = 128
V = 4
TAPS = 31
RADIUS = 15
FIELD = BX * NZ
STRIP = 16
LANES = 128
WORKSPACE = 8 * 2**20
PEAK = 14.0
ROLES = 3


def iota(shape, axis):
    return lax.broadcasted_iota(i32, shape, axis)


def one_hot(mask):
    return jnp.where(mask, 1.0, 0.0).astype(bf16)


def split(a):
    hi = a.astype(bf16)
    return hi, (a - hi.astype(f32)).astype(bf16)


def dot(a, b):
    return jnp.dot(a, b, preferred_element_type=f32)


def earlier(count):
    return one_hot(iota((count, count), 0) < iota((count, count), 1))


def route_kernel(cap, me_ref, slots_ref, stored_ref, out_ref, wide_ref):
    rows, slots = out_ref.shape[0], stored_ref.shape[0]
    wide_ref[...] = stored_ref[...].reshape(slots * BX, BY).astype(f32)
    target = jnp.right_shift(slots_ref[pl.ds(me_ref[0], 1), :], slots.bit_length() - 1)
    place = iota((rows, slots), 0) - target * cap
    marked = jnp.logical_and(place >= 0, place < cap)
    rank = dot(one_hot(marked), earlier(slots))
    chosen = one_hot(jnp.logical_and(marked, rank == place.astype(f32)))
    for x in range(0, BX, 2):
        pair = [wide_ref[pl.ds(x + n, slots, stride=BX), :].astype(bf16) for n in range(2)]
        out_ref[:, x * BY : (x + 2) * BY] = dot(chosen, jnp.concatenate(pair, axis=1)).astype(bf16)


def arrival_kernel(cap, me_ref, slots_ref, out_ref, table_ref, sem):
    rows, slots = slots_ref.shape
    item = slots_ref[...] - me_ref[0] * slots
    wanted = jnp.logical_and(item >= 0, item < slots)
    rank = dot(one_hot(wanted), earlier(slots))
    order = jnp.bitwise_and(iota((rows, slots), 0), cap - 1)
    found = jnp.logical_and(wanted, rank == order.astype(f32))
    item_of = jnp.sum(jnp.where(found, item + 1, 0).astype(f32), axis=1, keepdims=True) - 1.0
    table = jnp.where(item_of == iota((rows, slots), 1).astype(f32), 1.0, 0.0)
    table_ref[...] = table.T.astype(bf16)
    copy = pltpu.make_async_copy(table_ref, out_ref, sem)
    copy.start()
    copy.wait()


def toeplitz(row, count):
    spread = jnp.broadcast_to(row, (count, LANES))
    return pltpu.roll(spread, LANES - RADIUS, 1, stride=1, stride_axis=0)


def expand(table, selector):
    first = table.astype(bf16)
    rest = table - first.astype(f32)
    second = rest.astype(bf16)
    third = (rest - second.astype(f32)).astype(bf16)
    return dot(first, selector) + dot(second, selector) + dot(third, selector)


def selectors(width, count):
    lane = iota((LANES, width * count), 1)
    row = iota((LANES, width * count), 0)
    each = one_hot(row == jnp.right_shift(lane, width.bit_length() - 1))
    tiled = one_hot(row == jnp.bitwise_and(lane, width - 1))
    return each, tiled


def row_of(xr, yr, view, axis):
    return ((xr * ROLES + yr) * V + view) * 3 + axis


def kron_rows(out, outer, inner, count, width):
    for i in range(count):
        out[i * width : (i + 1) * width, :] = (inner * outer[i : i + 1, :]).astype(bf16)


def stack3(table):
    hi, lo = split(table)
    return jnp.concatenate([hi, hi, lo], axis=0)


def lanes3(table, width):
    inside = iota(table.shape, 1) < width
    kept = jnp.where(inside, table, 0.0)
    hi, lo = split(kept)
    hi, lo = hi.astype(f32), lo.astype(f32)
    return (hi + pltpu.roll(lo, width, 1) + pltpu.roll(hi, 2 * width, 1)).astype(bf16)


def banded_y(row):
    table = toeplitz(row, BY)
    off = iota((BY, BY), 0) - iota((BY, BY), 1)
    return jnp.where(jnp.abs(off) <= RADIUS, table, 0.0)


def build_forward_kernel(taps_ref, back_ref, *refs):
    held, out, sems = refs[8:16], refs[:8], refs[16]
    copies = [pltpu.make_async_copy(a, b, sems.at[n]) for n, (a, b) in enumerate(zip(held, out))]
    each, tiled = selectors(NZ, BX)
    each16, tiled16 = selectors(STRIP, BX)
    for xr in range(ROLES):
        k_ref, y_ref, xy_ref, z_ref = held[:4] if xr == 0 else held[4:]
        n = max(xr - 1, 0)
        for v in range(V):
            def fwd(yr, e):
                r = row_of(xr, yr, v, e)
                return taps_ref[r : r + 1, :]

            def bwd(yr, e):
                r = row_of(xr, yr, v, e)
                return back_ref[r : r + 1, :]

            outer = expand(toeplitz(fwd(0, 0), BX), each)
            inner = expand(toeplitz(fwd(0, 2), NZ), tiled)
            kron_rows(k_ref.at[n, v], outer, inner, BX, NZ)
            y_ref[n, :, v * BY : (v + 1) * BY] = stack3(banded_y(bwd(0, 1)))
            for yr in (1, 2):
                outer = expand(toeplitz(bwd(yr, 0), BX), each16)
                inner = expand(toeplitz(bwd(yr, 1), STRIP), tiled16)
                kron_rows(xy_ref.at[n, yr - 1, v], outer, inner, BX, STRIP)
                z_ref[n, yr - 1, v * NZ : (v + 1) * NZ, :] = lanes3(toeplitz(fwd(yr, 2), NZ), NZ)
        if xr == 0:
            for copy in copies[:4]:
                copy.start()
    for copy in copies[4:]:
        copy.start()
    for copy in copies:
        copy.wait()


def build_adjoint_kernel(taps_ref, back_ref, *refs):
    held, out, sems = refs[8:16], refs[:8], refs[16]
    copies = [pltpu.make_async_copy(a, b, sems.at[n]) for n, (a, b) in enumerate(zip(held, out))]
    each, tiled = selectors(NZ, BX)
    each16, tiled16 = selectors(STRIP, BX)
    for xr in range(ROLES):
        k_ref, y_ref, xy_ref, z_ref = held[:4] if xr == 0 else held[4:]
        n = max(xr - 1, 0)
        for v in range(V):
            def fwd(yr, e):
                r = row_of(xr, yr, v, e)
                return taps_ref[r : r + 1, :]

            def bwd(yr, e):
                r = row_of(xr, yr, v, e)
                return back_ref[r : r + 1, :]

            outer = expand(toeplitz(bwd(0, 0), BX), each)
            inner = expand(toeplitz(bwd(0, 2), NZ), tiled) * (1.0 / V)
            kron_rows(k_ref.at[n, v], outer, inner, BX, NZ)
            y_ref[v, :, n * BY : (n + 1) * BY] = stack3(banded_y(fwd(0, 1)))
            for yr in (1, 2):
                outer = expand(toeplitz(fwd(yr, 0), BX), each16)
                inner = expand(toeplitz(fwd(yr, 1), STRIP), tiled16)
                kron_rows(xy_ref.at[n, yr - 1, v], outer, inner, BX, STRIP)
                z_ref[n, yr - 1, :, v * LANES : (v + 1) * LANES] = lanes3(
                    toeplitz(bwd(yr, 2), NZ) * (1.0 / V), NZ
                )
        if xr == 0:
            for copy in copies[:4]:
                copy.start()
    for copy in copies[4:]:
        copy.start()
    for copy in copies:
        copy.wait()


def pack_strip(field, shift):
    lane = iota((NZ, LANES), 1)
    halves = []
    for half in range(2):
        total = jnp.zeros((NZ, LANES), f32)
        for j in range(8):
            x = half * 8 + j
            moved = pltpu.roll(field[x * NZ : (x + 1) * NZ, :], shift + STRIP * j, 1)
            inside = jnp.logical_and(lane >= STRIP * j, lane < STRIP * (j + 1))
            total = jnp.where(inside, moved, total)
        halves.append(total)
    return jnp.concatenate(halves, axis=0)


def unpack_strip(halves, shift):
    lane = iota((NZ, LANES), 1)
    first = jnp.where(shift > 0, BY - STRIP, 0)
    inside = jnp.logical_and(lane >= first, lane < first + STRIP)
    rows = []
    for x in range(BX):
        half, j = x // 8, x % 8
        moved = pltpu.roll(halves[half * NZ : (half + 1) * NZ, :], 2 * LANES - shift - STRIP * j, 1)
        rows.append(jnp.where(inside, moved, 0.0))
    return jnp.concatenate(rows, axis=0)


def wide(halves):
    return jnp.concatenate([halves[:NZ], halves[NZ:]], axis=1)


def tall(strip):
    return jnp.concatenate([strip[:, :LANES], strip[:, LANES:]], axis=0)


def column3(a):
    hi, lo = split(a)
    return jnp.concatenate([hi, hi, lo, jnp.zeros_like(hi)], axis=0)


def two_rows(a, matrix):
    hi, lo = split(a)
    both = dot(jnp.concatenate([hi, lo], axis=0), matrix)
    return both[: a.shape[0]] + both[a.shape[0] :]


def two_lanes(matrix, a):
    hi, lo = split(a)
    both = dot(matrix, jnp.concatenate([hi, lo], axis=1))
    return both[:, :LANES] + both[:, LANES:]


def three_lanes(a, stacked):
    hi, lo = split(a)
    return dot(jnp.concatenate([hi, lo, hi], axis=1), stacked)


def forward_parts(sources, shifts, add):
    for field, _, (k, y, _, _) in sources:
        spread = three_lanes(field, y[...])
        for v in range(V):
            add(v, two_lanes(k[v], spread[:, v * BY : (v + 1) * BY]))
    for yr in range(2):
        totals = [jnp.zeros((NZ, 2 * LANES), f32) for _ in range(V)]
        for _, strips, (_, _, xy, z) in sources:
            along = dot(z[yr], column3(wide(strips[yr])))
            for v in range(V):
                totals[v] += two_rows(along[v * NZ : (v + 1) * NZ], xy[yr, v])
        for v in range(V):
            add(v, unpack_strip(tall(totals[v]), shifts[yr]))


def brick(refs, n):
    k, y, xy, z = refs
    return k.at[n], y.at[n], xy.at[n], z.at[n]


def adjoint_parts(count, quotient_ref, edge_ref, refs, ready=lambda v: None):
    k_ref, y_ref, xy_ref, z_ref = refs
    totals = [jnp.zeros((FIELD, LANES), f32) for _ in range(count)]
    for v in range(V):
        spread = three_lanes(quotient_ref[v], y_ref[v])
        ready(v)
        for n in range(count):
            totals[n] += two_lanes(k_ref[n, v], spread[:, n * BY : (n + 1) * BY])
    ready(V)
    strips = [[], []]
    for yr in range(2):
        packed = [wide(edge_ref[v, yr]) for v in range(V)]
        for n in range(count):
            parts = [column3(two_rows(packed[v], xy_ref[n, yr, v])) for v in range(V)]
            strips[yr].append(tall(dot(z_ref[n, yr], jnp.concatenate(parts, axis=0))))
    return totals, strips


def write_message(ref, field, strips):
    ref[:FIELD] = field
    for n in range(2):
        ref[FIELD + n * 2 * NZ : FIELD + (n + 1) * 2 * NZ] = strips[n]


def write_scaled(ref, field, strips):
    peak = jnp.max(jnp.abs(field), axis=0, keepdims=True)
    for strip in strips:
        peak = jnp.maximum(peak, jnp.max(jnp.abs(strip), axis=0, keepdims=True))
    peak = jnp.maximum(jnp.max(peak, axis=1, keepdims=True), 1e-30)
    power = PEAK - jnp.ceil(jnp.log2(peak))
    scale = jnp.exp2(power)
    write_message(ref, field * scale, [strip * scale for strip in strips])
    ref[FIELD + 4 * NZ :] = jnp.broadcast_to(power, (STRIP, LANES))


def read_scaled(ref):
    scale = jnp.exp2(-ref[FIELD + 4 * NZ : FIELD + 4 * NZ + 1, :1])
    return ref[: FIELD + 4 * NZ] * scale


def message_parts(message):
    return message[:FIELD], [message[FIELD : FIELD + 2 * NZ], message[FIELD + 2 * NZ :]]


def start_kernel(info_ref, estimate_ref, field_ref, first_ref, second_ref):
    for x in range(BX):
        field_ref[x * NZ : (x + 1) * NZ, :] = estimate_ref[:, x, :]
    field = field_ref[...]
    first_ref[...] = pack_strip(field, info_ref[0])
    second_ref[...] = pack_strip(field, info_ref[1])


def forward_first_kernel(info_ref, own_ref, first_ref, second_ref, *rest):
    far, result_ref, held, out_ref, sems = rest[:8], rest[8], rest[9:17], rest[17], rest[18]
    copies = [pltpu.make_async_copy(a, b, sems.at[n]) for n, (a, b) in enumerate(zip(far, held))]
    for copy in copies:
        copy.start()
    for copy in copies:
        copy.wait()
    center, sides = held[:4], held[4:]
    shifts = (info_ref[0], info_ref[1])
    out_ref[...] = jnp.zeros_like(out_ref)

    def add(v, part):
        out_ref[v] += part

    bricks = (brick(center, 0), brick(sides, 0), brick(sides, 1))
    messages = (own_ref[...], first_ref[...], second_ref[...])
    sources = [(*message_parts(m), matrices) for m, matrices in zip(messages, bricks)]
    forward_parts(sources, shifts, add)
    for v in range(V):
        out_ref[v] = 1.0 / out_ref[v]
    copy = pltpu.make_async_copy(out_ref, result_ref, sems.at[len(copies)])
    copy.start()
    copy.wait()


def adjoint_sides(quotient_ref, edge_ref, shifts, refs, first_ref, second_ref, ready=lambda v: None):
    for v in range(V):
        for yr in range(2):
            edge_ref[v, yr] = pack_strip(quotient_ref[v], shifts[yr])
    totals, strips = adjoint_parts(2, quotient_ref, edge_ref, refs, ready)
    write_message(first_ref, totals[0], [strips[0][0], strips[1][0]])
    write_scaled(second_ref, totals[1], [strips[0][1], strips[1][1]])


def quotient_first_kernel(info_ref, *refs):
    far, (data_ref, quotient_ref, edge_ref, first_ref, second_ref), held, sems = (
        refs[:7], refs[7:12], refs[12:19], refs[19],
    )
    pairs = list(zip(far[:4], held[:4]))
    pairs += [(far[6].at[:, v], held[6].at[:, v]) for v in range(V)]
    pairs += list(zip(far[4:6], held[4:6]))
    copies = [pltpu.make_async_copy(a, b, sems.at[n]) for n, (a, b) in enumerate(pairs)]
    for copy in copies:
        copy.start()
    table_ref, arrived_ref, inverse_ref, y_ref, xy_ref, z_ref, k_ref = held
    shifts = (info_ref[0], info_ref[1])
    copies[0].wait()
    copies[1].wait()
    planes = dot(table_ref[...], arrived_ref[...])
    copies[2].wait()
    for v in range(V):
        for x in range(BX):
            rows = slice(x * NZ, (x + 1) * NZ)
            piece = planes[v * NZ : (v + 1) * NZ, x * BY : (x + 1) * BY]
            data_ref[v, rows, :] = piece.astype(bf16)
            quotient_ref[v, rows, :] = piece * inverse_ref[v, rows, :]
    copies[3].wait()

    def ready(v):
        for copy in copies[4 + v : 5 + v] if v < V else copies[4 + V :]:
            copy.wait()

    adjoint_sides(
        quotient_ref, edge_ref, shifts, (k_ref, y_ref, xy_ref, z_ref), first_ref, second_ref, ready
    )


def adjoint_center_kernel(quotient_ref, edge_ref, k_ref, y_ref, xy_ref, z_ref, field_ref, strips_ref):
    totals, strips = adjoint_parts(1, quotient_ref, edge_ref, (k_ref, y_ref, xy_ref, z_ref))
    field_ref[...] = totals[0]
    strips_ref[0] = strips[0][0]
    strips_ref[1] = strips[1][0]


def gather_kernel(info_ref, field_ref, strips_ref, first_ref, second_ref, total_ref, up_ref, down_ref):
    second = read_scaled(second_ref)
    total = field_ref[...] + first_ref[:FIELD] + second[:FIELD]
    total_ref[...] = total
    for n, ref in enumerate((up_ref, down_ref)):
        rows = slice(FIELD + n * 2 * NZ, FIELD + (n + 1) * 2 * NZ)
        ref[: 2 * NZ] = strips_ref[n] + first_ref[rows] + second[rows]
        ref[2 * NZ :] = pack_strip(total, info_ref[n])


def gather_last_kernel(field_ref, strips_ref, first_ref, second_ref, total_ref, up_ref, down_ref):
    second = read_scaled(second_ref)
    total_ref[...] = field_ref[...] + first_ref[:FIELD] + second[:FIELD]
    for n, ref in enumerate((up_ref, down_ref)):
        rows = slice(FIELD + n * 2 * NZ, FIELD + (n + 1) * 2 * NZ)
        ref[...] = strips_ref[n] + first_ref[rows] + second[rows]


def update_kernel(
    info_ref, old_ref, total_ref, up_ref, down_ref, up_in_ref, down_in_ref, new_ref, scaled_ref
):
    half = 2 * NZ
    correction = total_ref[...]
    for n, ref in enumerate((up_in_ref, down_in_ref)):
        correction += unpack_strip(ref[:half], info_ref[n])
    field = old_ref[:FIELD] * correction
    strips = []
    for n, (ref, own) in enumerate(((up_in_ref, up_ref), (down_in_ref, down_ref))):
        rows = slice(FIELD + n * half, FIELD + (n + 1) * half)
        strips.append(old_ref[rows] * (ref[half:] + own[:half]))
    write_message(new_ref, field, strips)
    write_scaled(scaled_ref, field, strips)


def forward_center_kernel(info_ref, own_ref, k_ref, y_ref, xy_ref, z_ref, out_ref):
    shifts = (info_ref[0], info_ref[1])
    out_ref[...] = jnp.zeros_like(out_ref)

    def add(v, part):
        out_ref[v] += part

    forward_parts([(*message_parts(own_ref[...]), brick((k_ref, y_ref, xy_ref, z_ref), 0))], shifts, add)


def middle_kernel(
    info_ref, data_ref, blurred_ref, from_first_ref, from_second_ref,
    k_ref, y_ref, xy_ref, z_ref, ka_ref, ya_ref, xya_ref, za_ref,
    quotient_ref, edge_ref, first_ref, second_ref,
):
    shifts = (info_ref[0], info_ref[1])
    quotient_ref[...] = blurred_ref[...]

    def add(v, part):
        quotient_ref[v] += part

    refs = (k_ref, y_ref, xy_ref, z_ref)
    sources = [
        (*message_parts(from_first_ref[...]), brick(refs, 0)),
        (*message_parts(read_scaled(from_second_ref)), brick(refs, 1)),
    ]
    forward_parts(sources, shifts, add)
    for v in range(V):
        quotient_ref[v] = data_ref[v].astype(f32) / quotient_ref[v]
    adjoint_sides(quotient_ref, edge_ref, shifts, (ka_ref, ya_ref, xya_ref, za_ref), first_ref, second_ref)


def final_kernel(info_ref, old_ref, total_ref, up_in_ref, down_in_ref, out_ref):
    correction = total_ref[...]
    for n, ref in enumerate((up_in_ref, down_in_ref)):
        correction += unpack_strip(ref[...], info_ref[n])
    result = old_ref[:FIELD] * correction
    for x in range(BX):
        out_ref[:, x, :] = result[x * NZ : (x + 1) * NZ]


SMEM, VMEM, HBM = pltpu.SMEM, pltpu.VMEM, pltpu.HBM


def call(kernel, outs, *args, scalars=0, far=(), out_place=VMEM, scratch=(), cost=1.0):
    arrays = [(a.size, a.dtype) for a in (*args[scalars:], *far)]
    arrays += [(math.prod(s), d) for s, d in outs]
    need = sum(count * jnp.dtype(d).itemsize for count, d in arrays)
    specs = [pl.BlockSpec(memory_space=SMEM)] * scalars
    specs += [pl.BlockSpec(memory_space=VMEM)] * (len(args) - scalars)
    specs += [pl.BlockSpec(memory_space=HBM)] * len(far)
    args += tuple(pltpu.with_memory_space_constraint(a, HBM) for a in far)
    return pl.pallas_call(
        kernel,
        out_shape=[HBM(s, d) if out_place is HBM else jax.ShapeDtypeStruct(s, d) for s, d in outs],
        in_specs=specs,
        out_specs=[pl.BlockSpec(memory_space=out_place)] * len(outs),
        scratch_shapes=list(scratch),
        compiler_params=pltpu.CompilerParams(vmem_limit_bytes=need + WORKSPACE),
        cost_estimate=pl.CostEstimate(flops=0, bytes_accessed=int(cost * 3.5e6), transcendentals=0),
    )(*args)


def held(shapes):
    return [pltpu.VMEM(s, d) for s, d in shapes]


def partner_swaps(axis):
    count_x, count_y = lax.axis_size("gx"), lax.axis_size("gy")
    near, far = [], []
    for x in range(count_x):
        for y in range(count_y):
            me = x * count_y + y
            across, along = x * count_y + (y ^ 1), (x ^ 1) * count_y + y
            if axis == "gx":
                other = x - 1 if x % 2 == 0 else x + 1
                near.append((me, along))
                far.append((me, other * count_y + y if 0 <= other < count_x else across))
            else:
                other = y - 1 if y % 2 == 0 else y + 1
                near.append((me, across))
                far.append((me, x * count_y + other if 0 <= other < count_y else along))
    return near, far


def swap(axis, near_value, far_value):
    near, far = partner_swaps(axis)
    far_in = lax.ppermute(far_value, ("gx", "gy"), far)
    near_in = lax.ppermute(near_value, ("gx", "gy"), near)
    return near_in, far_in


def swap_x(near_value, far_value):
    near_in, far_in = swap("gx", near_value, far_value.astype(jnp.float16))
    return near_in, far_in.astype(f32)


def tap_tables(psf_taps, kernel_index):
    gx, gy = lax.axis_index("gx"), lax.axis_index("gy")
    even_x, even_y = gx % 2 == 0, gy % 2 == 0
    anchor = jnp.zeros((), i32)
    bordered = jnp.pad(kernel_index, ((1, 1), (1, 1), (0, 0), (0, 0)), constant_values=-1)
    around = lax.dynamic_slice(
        bordered, (gx.astype(i32), gy.astype(i32), anchor, anchor), (ROLES, ROLES, V, 3)
    )
    low, middle, high = around[:1], around[1:2], around[2:]
    around = jnp.where(
        even_x, jnp.concatenate([middle, high, low]), jnp.concatenate([middle, low, high])
    )
    low, middle, high = around[:, :1], around[:, 1:2], around[:, 2:]
    around = jnp.where(
        even_y, jnp.concatenate([middle, high, low], 1), jnp.concatenate([middle, low, high], 1)
    )
    normal = psf_taps / jnp.sum(psf_taps, axis=-1, keepdims=True)
    chosen = (around.reshape(-1)[:, None] == jnp.arange(psf_taps.shape[0], dtype=i32)).astype(f32)
    kernels = jnp.dot(chosen, normal, precision=lax.Precision.HIGHEST)
    kernels = jnp.pad(kernels, ((0, 0), (0, LANES - TAPS)))
    backward = jnp.pad(kernels[:, :TAPS][:, ::-1], ((0, 0), (0, LANES - TAPS)))
    role = jnp.arange(kernels.shape[0])
    axis, yr, xr = role % 3, role // (3 * V) % ROLES, role // (3 * V * ROLES)
    step = jnp.where(axis == 0, jnp.where(xr == 1, 1, jnp.where(xr == 2, -1, 0)), 0)
    step = step * jnp.where(even_x, 1, -1)
    step_y = jnp.where(axis == 1, jnp.where(yr == 1, 1, jnp.where(yr == 2, -1, 0)), 0)
    step = (step + step_y * jnp.where(even_y, 1, -1))[:, None]

    def moved(a, sign):
        return jnp.where(
            step * sign > 0, jnp.roll(a, -STRIP, 1), jnp.where(step * sign < 0, jnp.roll(a, STRIP, 1), a)
        )

    return moved(kernels, 1), moved(backward, -1)


def shards(estimate, stored, placement, psf_taps, kernel_index):
    devices_y = lax.axis_size("gy")
    devices = lax.axis_size("gx") * devices_y
    slots = stored.shape[0]
    cap = 2 * slots // devices
    rows = devices * cap
    plane = BX * BY
    me = (lax.axis_index("gx") * devices_y + lax.axis_index("gy")).astype(i32)

    half, message = (2 * NZ, LANES), (FIELD + 4 * NZ, LANES)
    scaled = (FIELD + 4 * NZ + STRIP, LANES)
    one, every = (FIELD, LANES), (V, FIELD, LANES)
    even_y = lax.axis_index("gy") % 2 == 0
    info = jnp.stack([jnp.where(even_y, STRIP, 0), jnp.where(even_y, 0, STRIP)]).astype(i32)
    field, up, down = call(start_kernel, [(one, f32), (half, f32), (half, f32)], info, estimate, scalars=1)
    up_in, down_in = swap("gy", up, down)
    slots_of = placement.reshape(devices, slots)
    (outgoing,) = call(
        functools.partial(route_kernel, cap),
        [((rows, plane), bf16)],
        me.reshape(1), slots_of, stored,
        scalars=1, scratch=[pltpu.VMEM((slots * BX, BY), f32)],
    )
    outgoing, up_in, down_in, psf_taps, kernel_index, slots_of = lax.optimization_barrier(
        (outgoing, up_in, down_in, psf_taps, kernel_index, slots_of)
    )
    arrived = lax.all_to_all(
        outgoing.reshape(devices, cap, plane), ("gx", "gy"), split_axis=0, concat_axis=0, tiled=True
    ).reshape(rows, plane)

    old = jnp.concatenate([field, up_in, down_in], axis=0)
    narrow = old.astype(jnp.float16)
    first, second = (a.astype(f32) for a in swap("gx", narrow, narrow))
    taps, backward = tap_tables(psf_taps, kernel_index)

    def shapes(y_of, z_shape):
        return [
            shape
            for count in (1, ROLES - 1)
            for shape in (
                ((count, V, FIELD, FIELD), bf16),
                (y_of(count), bf16),
                ((count, 2, V, 2 * LANES, 2 * LANES), bf16),
                ((count, 2) + z_shape, bf16),
            )
        ]

    forward_shapes = shapes(lambda n: (n, 3 * BY, V * BY), (V * NZ, LANES))
    adjoint_shapes = shapes(lambda n: (V, 3 * BY, n * BY), (NZ, V * LANES))
    sems = [pltpu.SemaphoreType.DMA((8,))]
    forward = call(
        build_forward_kernel, forward_shapes, taps, backward,
        out_place=HBM, scratch=held(forward_shapes) + sems, cost=3.0,
    )
    adjoint = call(
        build_adjoint_kernel, adjoint_shapes, taps, backward,
        out_place=HBM, scratch=held(adjoint_shapes) + sems, cost=3.0,
    )
    forward_center, forward_sides = forward[:4], forward[4:]
    adjoint_center, adjoint_sides = adjoint[:4], adjoint[4:]
    (inverse,) = call(
        forward_first_kernel, [(every, f32)], info, old, first, second,
        scalars=1, far=forward, out_place=HBM,
        scratch=held(forward_shapes) + [pltpu.VMEM(every, f32), pltpu.SemaphoreType.DMA((9,))], cost=5.0,
    )
    repeated = jnp.repeat(slots_of, cap, axis=0)
    (table,) = call(
        functools.partial(arrival_kernel, cap), [((slots, rows), bf16)], me.reshape(1), repeated, scalars=1,
        out_place=HBM, scratch=[pltpu.VMEM((slots, rows), bf16), pltpu.SemaphoreType.DMA],
    )

    edges = ((V, 2) + half, f32)
    k, y, xy, z = adjoint_sides
    fetched = (table, arrived, inverse, y, xy, z, k)
    outs = [(every, bf16), (every, f32), edges, (message, f32), (scaled, f32)]
    data, quotient, edge, first, second = call(
        quotient_first_kernel, outs, info, scalars=1, far=fetched,
        scratch=held([(a.shape, a.dtype) for a in fetched]) + [pltpu.SemaphoreType.DMA((len(fetched) + V - 1,))],
    )
    first, second = swap_x(first, second)
    center = [(one, f32), ((2,) + half, f32)]
    field, strips = call(adjoint_center_kernel, center, quotient, edge, *adjoint_center)
    both = (4 * NZ, LANES)
    total, up, down = call(
        gather_kernel, [(one, f32), (both, f32), (both, f32)],
        info, field, strips, first, second, scalars=1,
    )
    up_in, down_in = swap("gy", up, down)
    new, new_scaled = call(
        update_kernel, [(message, f32), (scaled, f32)],
        info, old, total, up, down, up_in, down_in, scalars=1,
    )
    first, second = swap_x(new, new_scaled)
    (blurred,) = call(forward_center_kernel, [(every, f32)], info, new, *forward_center, scalars=1)
    quotient, edge, first, second = call(
        middle_kernel, [(every, f32), edges, (message, f32), (scaled, f32)],
        info, data, blurred, first, second, *forward_sides, *adjoint_sides, scalars=1,
    )
    first, second = swap_x(first, second)
    field, strips = call(adjoint_center_kernel, center, quotient, edge, *adjoint_center)
    total, up, down = call(
        gather_last_kernel, [(one, f32), (half, f32), (half, f32)], field, strips, first, second
    )
    up_in, down_in = swap("gy", up, down)
    (refined,) = call(final_kernel, [(estimate.shape, f32)], info, new, total, up_in, down_in, scalars=1)
    return refined


def solution(mesh):
    return jax.shard_map(
        shards,
        mesh=mesh,
        in_specs=(P(None, "gx", "gy"), P(("gx", "gy"), None, None), P(), P(), P()),
        out_specs=P(None, "gx", "gy"),
        check_vma=False,
    )
```

time: 135 us -> 90.4 us (0.67)
  Pallas kernels: 82.5 us -> 49.8 us
  waiting for transfers between devices: 16.6 us -> 9.22 us
  local copies, waits for them, and re-layouts: 11.2 us -> 4.69 us
  starting transfers between devices: 20 us -> 23.9 us
  other arithmetic: 3.61 us -> 0.66 us
    pallas_call x15, Pallas kernels: 82.5 us -> 49.8 us  [call(): pl.pallas_call(kernel, out_shape=[HBM(s, d) if out_place is HBM else jax....]
    ppermute x14, waiting for transfers between devices: 16.6 us -> 9.22 us  [the longest x7 5.74 us: swap(): far_in = lax.ppermute(far_value, ('gx', 'gy'), far)]
    unnamed x44 -> x48, local copies, waits for them, and re-layouts: 7.67 us -> 3.77 us
    gather x4 -> x0, local copies, waits for them, and re-layouts: 2.29 us -> none  [the longest x2 1.15 us: tap_tables(): around = jnp.where(even_y, around[:, up], around[:, down])]
    ppermute x14, starting transfers between devices: 16.4 us -> 18.5 us  [the longest x7 10.3 us: swap(): far_in = lax.ppermute(far_value, ('gx', 'gy'), far)]
    all_to_all x1, starting transfers between devices: 3.59 us -> 5.41 us  [shards(): lax.all_to_all(outgoing.reshape(devices, cap, plane), ('gx', 'gy'), split...]
    reshape x1 -> x0, other arithmetic: 1.36 us -> none  [shards(): (own // slots).reshape(1, slots)]
  transfers between devices with their start and end apart: 15 -> 15, of which waited for: 7 -> 6; matrix products, arithmetic and copies ran while one was open for 7% -> 2% of each run, Pallas kernels for 36% -> 36%
where the time goes in v1:
time: 90.4 us; the launch traced here: 89 us
  Pallas kernels  49.8 us (55%)
  starting transfers between devices  23.9 us (26%)
  waiting for transfers between devices  9.22 us (10%)
  local copies, waits for them, and re-layouts  4.69 us (5%)
    pallas_call x15, Pallas kernels, call(): pl.pallas_call(kernel, out_shape=[HBM(s, d) if out_place is HBM else jax....  49.8 us
    ppermute x7, starting transfers between devices, swap(): far_in = lax.ppermute(far_value, ('gx', 'gy'), far)  10.3 us
    ppermute x7, starting transfers between devices, swap(): near_in = lax.ppermute(near_value, ('gx', 'gy'), near)  8.19 us
    ppermute x7, waiting for transfers between devices, swap(): far_in = lax.ppermute(far_value, ('gx', 'gy'), far)  5.74 us
    all_to_all x1, starting transfers between devices, shards(): lax.all_to_all(outgoing.reshape(devices, cap, plane), ('gx', 'gy'), split...  5.41 us
    unnamed x48, local copies, waits for them, and re-layouts  3.77 us
    ppermute x7, waiting for transfers between devices, swap(): near_in = lax.ppermute(near_value, ('gx', 'gy'), near)  3.47 us
  transfers between devices with their start and end apart: 15, of which 6 were waited for; matrix products, arithmetic and copies ran while one was open for 2% of the time, Pallas kernels for 36%

profile of v1, /device:TPU:0, one launch (start us, length us, event | category | flops | bytes accessed | tf_op | source)
XLA Modules:
  0.0 89.0 jit_solution(7021577773677238312)
XLA Ops:
  0.1 0.9 %copy-done.17 = f32[32,16,128]{2,1,0:T(8,128)S(1)} copy-done((f32[32,16,128]{2,1,0:T(8,128)S(1)}, f32[32,16,128]{2,1,0:T(8,128)}, u32[]{:S(2)}) %copy-start.17) | copy-done | bytes 262168
  1.0 0.8 shard_map.55
  1.8 3.1 %collective-permute-start = (f32[64,128]{1,0:T(8,128)S(1)}, f32[64,128]{1,0:T(8,128)S(1)}, u32[]{:S(2)}, u32[]{:S(2)}) collective-permute-start(f32[64,128]{1,0:T(8,128)S(1)} %get-tuple-element.52), channel_id=1, source_target_pairs={{0,1},{1,0},{2,3},{3,2},{4,5},{5,4},{6,7},{7,6},{8,9},{9,8},{10,11... | collective-permute-start | bytes 98312 | tf_op jit(solution)/shard_map/ppermute | solution.py:523
  5.0 1.0 %copy-done.14 = bf16[128,16,128]{2,1,0:T(8,128)(2,1)S(1)} copy-done((bf16[128,16,128]{2,1,0:T(8,128)(2,1)S(1)}, bf16[128,16,128]{2,1,0:T(8,128)(2,1)}, u32[]{:S(2)}) %copy-start.14) | copy-done | bytes 524312
  6.8 1.7 %shard_map.56 = bf16[256,2048]{1,0:T(8,128)(2,1)} custom-call(s32[1]{0:T(128)} %bitcast.2.me_ref, s32[32,128]{1,0:T(8,128)S(1)} %bitcast.8, bf16[128,16,128]{2,1,0:T(8,128)(2,1)S(1)} %copy-done.14), custom_call_target="tpu_custom_call" | custom-call | bytes 3500000 | tf_op jit(solution)/shard_map/pallas_call | solution.py:487
  8.4 5.4 %all-to-all-start = ((bf16[32,8,2048]{2,1,0:T(8,128)(2,1)}), bf16[32,8,2048]{2,1,0:T(8,128)(2,1)S(1)}, u32[]{:S(2)}, u32[]{:S(2)}) async-start(bf16[32,8,2048]{2,1,0:T(8,128)(2,1)} %bitcast.5), calls=%async_computation | async-start | bytes 2097152 | tf_op jit(solution)/shard_map/all_to_all | solution.py:594
  13.9 1.8 %collective-permute-start.3 = (f16[640,128]{1,0:T(8,128)(2,1)S(1)}, f16[640,128]{1,0:T(8,128)(2,1)S(1)}, u32[]{:S(2)}, u32[]{:S(2)}) collective-permute-start(f16[640,128]{1,0:T(8,128)(2,1)S(1)} %convert_element_type.31), channel_id=1, source_target_pairs={{0,1},{1,0},{2,3},{3,2},{4,8},{5,9},{6,10},{7,11},{8,4},{9,5},{10,... | collective-permute-start | bytes 491528 | tf_op jit(solution)/shard_map/ppermute | solution.py:522
  17.4 6.9 %shard_map.60 = (bf16[1,4,512,512]{3,2,1,0:T(8,128)(2,1)}, bf16[4,384,128]{2,1,0:T(8,128)(2,1)}, bf16[1,2,4,256,256]{4,3,2,1,0:T(8,128)(2,1)}, bf16[1,2,32,512]{...) custom-call(f32[108,128]{1,0:T(8,128)S(1)} %get-tuple-element.114.ta, ...), custom_call_target="tpu_custom_call" | custom-call | bytes 10500000 | tf_op jit(solution)/shard_map/pallas_call | solution.py:487
  24.3 6.6 %shard_map.58 = (bf16[1,4,512,512]{3,2,1,0:T(8,128)(2,1)}, bf16[1,384,512]{2,1,0:T(8,128)(2,1)}, bf16[1,2,4,256,256]{4,3,2,1,0:T(8,128)(2,1)}, bf16[1,2,128,128]...) custom-call(f32[108,128]{1,0:T(8,128)S(1)} %get-tuple-element.114.ta, ...), custom_call_target="tpu_custom_call" | custom-call | bytes 10500000 | tf_op jit(solution)/shard_map/pallas_call | solution.py:487
  30.9 1.0 %shard_map.57.refs_0_ = bf16[128,256]{1,0:T(8,128)(2,1)} custom-call(s32[1]{0:T(128)} %bitcast.2.me_ref, s32[256,128]{1,0:T(8,128)S(1)} %broadcast_bitcast_fusion.slots_ref), custom_call_target="tpu_custom_call" | custom-call | bytes 3500000 | tf_op jit(solution)/shard_map/pallas_call | solution.py:487
  31.9 1.4 %collective-permute-done.3 = f16[640,128]{1,0:T(8,128)(2,1)S(1)} collective-permute-done((f16[640,128]{1,0:T(8,128)(2,1)S(1)}, f16[640,128]{1,0:T(8,128)(2,1)S(1)}, u32[]{:S(2)}, u32[]{:S(2)}) %collective-permute-start.3) | collective-permute-done | bytes 163872 | tf_op jit(solution)/shard_map/ppermute | solution.py:522
  33.3 10.0 %shard_map.59.refs_2_ = f32[4,512,128]{2,1,0:T(8,128)} custom-call(s32[2]{0:T(128)S(1)} %pad_add_fusion.info_ref, f32[640,128]{1,0:T(8,128)S(1)} %constant_dynamic-update-slice_fusion.own_ref.old_ref, f32[640,128]{1,0:T(8,128)S(1)} %convert_element_type.32.first_ref, f32[640,128]{1,0:T(8,128)S(1)} %convert_element_type.33.second_ref, ...), custom_call_target="tpu_custom_call" | custom-call | bytes 17500000 | tf_op jit(solution)/shard_map/pallas_call | solution.py:487
  43.3 1.0 %copy-done.20 = bf16[32,8,2048]{2,1,0:T(8,128)(2,1)} copy-done((bf16[32,8,2048]{2,1,0:T(8,128)(2,1)}, bf16[32,8,2048]{2,1,0:T(8,128)(2,1)S(1)}, u32[]{:S(2)}) %copy-start.20) | copy-done | bytes 1048600
  44.3 7.2 %shard_map.61 = (bf16[4,512,128]{2,1,0:T(8,128)(2,1)S(1)}, f32[4,512,128]{2,1,0:T(8,128)S(1)}, f32[4,2,64,128]{3,2,1,0:T(8,128)S(1)}, f32[640,128]{1,0:T(8,128)S(1)}, f32[656,128]{1,0:T(8,128)S(1)}) custom-call(s32[2]{0:T(128)S(1)} %pad_add_fusion.info_ref, bf16[128,256]{1,0:T(8,128)(2,1)} %shard_map.57.refs_0_, bf16[256,2048]{1,0:T(8,128)(2,1)} %bitcast.10, ...), custom_call_target="tpu_custom_call" | custom-call | bytes 3500000 | tf_op jit(solution)/shard_map/pallas_call | solution.py:487
  51.6 2.5 %collective-permute-start.5 = (f16[656,128]{1,0:T(8,128)(2,1)S(1)}, f16[656,128]{1,0:T(8,128)(2,1)S(1)}, u32[]{:S(2)}, u32[]{:S(2)}) collective-permute-start(f16[656,128]{1,0:T(8,128)(2,1)S(1)} %convert_element_type.34), channel_id=1, source_target_pairs={{0,1},{1,0},{2,3},{3,2},{4,8},{5,9},{6,10},{7,11},{8,4},{9,5},{10,... | collective-permute-start | bytes 503816 | tf_op jit(solution)/shard_map/ppermute | solution.py:522
  54.2 1.6 %shard_map.62 = (f32[512,128]{1,0:T(8,128)S(1)}, f32[2,64,128]{2,1,0:T(8,128)S(1)}) custom-call(f32[4,512,128]{2,1,0:T(8,128)S(1)} %get-tuple-element.72.quotient_ref, f32[4,2,64,128]{3,2,1,0:T(8,128)S(1)} %get-tuple-element.73.edge_ref, bf16[1,4,512,512]{3,2,1,0:T(8,128)(2,1)S(1)} %copy-done.3, bf16[4,384,128]{2,1,0:T(8,128)(2,1)S(1)} %copy-done.11, ...), custom_call_target="tpu_custom_call" | custom-call | bytes 3500000 | tf_op jit(solution)/shard_map/pallas_call | solution.py:487
  55.8 1.7 %collective-permute-done.5 = f16[656,128]{1,0:T(8,128)(2,1)S(1)} collective-permute-done((f16[656,128]{1,0:T(8,128)(2,1)S(1)}, f16[656,128]{1,0:T(8,128)(2,1)S(1)}, u32[]{:S(2)}, u32[]{:S(2)}) %collective-permute-start.5) | collective-permute-done | bytes 167968 | tf_op jit(solution)/shard_map/ppermute | solution.py:522
  57.6 0.8 shard_map.63
  58.4 2.1 %collective-permute-start.6 = (f32[128,128]{1,0:T(8,128)S(1)}, f32[128,128]{1,0:T(8,128)S(1)}, u32[]{:S(2)}, u32[]{:S(2)}) collective-permute-start(f32[128,128]{1,0:T(8,128)S(1)} %get-tuple-element.83.up_ref), channel_id=1, source_target_pairs={{0,1},{1,0},{2,3},{3,2},{4,5},{5,4},{6,7},{7,6},{8,9},{9,8},{10,11... | collective-permute-start | bytes 196616 | tf_op jit(solution)/shard_map/ppermute | solution.py:523
  60.5 2.4 %collective-permute-done.6.up_in_ref = f32[128,128]{1,0:T(8,128)S(1)} collective-permute-done((f32[128,128]{1,0:T(8,128)S(1)}, f32[128,128]{1,0:T(8,128)S(1)}, u32[]{:S(2)}, u32[]{:S(2)}) %collective-permute-start.6) | collective-permute-done | bytes 65568 | tf_op jit(solution)/shard_map/ppermute | solution.py:523
  62.8 0.9 shard_map.64
  63.9 2.7 %collective-permute-start.9 = (f16[656,128]{1,0:T(8,128)(2,1)S(1)}, f16[656,128]{1,0:T(8,128)(2,1)S(1)}, u32[]{:S(2)}, u32[]{:S(2)}) collective-permute-start(f16[656,128]{1,0:T(8,128)(2,1)S(1)} %convert_element_type.36), channel_id=1, source_target_pairs={{0,1},{1,0},{2,3},{3,2},{4,8},{5,9},{6,10},{7,11},{8,4},{9,5},{10,... | collective-permute-start | bytes 503816 | tf_op jit(solution)/shard_map/ppermute | solution.py:522
  66.6 2.4 %shard_map.65.blurred_ref = f32[4,512,128]{2,1,0:T(8,128)S(1)} custom-call(s32[2]{0:T(128)S(1)} %pad_add_fusion.info_ref, f32[640,128]{1,0:T(8,128)S(1)} %get-tuple-element.85.own_ref.old_ref, bf16[1,4,512,512]{3,2,1,0:T(8,128)(2,1)S(1)} %copy-done.4, bf16[1,384,512]{2,1,0:T(8,128)(2,1)S(1)} %copy-done.10, bf16[1,2,4,256,256]{4,3,2,1,0:T(8,128)(2,1)S(1)} %copy-done.7, ...), custom_call_target="tpu_custom_call" | custom-call | bytes 3500000 | tf_op jit(solution)/shard_map/pallas_call | solution.py:487
  69.0 0.9 %collective-permute-done.9 = f16[656,128]{1,0:T(8,128)(2,1)S(1)} collective-permute-done((f16[656,128]{1,0:T(8,128)(2,1)S(1)}, f16[656,128]{1,0:T(8,128)(2,1)S(1)}, u32[]{:S(2)}, u32[]{:S(2)}) %collective-permute-start.9) | collective-permute-done | bytes 167968 | tf_op jit(solution)/shard_map/ppermute | solution.py:522
  70.0 6.9 %shard_map.66 = (f32[4,512,128]{2,1,0:T(8,128)S(1)}, f32[4,2,64,128]{3,2,1,0:T(8,128)S(1)}, f32[640,128]{1,0:T(8,128)S(1)}, f32[656,128]{1,0:T(8,128)S(1)}) custom-call(s32[2]{0:T(128)S(1)} %pad_add_fusion.info_ref, bf16[4,512,128]{2,1,0:T(8,128)(2,1)S(1)} %get-tuple-element.86.data_ref, f32[4,512,128]{2,1,0:T(8,128)S(1)} %shard_map.65.blurred_ref, ...), custom_call_target="tpu_custom_call" | custom-call | bytes 3500000 | tf_op jit(solution)/shard_map/pallas_call | solution.py:487
  77.6 2.4 %collective-permute-start.11 = (f16[656,128]{1,0:T(8,128)(2,1)S(1)}, f16[656,128]{1,0:T(8,128)(2,1)S(1)}, u32[]{:S(2)}, u32[]{:S(2)}) collective-permute-start(f16[656,128]{1,0:T(8,128)(2,1)S(1)} %convert_element_type.38), channel_id=1, source_target_pairs={{0,1},{1,0},{2,3},{3,2},{4,8},{5,9},{6,10},{7,11},{8,4},{9,5},{10,... | collective-permute-start | bytes 503816 | tf_op jit(solution)/shard_map/ppermute | solution.py:522
  80.0 1.6 %shard_map.67 = (f32[512,128]{1,0:T(8,128)S(1)}, f32[2,64,128]{2,1,0:T(8,128)S(1)}) custom-call(f32[4,512,128]{2,1,0:T(8,128)S(1)} %get-tuple-element.88.quotient_ref, f32[4,2,64,128]{3,2,1,0:T(8,128)S(1)} %get-tuple-element.89.edge_ref, bf16[1,4,512,512]{3,2,1,0:T(8,128)(2,1)S(1)} %copy-done.3, bf16[4,384,128]{2,1,0:T(8,128)(2,1)S(1)} %copy-done.11, ...), custom_call_target="tpu_custom_call" | custom-call | bytes 3500000 | tf_op jit(solution)/shard_map/pallas_call | solution.py:487
  81.6 1.7 %collective-permute-done.11 = f16[656,128]{1,0:T(8,128)(2,1)S(1)} collective-permute-done((f16[656,128]{1,0:T(8,128)(2,1)S(1)}, f16[656,128]{1,0:T(8,128)(2,1)S(1)}, u32[]{:S(2)}, u32[]{:S(2)}) %collective-permute-start.11) | collective-permute-done | bytes 167968 | tf_op jit(solution)/shard_map/ppermute | solution.py:522
  83.5 2.1 %collective-permute-start.12 = (f32[64,128]{1,0:T(8,128)S(1)}, f32[64,128]{1,0:T(8,128)S(1)}, u32[]{:S(2)}, u32[]{:S(2)}) collective-permute-start(f32[64,128]{1,0:T(8,128)S(1)} %get-tuple-element.95), channel_id=1, source_target_pairs={{0,1},{1,0},{2,3},{3,2},{4,5},{5,4},{6,7},{7,6},{8,9},{9,8},{10,11... | collective-permute-start | bytes 98312 | tf_op jit(solution)/shard_map/ppermute | solution.py:523
  85.6 0.8 collective-permute-start.13
  86.4 1.1 %collective-permute-done.12.up_in_ref = f32[64,128]{1,0:T(8,128)S(1)} collective-permute-done((f32[64,128]{1,0:T(8,128)S(1)}, f32[64,128]{1,0:T(8,128)S(1)}, u32[]{:S(2)}, u32[]{:S(2)}) %collective-permute-start.12) | collective-permute-done | bytes 32800 | tf_op jit(solution)/shard_map/ppermute | solution.py:523
  87.5 1.6 %shard_map.69 = f32[32,16,128]{2,1,0:T(8,128)} custom-call(s32[2]{0:T(128)S(1)} %pad_add_fusion.info_ref, f32[640,128]{1,0:T(8,128)S(1)} %get-tuple-element.85.own_ref.old_ref, f32[512,128]{1,0:T(8,128)S(1)} %get-tuple-element.94.total_ref, f32[64,128]{1,0:T(8,128)S(1)} %collective-permute-done.12.up_in_ref, f32[64,128]{1,0:T(8,128)S(1)} %collective-permute-done.13.down_in_ref), custom_call_target="tpu_custom_call" | custom-call | bytes 3500000 | tf_op jit(solution)/shard_map/pallas_call | solution.py:487
  (91 shorter events, 3.7 us)
Async XLA Ops:
  1.8 6.6 %collective-permute-start = (f32[64,128]{1,0:T(8,128)S(1)}, f32[64,128]{1,0:T(8,128)S(1)}, u32[]{:S(2)}, u32[]{:S(2)}) collective-permute-start(f32[64,128]{1,0:T(8,128)S(1)} %get-tuple-element.52), channel_id=1, source_target_pairs={{0,1},{1,0},{2,3},{3,2},{4,5},{5,4},{6,7},{7,6},{8,9},{9,8},{10,11... | collective-permute-start | bytes 98312 | tf_op jit(solution)/shard_map/ppermute | solution.py:523
  4.9 3.5 %collective-permute-start.1 = (f32[64,128]{1,0:T(8,128)S(1)}, f32[64,128]{1,0:T(8,128)S(1)}, u32[]{:S(2)}, u32[]{:S(2)}) collective-permute-start(f32[64,128]{1,0:T(8,128)S(1)} %get-tuple-element.53), channel_id=1, source_target_pairs={{0,4},{1,2},{2,1},{3,7},{4,0},{5,6},{6,5},{7,3},{8,12},{9,10},{10,... | collective-permute-start | bytes 98312 | tf_op jit(solution)/shard_map/ppermute | solution.py:522
  6.8 9.1 %copy-start.21 = (s32[8,4,4,3]{0,2,3,1:T(4,128)S(1)}, s32[8,4,4,3]{0,2,3,1:T(4,128)}, u32[]{:S(2)}) copy-start(s32[8,4,4,3]{0,2,3,1:T(4,128)} %param.9) | copy-start | bytes 4612
  6.8 9.7 %copy-start.22 = (f32[48,31]{0,1:T(8,128)S(1)}, f32[48,31]{0,1:T(8,128)}, u32[]{:S(2)}) copy-start(f32[48,31]{0,1:T(8,128)} %param.8) | copy-start | bytes 17860
  8.4 22.4 %copy-start.19 = (s32[4096]{0:T(1024)S(1)}, s32[4096]{0:T(1024)}, u32[]{:S(2)}) copy-start(s32[4096]{0:T(1024)} %param.7) | copy-start | bytes 49156
  8.4 34.8 %all-to-all-start = ((bf16[32,8,2048]{2,1,0:T(8,128)(2,1)}), bf16[32,8,2048]{2,1,0:T(8,128)(2,1)S(1)}, u32[]{:S(2)}, u32[]{:S(2)}) async-start(bf16[32,8,2048]{2,1,0:T(8,128)(2,1)} %bitcast.5), calls=%async_computation | async-start | bytes 2097152 | tf_op jit(solution)/shard_map/all_to_all | solution.py:594
  13.9 19.3 %collective-permute-start.3 = (f16[640,128]{1,0:T(8,128)(2,1)S(1)}, f16[640,128]{1,0:T(8,128)(2,1)S(1)}, u32[]{:S(2)}, u32[]{:S(2)}) collective-permute-start(f16[640,128]{1,0:T(8,128)(2,1)S(1)} %convert_element_type.31), channel_id=1, source_target_pairs={{0,1},{1,0},{2,3},{3,2},{4,8},{5,9},{6,10},{7,11},{8,4},{9,5},{10,... | collective-permute-start | bytes 491528 | tf_op jit(solution)/shard_map/ppermute | solution.py:522
  15.8 17.5 %collective-permute-start.2 = (f16[640,128]{1,0:T(8,128)(2,1)S(1)}, f16[640,128]{1,0:T(8,128)(2,1)S(1)}, u32[]{:S(2)}, u32[]{:S(2)}) collective-permute-start(f16[640,128]{1,0:T(8,128)(2,1)S(1)} %convert_element_type.31), channel_id=1, source_target_pairs={{0,4},{1,5},{2,6},{3,7},{4,0},{5,1},{6,2},{7,3},{8,12},{9,13},{10,... | collective-permute-start | bytes 491528 | tf_op jit(solution)/shard_map/ppermute | solution.py:523
  44.3 9.9 %copy-start.3 = (bf16[1,4,512,512]{3,2,1,0:T(8,128)(2,1)S(1)}, bf16[1,4,512,512]{3,2,1,0:T(8,128)(2,1)}, u32[]{:S(2)}) copy-start(bf16[1,4,512,512]{3,2,1,0:T(8,128)(2,1)} %get-tuple-element.74.k_ref) | copy-start | bytes 6291460
  44.3 9.9 %copy-start.6 = (bf16[1,2,4,256,256]{4,3,2,1,0:T(8,128)(2,1)S(1)}, bf16[1,2,4,256,256]{4,3,2,1,0:T(8,128)(2,1)}, u32[]{:S(2)}) copy-start(bf16[1,2,4,256,256]{4,3,2,1,0:T(8,128)(2,1)} %get-tuple-element.76.xy_ref) | copy-start | bytes 3145732
  44.3 9.9 %copy-start.11 = (bf16[4,384,128]{2,1,0:T(8,128)(2,1)S(1)}, bf16[4,384,128]{2,1,0:T(8,128)(2,1)}, u32[]{:S(2)}) copy-start(bf16[4,384,128]{2,1,0:T(8,128)(2,1)} %get-tuple-element.75.y_ref) | copy-start | bytes 1179652
  44.3 9.9 %copy-start.15 = (bf16[1,2,32,512]{3,2,1,0:T(8,128)(2,1)S(1)}, bf16[1,2,32,512]{3,2,1,0:T(8,128)(2,1)}, u32[]{:S(2)}) copy-start(bf16[1,2,32,512]{3,2,1,0:T(8,128)(2,1)} %get-tuple-element.77.z_ref) | copy-start | bytes 196612
  44.3 22.3 %copy-start.10 = (bf16[1,384,512]{2,1,0:T(8,128)(2,1)S(1)}, bf16[1,384,512]{2,1,0:T(8,128)(2,1)}, u32[]{:S(2)}) copy-start(bf16[1,384,512]{2,1,0:T(8,128)(2,1)} %get-tuple-element.61.rest_1_.y_ref) | copy-start | bytes 1179652
  44.3 22.3 %copy-start.16 = (bf16[1,2,128,128]{3,2,1,0:T(8,128)(2,1)S(1)}, bf16[1,2,128,128]{3,2,1,0:T(8,128)(2,1)}, u32[]{:S(2)}) copy-start(bf16[1,2,128,128]{3,2,1,0:T(8,128)(2,1)} %get-tuple-element.63.rest_3_.z_ref) | copy-start | bytes 196612
  44.3 25.6 %copy-start.5 = (bf16[2,2,4,256,256]{4,3,2,1,0:T(8,128)(2,1)S(1)}, bf16[2,2,4,256,256]{4,3,2,1,0:T(8,128)(2,1)}, u32[]{:S(2)}) copy-start(bf16[2,2,4,256,256]{4,3,2,1,0:T(8,128)(2,1)} %get-tuple-element.69.refs_4_.xya_ref) | copy-start | bytes 6291460
  44.3 25.6 %copy-start.8 = (bf16[4,384,256]{2,1,0:T(8,128)(2,1)S(1)}, bf16[4,384,256]{2,1,0:T(8,128)(2,1)}, u32[]{:S(2)}) copy-start(bf16[4,384,256]{2,1,0:T(8,128)(2,1)} %get-tuple-element.68.refs_3_.ya_ref) | copy-start | bytes 2359300
  44.3 25.6 %copy-start.9 = (bf16[2,384,512]{2,1,0:T(8,128)(2,1)S(1)}, bf16[2,384,512]{2,1,0:T(8,128)(2,1)}, u32[]{:S(2)}) copy-start(bf16[2,384,512]{2,1,0:T(8,128)(2,1)} %get-tuple-element.65.rest_5_.y_ref) | copy-start | bytes 2359300
  44.3 25.6 %copy-start.13 = (bf16[2,2,128,128]{3,2,1,0:T(8,128)(2,1)S(1)}, bf16[2,2,128,128]{3,2,1,0:T(8,128)(2,1)}, u32[]{:S(2)}) copy-start(bf16[2,2,128,128]{3,2,1,0:T(8,128)(2,1)} %get-tuple-element.67.rest_7_.z_ref) | copy-start | bytes 393220
  51.5 6.0 %collective-permute-start.4 = (f32[640,128]{1,0:T(8,128)S(1)}, f32[640,128]{1,0:T(8,128)S(1)}, u32[]{:S(2)}, u32[]{:S(2)}) collective-permute-start(f32[640,128]{1,0:T(8,128)S(1)} %get-tuple-element.80), channel_id=1, source_target_pairs={{0,4},{1,5},{2,6},{3,7},{4,0},{5,1},{6,2},{7,3},{8,12},{9,13},{10,... | collective-permute-start | bytes 983048 | tf_op jit(solution)/shard_map/ppermute | solution.py:523
  51.6 15.0 %copy-start.7 = (bf16[1,2,4,256,256]{4,3,2,1,0:T(8,128)(2,1)S(1)}, bf16[1,2,4,256,256]{4,3,2,1,0:T(8,128)(2,1)}, u32[]{:S(2)}) copy-start(bf16[1,2,4,256,256]{4,3,2,1,0:T(8,128)(2,1)} %get-tuple-element.62.rest_2_.xy_ref) | copy-start | bytes 3145732
  51.6 5.9 %collective-permute-start.5 = (f16[656,128]{1,0:T(8,128)(2,1)S(1)}, f16[656,128]{1,0:T(8,128)(2,1)S(1)}, u32[]{:S(2)}, u32[]{:S(2)}) collective-permute-start(f16[656,128]{1,0:T(8,128)(2,1)S(1)} %convert_element_type.34), channel_id=1, source_target_pairs={{0,1},{1,0},{2,3},{3,2},{4,8},{5,9},{6,10},{7,11},{8,4},{9,5},{10,... | collective-permute-start | bytes 503816 | tf_op jit(solution)/shard_map/ppermute | solution.py:522
  54.2 12.4 %copy-start.4 = (bf16[1,4,512,512]{3,2,1,0:T(8,128)(2,1)S(1)}, bf16[1,4,512,512]{3,2,1,0:T(8,128)(2,1)}, u32[]{:S(2)}) copy-start(bf16[1,4,512,512]{3,2,1,0:T(8,128)(2,1)} %get-tuple-element.60.rest_0_.k_ref) | copy-start | bytes 6291460
  54.2 15.8 %copy-start.1 = (bf16[2,4,512,512]{3,2,1,0:T(8,128)(2,1)S(1)}, bf16[2,4,512,512]{3,2,1,0:T(8,128)(2,1)}, u32[]{:S(2)}) copy-start(bf16[2,4,512,512]{3,2,1,0:T(8,128)(2,1)} %get-tuple-element.64.rest_4_.k_ref) | copy-start | bytes 12582916
  58.4 4.5 %collective-permute-start.6 = (f32[128,128]{1,0:T(8,128)S(1)}, f32[128,128]{1,0:T(8,128)S(1)}, u32[]{:S(2)}, u32[]{:S(2)}) collective-permute-start(f32[128,128]{1,0:T(8,128)S(1)} %get-tuple-element.83.up_ref), channel_id=1, source_target_pairs={{0,1},{1,0},{2,3},{3,2},{4,5},{5,4},{6,7},{7,6},{8,9},{9,8},{10,11... | collective-permute-start | bytes 196616 | tf_op jit(solution)/shard_map/ppermute | solution.py:523
  60.5 2.4 %collective-permute-start.7 = (f32[128,128]{1,0:T(8,128)S(1)}, f32[128,128]{1,0:T(8,128)S(1)}, u32[]{:S(2)}, u32[]{:S(2)}) collective-permute-start(f32[128,128]{1,0:T(8,128)S(1)} %get-tuple-element.84.down_ref), channel_id=1, source_target_pairs={{0,4},{1,2},{2,1},{3,7},{4,0},{5,6},{6,5},{7,3},{8,12},{9,10},{10,... | collective-permute-start | bytes 196616 | tf_op jit(solution)/shard_map/ppermute | solution.py:522
  62.8 7.2 %copy-start.2 = (bf16[2,2,4,256,256]{4,3,2,1,0:T(8,128)(2,1)S(1)}, bf16[2,2,4,256,256]{4,3,2,1,0:T(8,128)(2,1)}, u32[]{:S(2)}) copy-start(bf16[2,2,4,256,256]{4,3,2,1,0:T(8,128)(2,1)} %get-tuple-element.66.rest_6_.xy_ref) | copy-start | bytes 6291460
  63.7 6.2 %collective-permute-start.8 = (f32[640,128]{1,0:T(8,128)S(1)}, f32[640,128]{1,0:T(8,128)S(1)}, u32[]{:S(2)}, u32[]{:S(2)}) collective-permute-start(f32[640,128]{1,0:T(8,128)S(1)} %get-tuple-element.85.own_ref.old_ref), channel_id=1, source_target_pairs={{0,4},{1,5},{2,6},{3,7},{4,0},{5,1},{6,2},{7,3},{8,12},{9,13},{10,... | collective-permute-start | bytes 983048 | tf_op jit(solution)/shard_map/ppermute | solution.py:523
  63.9 6.1 %collective-permute-start.9 = (f16[656,128]{1,0:T(8,128)(2,1)S(1)}, f16[656,128]{1,0:T(8,128)(2,1)S(1)}, u32[]{:S(2)}, u32[]{:S(2)}) collective-permute-start(f16[656,128]{1,0:T(8,128)(2,1)S(1)} %convert_element_type.36), channel_id=1, source_target_pairs={{0,1},{1,0},{2,3},{3,2},{4,8},{5,9},{6,10},{7,11},{8,4},{9,5},{10,... | collective-permute-start | bytes 503816 | tf_op jit(solution)/shard_map/ppermute | solution.py:522
  76.9 6.5 %collective-permute-start.10 = (f32[640,128]{1,0:T(8,128)S(1)}, f32[640,128]{1,0:T(8,128)S(1)}, u32[]{:S(2)}, u32[]{:S(2)}) collective-permute-start(f32[640,128]{1,0:T(8,128)S(1)} %get-tuple-element.92), channel_id=1, source_target_pairs={{0,4},{1,5},{2,6},{3,7},{4,0},{5,1},{6,2},{7,3},{8,12},{9,13},{10,... | collective-permute-start | bytes 983048 | tf_op jit(solution)/shard_map/ppermute | solution.py:523
  77.6 5.8 %collective-permute-start.11 = (f16[656,128]{1,0:T(8,128)(2,1)S(1)}, f16[656,128]{1,0:T(8,128)(2,1)S(1)}, u32[]{:S(2)}, u32[]{:S(2)}) collective-permute-start(f16[656,128]{1,0:T(8,128)(2,1)S(1)} %convert_element_type.38), channel_id=1, source_target_pairs={{0,1},{1,0},{2,3},{3,2},{4,8},{5,9},{6,10},{7,11},{8,4},{9,5},{10,... | collective-permute-start | bytes 503816 | tf_op jit(solution)/shard_map/ppermute | solution.py:522
  83.5 4.0 %collective-permute-start.12 = (f32[64,128]{1,0:T(8,128)S(1)}, f32[64,128]{1,0:T(8,128)S(1)}, u32[]{:S(2)}, u32[]{:S(2)}) collective-permute-start(f32[64,128]{1,0:T(8,128)S(1)} %get-tuple-element.95), channel_id=1, source_target_pairs={{0,1},{1,0},{2,3},{3,2},{4,5},{5,4},{6,7},{7,6},{8,9},{9,8},{10,11... | collective-permute-start | bytes 98312 | tf_op jit(solution)/shard_map/ppermute | solution.py:523
  85.6 1.9 %collective-permute-start.13 = (f32[64,128]{1,0:T(8,128)S(1)}, f32[64,128]{1,0:T(8,128)S(1)}, u32[]{:S(2)}, u32[]{:S(2)}) collective-permute-start(f32[64,128]{1,0:T(8,128)S(1)} %get-tuple-element.96), channel_id=1, source_target_pairs={{0,4},{1,2},{2,1},{3,7},{4,0},{5,6},{6,5},{7,3},{8,12},{9,10},{10,... | collective-permute-start | bytes 98312 | tf_op jit(solution)/shard_map/ppermute | solution.py:522
  (6 other events, 16.0 us)

commit v2 on v1

--- a/solution.py
+++ b/solution.py
@@ -23,7 +23,10 @@
 LANES = 128
 WORKSPACE = 8 * 2**20
 PEAK = 14.0
+QUICK = 0.02
 ROLES = 3
+CENTER, NEAR, FAR = range(ROLES)
+ORDER = (FAR, NEAR, CENTER)
 
 
 def iota(shape, axis):
@@ -47,10 +50,18 @@
     return one_hot(iota((count, count), 0) < iota((count, count), 1))
 
 
+def fetch(outside, held, sems):
+    copies = [pltpu.make_async_copy(a, b, sems.at[n]) for n, (a, b) in enumerate(zip(outside, held))]
+    for copy in copies:
+        copy.start()
+    return copies
+
+
 def route_kernel(cap, me_ref, slots_ref, stored_ref, out_ref, wide_ref):
     rows, slots = out_ref.shape[0], stored_ref.shape[0]
+    me = me_ref[0]
     wide_ref[...] = stored_ref[...].reshape(slots * BX, BY).astype(f32)
-    target = jnp.right_shift(slots_ref[pl.ds(me_ref[0], 1), :], slots.bit_length() - 1)
+    target = jnp.right_shift(slots_ref[pl.ds(me, 1), :], slots.bit_length() - 1)
     place = iota((rows, slots), 0) - target * cap
     marked = jnp.logical_and(place >= 0, place < cap)
     rank = dot(one_hot(marked), earlier(slots))
@@ -124,14 +135,11 @@
     return jnp.where(jnp.abs(off) <= RADIUS, table, 0.0)
 
 
-def build_forward_kernel(taps_ref, back_ref, *refs):
-    held, out, sems = refs[8:16], refs[:8], refs[16]
-    copies = [pltpu.make_async_copy(a, b, sems.at[n]) for n, (a, b) in enumerate(zip(held, out))]
+def build_forward_kernel(taps_ref, back_ref, *held):
     each, tiled = selectors(NZ, BX)
     each16, tiled16 = selectors(STRIP, BX)
-    for xr in range(ROLES):
-        k_ref, y_ref, xy_ref, z_ref = held[:4] if xr == 0 else held[4:]
-        n = max(xr - 1, 0)
+    for n, xr in enumerate(ORDER):
+        k_ref, y_ref, xy_ref, z_ref = held[4 * n : 4 * n + 4]
         for v in range(V):
             def fwd(yr, e):
                 r = row_of(xr, yr, v, e)
@@ -143,30 +151,22 @@
 
             outer = expand(toeplitz(fwd(0, 0), BX), each)
             inner = expand(toeplitz(fwd(0, 2), NZ), tiled)
-            kron_rows(k_ref.at[n, v], outer, inner, BX, NZ)
-            y_ref[n, :, v * BY : (v + 1) * BY] = stack3(banded_y(bwd(0, 1)))
+            kron_rows(k_ref.at[v], outer, inner, BX, NZ)
+            y_ref[:, v * BY : (v + 1) * BY] = stack3(banded_y(bwd(0, 1)))
             for yr in (1, 2):
                 outer = expand(toeplitz(bwd(yr, 0), BX), each16)
                 inner = expand(toeplitz(bwd(yr, 1), STRIP), tiled16)
-                kron_rows(xy_ref.at[n, yr - 1, v], outer, inner, BX, STRIP)
-                z_ref[n, yr - 1, v * NZ : (v + 1) * NZ, :] = lanes3(toeplitz(fwd(yr, 2), NZ), NZ)
-        if xr == 0:
-            for copy in copies[:4]:
-                copy.start()
-    for copy in copies[4:]:
-        copy.start()
-    for copy in copies:
-        copy.wait()
+                kron_rows(xy_ref.at[yr - 1, v], outer, inner, BX, STRIP)
+                z_ref[yr - 1, v * NZ : (v + 1) * NZ, :] = lanes3(toeplitz(fwd(yr, 2), NZ), NZ)
 
 
 def build_adjoint_kernel(taps_ref, back_ref, *refs):
-    held, out, sems = refs[8:16], refs[:8], refs[16]
+    out, held, sems = refs[:12], refs[12:24], refs[24]
     copies = [pltpu.make_async_copy(a, b, sems.at[n]) for n, (a, b) in enumerate(zip(held, out))]
     each, tiled = selectors(NZ, BX)
     each16, tiled16 = selectors(STRIP, BX)
-    for xr in range(ROLES):
-        k_ref, y_ref, xy_ref, z_ref = held[:4] if xr == 0 else held[4:]
-        n = max(xr - 1, 0)
+    for n, xr in enumerate(ORDER):
+        k_ref, y_ref, xy_ref, z_ref = held[4 * n : 4 * n + 4]
         for v in range(V):
             def fwd(yr, e):
                 r = row_of(xr, yr, v, e)
@@ -178,20 +178,21 @@
 
             outer = expand(toeplitz(bwd(0, 0), BX), each)
             inner = expand(toeplitz(bwd(0, 2), NZ), tiled) * (1.0 / V)
-            kron_rows(k_ref.at[n, v], outer, inner, BX, NZ)
-            y_ref[v, :, n * BY : (n + 1) * BY] = stack3(banded_y(fwd(0, 1)))
+            kron_rows(k_ref.at[v], outer, inner, BX, NZ)
+            hi, lo = split(banded_y(fwd(0, 1)))
+            y_ref[v, :BY, :BY] = hi
+            y_ref[v, :BY, BY:] = lo
+            y_ref[v, BY:, :BY] = hi
+            y_ref[v, BY:, BY:] = jnp.zeros_like(hi)
             for yr in (1, 2):
                 outer = expand(toeplitz(fwd(yr, 0), BX), each16)
                 inner = expand(toeplitz(fwd(yr, 1), STRIP), tiled16)
-                kron_rows(xy_ref.at[n, yr - 1, v], outer, inner, BX, STRIP)
-                z_ref[n, yr - 1, :, v * LANES : (v + 1) * LANES] = lanes3(
+                kron_rows(xy_ref.at[yr - 1, v], outer, inner, BX, STRIP)
+                z_ref[yr - 1, :, v * LANES : (v + 1) * LANES] = lanes3(
                     toeplitz(bwd(yr, 2), NZ) * (1.0 / V), NZ
                 )
-        if xr == 0:
-            for copy in copies[:4]:
-                copy.start()
-    for copy in copies[4:]:
-        copy.start()
+        for copy in copies[4 * n : 4 * n + 4]:
+            copy.start()
     for copy in copies:
         copy.wait()
 
@@ -267,27 +268,21 @@
             add(v, unpack_strip(tall(totals[v]), shifts[yr]))
 
 
-def brick(refs, n):
-    k, y, xy, z = refs
-    return k.at[n], y.at[n], xy.at[n], z.at[n]
-
-
-def adjoint_parts(count, quotient_ref, edge_ref, refs, ready=lambda v: None):
+def adjoint_parts(quotient_ref, edge_ref, refs, ready=lambda v: None):
     k_ref, y_ref, xy_ref, z_ref = refs
-    totals = [jnp.zeros((FIELD, LANES), f32) for _ in range(count)]
+    total = jnp.zeros((FIELD, LANES), f32)
     for v in range(V):
-        spread = three_lanes(quotient_ref[v], y_ref[v])
+        hi, lo = split(quotient_ref[v])
+        both = dot(jnp.concatenate([hi, lo], axis=1), y_ref[v])
+        spread = both[:, :BY] + both[:, BY:]
         ready(v)
-        for n in range(count):
-            totals[n] += two_lanes(k_ref[n, v], spread[:, n * BY : (n + 1) * BY])
+        total += two_lanes(k_ref[v], spread)
     ready(V)
-    strips = [[], []]
+    strips = []
     for yr in range(2):
-        packed = [wide(edge_ref[v, yr]) for v in range(V)]
-        for n in range(count):
-            parts = [column3(two_rows(packed[v], xy_ref[n, yr, v])) for v in range(V)]
-            strips[yr].append(tall(dot(z_ref[n, yr], jnp.concatenate(parts, axis=0))))
-    return totals, strips
+        parts = [column3(two_rows(wide(edge_ref[v, yr]), xy_ref[yr, v])) for v in range(V)]
+        strips.append(tall(dot(z_ref[yr], jnp.concatenate(parts, axis=0))))
+    return total, strips
 
 
 def write_message(ref, field, strips):
@@ -316,55 +311,56 @@
     return message[:FIELD], [message[FIELD : FIELD + 2 * NZ], message[FIELD + 2 * NZ :]]
 
 
-def start_kernel(info_ref, estimate_ref, field_ref, first_ref, second_ref):
+def start_kernel(info_ref, *refs):
+    outside, (field_ref, first_ref, second_ref), held, estimate_ref, sems = (
+        refs[:3], refs[3:6], refs[6:8], refs[8], refs[9],
+    )
+    copies = fetch(outside, (estimate_ref, *held), sems)
+    copies[0].wait()
     for x in range(BX):
         field_ref[x * NZ : (x + 1) * NZ, :] = estimate_ref[:, x, :]
     field = field_ref[...]
     first_ref[...] = pack_strip(field, info_ref[0])
     second_ref[...] = pack_strip(field, info_ref[1])
-
-
-def forward_first_kernel(info_ref, own_ref, first_ref, second_ref, *rest):
-    far, result_ref, held, out_ref, sems = rest[:8], rest[8], rest[9:17], rest[17], rest[18]
-    copies = [pltpu.make_async_copy(a, b, sems.at[n]) for n, (a, b) in enumerate(zip(far, held))]
-    for copy in copies:
-        copy.start()
+    for copy in copies[1:]:
+        copy.wait()
+
+
+def forward_first_kernel(last, info_ref, *refs):
+    before = len(refs) - (13 if last else 12)
+    message_ref, matrices, kept = refs[before], refs[before + 1 : before + 5], refs[before + 5 : before + 10]
+    result_ref, out_ref, sems = refs[before + 10 :] if last else (None, *refs[before + 10 :])
+    copies = fetch((*matrices, message_ref), kept, sems)
+    shifts = (info_ref[0], info_ref[1])
+    out_ref[...] = refs[0][...] if before else jnp.zeros_like(out_ref)
+
+    def add(v, part):
+        out_ref[v] += part
+
+    forward_parts([(*message_parts(message_ref[...]), matrices)], shifts, add)
+    if last:
+        for v in range(V):
+            out_ref[v] = 1.0 / out_ref[v]
+        copies.append(pltpu.make_async_copy(out_ref, result_ref, sems.at[len(copies)]))
+        copies[-1].start()
     for copy in copies:
         copy.wait()
-    center, sides = held[:4], held[4:]
-    shifts = (info_ref[0], info_ref[1])
-    out_ref[...] = jnp.zeros_like(out_ref)
-
-    def add(v, part):
-        out_ref[v] += part
-
-    bricks = (brick(center, 0), brick(sides, 0), brick(sides, 1))
-    messages = (own_ref[...], first_ref[...], second_ref[...])
-    sources = [(*message_parts(m), matrices) for m, matrices in zip(messages, bricks)]
-    forward_parts(sources, shifts, add)
-    for v in range(V):
-        out_ref[v] = 1.0 / out_ref[v]
-    copy = pltpu.make_async_copy(out_ref, result_ref, sems.at[len(copies)])
-    copy.start()
-    copy.wait()
-
-
-def adjoint_sides(quotient_ref, edge_ref, shifts, refs, first_ref, second_ref, ready=lambda v: None):
+
+
+def adjoint_far(quotient_ref, edge_ref, shifts, refs, far_ref, ready=lambda v: None):
     for v in range(V):
         for yr in range(2):
             edge_ref[v, yr] = pack_strip(quotient_ref[v], shifts[yr])
-    totals, strips = adjoint_parts(2, quotient_ref, edge_ref, refs, ready)
-    write_message(first_ref, totals[0], [strips[0][0], strips[1][0]])
-    write_scaled(second_ref, totals[1], [strips[0][1], strips[1][1]])
+    write_scaled(far_ref, *adjoint_parts(quotient_ref, edge_ref, refs, ready))
 
 
 def quotient_first_kernel(info_ref, *refs):
-    far, (data_ref, quotient_ref, edge_ref, first_ref, second_ref), held, sems = (
-        refs[:7], refs[7:12], refs[12:19], refs[19],
-    )
-    pairs = list(zip(far[:4], held[:4]))
-    pairs += [(far[6].at[:, v], held[6].at[:, v]) for v in range(V)]
-    pairs += list(zip(far[4:6], held[4:6]))
+    outside, (data_ref, quotient_ref, edge_ref, far_ref), held, sems = (
+        refs[:7], refs[7:11], refs[11:18], refs[18],
+    )
+    pairs = list(zip(outside[:4], held[:4]))
+    pairs += [(outside[6].at[v], held[6].at[v]) for v in range(V)]
+    pairs += list(zip(outside[4:6], held[4:6]))
     copies = [pltpu.make_async_copy(a, b, sems.at[n]) for n, (a, b) in enumerate(pairs)]
     for copy in copies:
         copy.start()
@@ -386,34 +382,36 @@
         for copy in copies[4 + v : 5 + v] if v < V else copies[4 + V :]:
             copy.wait()
 
-    adjoint_sides(
-        quotient_ref, edge_ref, shifts, (k_ref, y_ref, xy_ref, z_ref), first_ref, second_ref, ready
-    )
+    adjoint_far(quotient_ref, edge_ref, shifts, (k_ref, y_ref, xy_ref, z_ref), far_ref, ready)
+
+
+def adjoint_near_kernel(quotient_ref, edge_ref, k_ref, y_ref, xy_ref, z_ref, near_ref):
+    write_scaled(near_ref, *adjoint_parts(quotient_ref, edge_ref, (k_ref, y_ref, xy_ref, z_ref)))
 
 
 def adjoint_center_kernel(quotient_ref, edge_ref, k_ref, y_ref, xy_ref, z_ref, field_ref, strips_ref):
-    totals, strips = adjoint_parts(1, quotient_ref, edge_ref, (k_ref, y_ref, xy_ref, z_ref))
-    field_ref[...] = totals[0]
-    strips_ref[0] = strips[0][0]
-    strips_ref[1] = strips[1][0]
-
-
-def gather_kernel(info_ref, field_ref, strips_ref, first_ref, second_ref, total_ref, up_ref, down_ref):
-    second = read_scaled(second_ref)
-    total = field_ref[...] + first_ref[:FIELD] + second[:FIELD]
+    field, strips = adjoint_parts(quotient_ref, edge_ref, (k_ref, y_ref, xy_ref, z_ref))
+    field_ref[...] = field
+    strips_ref[0] = strips[0]
+    strips_ref[1] = strips[1]
+
+
+def gather_kernel(info_ref, field_ref, strips_ref, near_ref, far_ref, total_ref, up_ref, down_ref):
+    near, far = read_scaled(near_ref), read_scaled(far_ref)
+    total = field_ref[...] + near[:FIELD] + far[:FIELD]
     total_ref[...] = total
     for n, ref in enumerate((up_ref, down_ref)):
         rows = slice(FIELD + n * 2 * NZ, FIELD + (n + 1) * 2 * NZ)
-        ref[: 2 * NZ] = strips_ref[n] + first_ref[rows] + second[rows]
+        ref[: 2 * NZ] = strips_ref[n] + near[rows] + far[rows]
         ref[2 * NZ :] = pack_strip(total, info_ref[n])
 
 
-def gather_last_kernel(field_ref, strips_ref, first_ref, second_ref, total_ref, up_ref, down_ref):
-    second = read_scaled(second_ref)
-    total_ref[...] = field_ref[...] + first_ref[:FIELD] + second[:FIELD]
+def gather_last_kernel(field_ref, strips_ref, near_ref, far_ref, total_ref, up_ref, down_ref):
+    near, far = read_scaled(near_ref), read_scaled(far_ref)
+    total_ref[...] = field_ref[...] + near[:FIELD] + far[:FIELD]
     for n, ref in enumerate((up_ref, down_ref)):
         rows = slice(FIELD + n * 2 * NZ, FIELD + (n + 1) * 2 * NZ)
-        ref[...] = strips_ref[n] + first_ref[rows] + second[rows]
+        ref[...] = strips_ref[n] + near[rows] + far[rows]
 
 
 def update_kernel(
@@ -439,13 +437,22 @@
     def add(v, part):
         out_ref[v] += part
 
-    forward_parts([(*message_parts(own_ref[...]), brick((k_ref, y_ref, xy_ref, z_ref), 0))], shifts, add)
+    forward_parts([(*message_parts(own_ref[...]), (k_ref, y_ref, xy_ref, z_ref))], shifts, add)
+
+
+def forward_near_kernel(info_ref, blurred_ref, near_ref, k_ref, y_ref, xy_ref, z_ref, out_ref):
+    shifts = (info_ref[0], info_ref[1])
+    out_ref[...] = blurred_ref[...]
+
+    def add(v, part):
+        out_ref[v] += part
+
+    forward_parts([(*message_parts(read_scaled(near_ref)), (k_ref, y_ref, xy_ref, z_ref))], shifts, add)
 
 
 def middle_kernel(
-    info_ref, data_ref, blurred_ref, from_first_ref, from_second_ref,
-    k_ref, y_ref, xy_ref, z_ref, ka_ref, ya_ref, xya_ref, za_ref,
-    quotient_ref, edge_ref, first_ref, second_ref,
+    info_ref, data_ref, blurred_ref, from_far_ref, k_ref, y_ref, xy_ref, z_ref,
+    ka_ref, ya_ref, xya_ref, za_ref, quotient_ref, edge_ref, far_ref,
 ):
     shifts = (info_ref[0], info_ref[1])
     quotient_ref[...] = blurred_ref[...]
@@ -453,15 +460,11 @@
     def add(v, part):
         quotient_ref[v] += part
 
-    refs = (k_ref, y_ref, xy_ref, z_ref)
-    sources = [
-        (*message_parts(from_first_ref[...]), brick(refs, 0)),
-        (*message_parts(read_scaled(from_second_ref)), brick(refs, 1)),
-    ]
+    sources = [(*message_parts(read_scaled(from_far_ref)), (k_ref, y_ref, xy_ref, z_ref))]
     forward_parts(sources, shifts, add)
     for v in range(V):
         quotient_ref[v] = data_ref[v].astype(f32) / quotient_ref[v]
-    adjoint_sides(quotient_ref, edge_ref, shifts, (ka_ref, ya_ref, xya_ref, za_ref), first_ref, second_ref)
+    adjoint_far(quotient_ref, edge_ref, shifts, (ka_ref, ya_ref, xya_ref, za_ref), far_ref)
 
 
 def final_kernel(info_ref, old_ref, total_ref, up_in_ref, down_in_ref, out_ref):
@@ -476,19 +479,22 @@
 SMEM, VMEM, HBM = pltpu.SMEM, pltpu.VMEM, pltpu.HBM
 
 
-def call(kernel, outs, *args, scalars=0, far=(), out_place=VMEM, scratch=(), cost=1.0):
+def call(kernel, outs, *args, scalars=0, far=(), out_place=VMEM, scratch=(), cost=QUICK):
     arrays = [(a.size, a.dtype) for a in (*args[scalars:], *far)]
     arrays += [(math.prod(s), d) for s, d in outs]
     need = sum(count * jnp.dtype(d).itemsize for count, d in arrays)
+    places = out_place if isinstance(out_place, list) else [out_place] * len(outs)
     specs = [pl.BlockSpec(memory_space=SMEM)] * scalars
     specs += [pl.BlockSpec(memory_space=VMEM)] * (len(args) - scalars)
     specs += [pl.BlockSpec(memory_space=HBM)] * len(far)
     args += tuple(pltpu.with_memory_space_constraint(a, HBM) for a in far)
     return pl.pallas_call(
         kernel,
-        out_shape=[HBM(s, d) if out_place is HBM else jax.ShapeDtypeStruct(s, d) for s, d in outs],
+        out_shape=[
+            HBM(s, d) if where is HBM else jax.ShapeDtypeStruct(s, d) for (s, d), where in zip(outs, places)
+        ],
         in_specs=specs,
-        out_specs=[pl.BlockSpec(memory_space=out_place)] * len(outs),
+        out_specs=[pl.BlockSpec(memory_space=where) for where in places],
         scratch_shapes=list(scratch),
         compiler_params=pltpu.CompilerParams(vmem_limit_bytes=need + WORKSPACE),
         cost_estimate=pl.CostEstimate(flops=0, bytes_accessed=int(cost * 3.5e6), transcendentals=0),
@@ -517,16 +523,21 @@
     return near, far
 
 
+def swap_near(axis, value):
+    return lax.ppermute(narrow(axis, value), ("gx", "gy"), partner_swaps(axis)[0])
+
+
+def swap_far(axis, value):
+    return lax.ppermute(narrow(axis, value), ("gx", "gy"), partner_swaps(axis)[1])
+
+
+def narrow(axis, value):
+    return value.astype(jnp.float16) if axis == "gx" else value
+
+
 def swap(axis, near_value, far_value):
-    near, far = partner_swaps(axis)
-    far_in = lax.ppermute(far_value, ("gx", "gy"), far)
-    near_in = lax.ppermute(near_value, ("gx", "gy"), near)
-    return near_in, far_in
-
-
-def swap_x(near_value, far_value):
-    near_in, far_in = swap("gx", near_value, far_value.astype(jnp.float16))
-    return near_in, far_in.astype(f32)
+    far_in = swap_far(axis, far_value)
+    return swap_near(axis, near_value), far_in
 
 
 def tap_tables(psf_taps, kernel_index):
@@ -579,13 +590,16 @@
     one, every = (FIELD, LANES), (V, FIELD, LANES)
     even_y = lax.axis_index("gy") % 2 == 0
     info = jnp.stack([jnp.where(even_y, STRIP, 0), jnp.where(even_y, 0, STRIP)]).astype(i32)
-    field, up, down = call(start_kernel, [(one, f32), (half, f32), (half, f32)], info, estimate, scalars=1)
+    slots_of = placement.reshape(devices, slots)
+    field, up, down, slots_near, stored_near = call(
+        start_kernel,
+        [(one, f32), (half, f32), (half, f32), (slots_of.shape, i32), (stored.shape, bf16)],
+        info, scalars=1, far=(estimate, slots_of, stored),
+        scratch=[pltpu.VMEM(estimate.shape, f32), pltpu.SemaphoreType.DMA((3,))],
+    )
     up_in, down_in = swap("gy", up, down)
-    slots_of = placement.reshape(devices, slots)
     (outgoing,) = call(
-        functools.partial(route_kernel, cap),
-        [((rows, plane), bf16)],
-        me.reshape(1), slots_of, stored,
+        functools.partial(route_kernel, cap), [((rows, plane), bf16)], me.reshape(1), slots_near, stored_near,
         scalars=1, scratch=[pltpu.VMEM((slots * BX, BY), f32)],
     )
     outgoing, up_in, down_in, psf_taps, kernel_index, slots_of = lax.optimization_barrier(
@@ -596,77 +610,82 @@
     ).reshape(rows, plane)
 
     old = jnp.concatenate([field, up_in, down_in], axis=0)
-    narrow = old.astype(jnp.float16)
-    first, second = (a.astype(f32) for a in swap("gx", narrow, narrow))
+    near, far = (a.astype(f32) for a in swap("gx", old, old))
     taps, backward = tap_tables(psf_taps, kernel_index)
 
-    def shapes(y_of, z_shape):
-        return [
-            shape
-            for count in (1, ROLES - 1)
-            for shape in (
-                ((count, V, FIELD, FIELD), bf16),
-                (y_of(count), bf16),
-                ((count, 2, V, 2 * LANES, 2 * LANES), bf16),
-                ((count, 2) + z_shape, bf16),
-            )
+    def shapes(y_shape, z_shape):
+        return ROLES * [
+            ((V, FIELD, FIELD), bf16),
+            (y_shape, bf16),
+            ((2, V, 2 * LANES, 2 * LANES), bf16),
+            ((2,) + z_shape, bf16),
         ]
 
-    forward_shapes = shapes(lambda n: (n, 3 * BY, V * BY), (V * NZ, LANES))
-    adjoint_shapes = shapes(lambda n: (V, 3 * BY, n * BY), (NZ, V * LANES))
-    sems = [pltpu.SemaphoreType.DMA((8,))]
-    forward = call(
-        build_forward_kernel, forward_shapes, taps, backward,
-        out_place=HBM, scratch=held(forward_shapes) + sems, cost=3.0,
-    )
+    forward_shapes = shapes((3 * BY, V * BY), (V * NZ, LANES))
+    adjoint_shapes = shapes((V, 2 * BY, 2 * BY), (NZ, V * LANES))
+    sems = [pltpu.SemaphoreType.DMA((4 * ROLES,))]
+    forward = call(build_forward_kernel, forward_shapes, taps, backward, cost=3.0)
     adjoint = call(
         build_adjoint_kernel, adjoint_shapes, taps, backward,
-        out_place=HBM, scratch=held(adjoint_shapes) + sems, cost=3.0,
-    )
-    forward_center, forward_sides = forward[:4], forward[4:]
-    adjoint_center, adjoint_sides = adjoint[:4], adjoint[4:]
-    (inverse,) = call(
-        forward_first_kernel, [(every, f32)], info, old, first, second,
-        scalars=1, far=forward, out_place=HBM,
-        scratch=held(forward_shapes) + [pltpu.VMEM(every, f32), pltpu.SemaphoreType.DMA((9,))], cost=5.0,
-    )
-    repeated = jnp.repeat(slots_of, cap, axis=0)
+        out_place=HBM, scratch=held(adjoint_shapes) + sems, cost=4.0,
+    )
+    forward_far, forward_near, forward_center = forward[:4], forward[4:8], forward[8:]
+
+    def first_part(total, source, matrices, last=False):
+        return call(
+            functools.partial(forward_first_kernel, last), forward_shapes[:4] + [(message, f32), (every, f32)],
+            info, *total, source, *matrices, scalars=1, out_place=[HBM] * 5 + [HBM if last else VMEM],
+            scratch=[pltpu.VMEM(every, f32)] * last + [pltpu.SemaphoreType.DMA((6,))],
+        )
+
+    *forward_center, old, total = first_part((), old, forward_center)
+    *forward_near, _, total = first_part((total,), near, forward_near)
+    *forward_far, _, inverse = first_part((total,), far, forward_far, last=True)
+    adjoint_of_far, adjoint_near, adjoint_center = adjoint[:4], adjoint[4:8], adjoint[8:]
     (table,) = call(
-        functools.partial(arrival_kernel, cap), [((slots, rows), bf16)], me.reshape(1), repeated, scalars=1,
+        functools.partial(arrival_kernel, cap), [((slots, rows), bf16)],
+        me.reshape(1), jnp.repeat(slots_of, cap, axis=0), scalars=1,
         out_place=HBM, scratch=[pltpu.VMEM((slots, rows), bf16), pltpu.SemaphoreType.DMA],
     )
 
     edges = ((V, 2) + half, f32)
-    k, y, xy, z = adjoint_sides
+    k, y, xy, z = adjoint_of_far
     fetched = (table, arrived, inverse, y, xy, z, k)
-    outs = [(every, bf16), (every, f32), edges, (message, f32), (scaled, f32)]
-    data, quotient, edge, first, second = call(
-        quotient_first_kernel, outs, info, scalars=1, far=fetched,
+    data, quotient, edge, far = call(
+        quotient_first_kernel, [(every, bf16), (every, f32), edges, (scaled, f32)],
+        info, scalars=1, far=fetched, cost=QUICK,
         scratch=held([(a.shape, a.dtype) for a in fetched]) + [pltpu.SemaphoreType.DMA((len(fetched) + V - 1,))],
     )
-    first, second = swap_x(first, second)
-    center = [(one, f32), ((2,) + half, f32)]
-    field, strips = call(adjoint_center_kernel, center, quotient, edge, *adjoint_center)
+
+    def sides(quotient, edge, far):
+        far = swap_far("gx", far)
+        (near,) = call(adjoint_near_kernel, [(scaled, f32)], quotient, edge, *adjoint_near)
+        near = swap_near("gx", near)
+        center = [(one, f32), ((2,) + half, f32)]
+        field, strips = call(adjoint_center_kernel, center, quotient, edge, *adjoint_center, cost=QUICK)
+        return field, strips, near.astype(f32), far.astype(f32)
+
     both = (4 * NZ, LANES)
     total, up, down = call(
-        gather_kernel, [(one, f32), (both, f32), (both, f32)],
-        info, field, strips, first, second, scalars=1,
+        gather_kernel, [(one, f32), (both, f32), (both, f32)], info, *sides(quotient, edge, far), scalars=1
     )
     up_in, down_in = swap("gy", up, down)
     new, new_scaled = call(
         update_kernel, [(message, f32), (scaled, f32)],
         info, old, total, up, down, up_in, down_in, scalars=1,
     )
-    first, second = swap_x(new, new_scaled)
-    (blurred,) = call(forward_center_kernel, [(every, f32)], info, new, *forward_center, scalars=1)
-    quotient, edge, first, second = call(
-        middle_kernel, [(every, f32), edges, (message, f32), (scaled, f32)],
-        info, data, blurred, first, second, *forward_sides, *adjoint_sides, scalars=1,
-    )
-    first, second = swap_x(first, second)
-    field, strips = call(adjoint_center_kernel, center, quotient, edge, *adjoint_center)
+    far = swap_far("gx", new_scaled)
+    near = swap_near("gx", new_scaled)
+    (blurred,) = call(forward_center_kernel, [(every, f32)], info, new, *forward_center, scalars=1, cost=QUICK)
+    (blurred,) = call(
+        forward_near_kernel, [(every, f32)], info, blurred, near.astype(f32), *forward_near, scalars=1, cost=QUICK
+    )
+    quotient, edge, far = call(
+        middle_kernel, [(every, f32), edges, (scaled, f32)],
+        info, data, blurred, far.astype(f32), *forward_far, *adjoint_of_far, scalars=1, cost=QUICK,
+    )
     total, up, down = call(
-        gather_last_kernel, [(one, f32), (half, f32), (half, f32)], field, strips, first, second
+        gather_last_kernel, [(one, f32), (half, f32), (half, f32)], *sides(quotient, edge, far)
     )
     up_in, down_in = swap("gy", up, down)
     (refined,) = call(final_kernel, [(estimate.shape, f32)], info, new, total, up_in, down_in, scalars=1)

time: 90.4 us -> 82.2 us (0.909); the launches traced: 89 us -> 82 us
  starting transfers between devices: 23.9 us -> 19.3 us
  local copies, waits for them, and re-layouts: 4.69 us -> 2.4 us
    ppermute x14, starting transfers between devices: 18.5 us -> 12.4 us  [the longest x7 6.75 us: swap_far(): lax.ppermute(narrow(axis, value), ('gx', 'gy'), partner_swaps(axis)[1])]
    unnamed x48 -> x60, local copies, waits for them, and re-layouts: 3.77 us -> 1.48 us
    all_to_all x1, starting transfers between devices: 5.41 us -> 6.85 us  [shards(): lax.all_to_all(outgoing.reshape(devices, cap, plane), ('gx', 'gy'), split...]
    pallas_call x15 -> x20, Pallas kernels: 49.8 us -> 50 us  [call(): pl.pallas_call(kernel, out_shape=[HBM(s, d) if where is HBM else jax.Shap...]
  transfers between devices with their start and end apart: 15 -> 15, of which waited for: 6 -> 4; matrix products, arithmetic and copies ran while one was open for 2% -> 2% of each run, Pallas kernels for 36% -> 43%
where the time goes in v2:
time: 82.2 us; the launch traced here: 82 us
  Pallas kernels  50 us (61%)
  starting transfers between devices  19.3 us (23%)
  waiting for transfers between devices  8.52 us (10%)
  local copies, waits for them, and re-layouts  2.4 us (3%)
    pallas_call x20, Pallas kernels, call(): pl.pallas_call(kernel, out_shape=[HBM(s, d) if where is HBM else jax.Shap...  50 us
    all_to_all x1, starting transfers between devices, shards(): lax.all_to_all(outgoing.reshape(devices, cap, plane), ('gx', 'gy'), split...  6.85 us
    ppermute x7, starting transfers between devices, swap_far(): lax.ppermute(narrow(axis, value), ('gx', 'gy'), partner_swaps(axis)[1])  6.75 us
    ppermute x7, waiting for transfers between devices, swap_near(): lax.ppermute(narrow(axis, value), ('gx', 'gy'), partner_swaps(axis)[0])  6.65 us
    ppermute x7, starting transfers between devices, swap_near(): lax.ppermute(narrow(axis, value), ('gx', 'gy'), partner_swaps(axis)[0])  5.65 us
    ppermute x7, waiting for transfers between devices, swap_far(): lax.ppermute(narrow(axis, value), ('gx', 'gy'), partner_swaps(axis)[1])  1.87 us
  transfers between devices with their start and end apart: 15, of which 4 were waited for; matrix products, arithmetic and copies ran while one was open for 2% of the time, Pallas kernels for 43%

profile of v2, /device:TPU:0, one launch (start us, length us, event | category | flops | bytes accessed | tf_op | source)
XLA Modules:
  0.0 82.0 jit_solution(3573723301639823686)
XLA Ops:
  0.1 1.8 %shard_map.55 = (f32[512,128]{1,0:T(8,128)S(1)}, f32[64,128]{1,0:T(8,128)S(1)}, f32[64,128]{1,0:T(8,128)S(1)}, s32[32,128]{1,0:T(8,128)S(1)}, bf16[128,16,128]{2,1,0:T(8,128)(2,1)S(1)}) custom-call(s32[2]{0:T(128)S(1)} %pad_add_fusion.info_ref, f32[32,16,128]{2,1,0:T(8,128)} %refs_0_.1, s32[32,128]{1,0:T(8,128)} %bitcast.9, bf16[128,16,128]{2,1,0:T(8,128)(2,1)} %refs_2_.1), custom_call_target="tpu_custom_call" | custom-call | bytes 70000 | tf_op jit(solution)/shard_map/pallas_call | solution.py:491
  1.9 3.1 %collective-permute-start = (f32[64,128]{1,0:T(8,128)S(1)}, f32[64,128]{1,0:T(8,128)S(1)}, u32[]{:S(2)}, u32[]{:S(2)}) collective-permute-start(f32[64,128]{1,0:T(8,128)S(1)} %get-tuple-element.78), channel_id=1, source_target_pairs={{0,1},{1,0},{2,3},{3,2},{4,5},{5,4},{6,7},{7,6},{8,9},{9,8},{10,11... | collective-permute-start | bytes 98312 | tf_op jit(solution)/shard_map/ppermute | solution.py:527
  5.1 1.6 %shard_map.56 = bf16[256,2048]{1,0:T(8,128)(2,1)} custom-call(s32[1]{0:T(128)} %bitcast.3.me_ref, s32[32,128]{1,0:T(8,128)S(1)} %get-tuple-element.76.slots_ref, bf16[128,16,128]{2,1,0:T(8,128)(2,1)S(1)} %get-tuple-element.77.stored_ref), custom_call_target="tpu_custom_call" | custom-call | bytes 70000 | tf_op jit(solution)/shard_map/pallas_call | solution.py:491
  6.9 6.9 %all-to-all-start = ((bf16[32,8,2048]{2,1,0:T(8,128)(2,1)}), bf16[32,8,2048]{2,1,0:T(8,128)(2,1)S(1)}, u32[]{:S(2)}, u32[]{:S(2)}) async-start(bf16[32,8,2048]{2,1,0:T(8,128)(2,1)} %bitcast.5), calls=%async_computation | async-start | bytes 2097152 | tf_op jit(solution)/shard_map/all_to_all | solution.py:608
  13.8 1.8 %collective-permute-start.3 = (f16[640,128]{1,0:T(8,128)(2,1)S(1)}, f16[640,128]{1,0:T(8,128)(2,1)S(1)}, u32[]{:S(2)}, u32[]{:S(2)}) collective-permute-start(f16[640,128]{1,0:T(8,128)(2,1)S(1)} %convert_element_type.48), channel_id=1, source_target_pairs={{0,1},{1,0},{2,3},{3,2},{4,8},{5,9},{6,10},{7,11},{8,4},{9,5},{10,... | collective-permute-start | bytes 491528 | tf_op jit(solution)/shard_map/ppermute | solution.py:531
  16.4 0.2 fusion
  17.3 2.5 %shard_map.57 = (bf16[4,512,512]{2,1,0:T(8,128)(2,1)S(1)}, bf16[384,512]{1,0:T(8,128)(2,1)S(1)}, bf16[2,4,256,256]{3,2,1,0:T(8,128)(2,1)S(1)}, bf16[2,128,128]{2...) custom-call(f32[108,128]{1,0:T(8,128)S(1)} %get-tuple-element.162.ta, ...), custom_call_target="tpu_custom_call" | custom-call | bytes 10500000 | tf_op jit(solution)/shard_map/pallas_call | solution.py:491
  19.8 7.1 %shard_map.62 = (bf16[4,512,512]{2,1,0:T(8,128)(2,1)}, bf16[4,256,256]{2,1,0:T(8,128)(2,1)}, bf16[2,4,256,256]{3,2,1,0:T(8,128)(2,1)}, bf16[2,32,512]{2,1,0:T(8,...) custom-call(f32[108,128]{1,0:T(8,128)S(1)} %get-tuple-element.162.ta, ...), custom_call_target="tpu_custom_call" | custom-call | bytes 14000000 | tf_op jit(solution)/shard_map/pallas_call | solution.py:491
  26.9 1.0 %shard_map.59.refs_0_ = bf16[128,256]{1,0:T(8,128)(2,1)} custom-call(s32[1]{0:T(128)} %bitcast.3.me_ref, s32[256,128]{1,0:T(8,128)S(1)} %broadcast_bitcast_fusion.slots_ref), custom_call_target="tpu_custom_call" | custom-call | bytes 70000 | tf_op jit(solution)/shard_map/pallas_call | solution.py:491
  27.9 3.6 %shard_map.58 = (bf16[4,512,512]{2,1,0:T(8,128)(2,1)}, bf16[384,512]{1,0:T(8,128)(2,1)}, bf16[2,4,256,256]{3,2,1,0:T(8,128)(2,1)}, bf16[2,128,128]{2,1,0:T(8,128...) custom-call(s32[2]{0:T(128)S(1)} %pad_add_fusion.info_ref, ...), custom_call_target="tpu_custom_call" | custom-call | bytes 70000 | tf_op jit(solution)/shard_map/pallas_call | solution.py:491
  31.5 3.6 %shard_map.60 = (bf16[4,512,512]{2,1,0:T(8,128)(2,1)}, bf16[384,512]{1,0:T(8,128)(2,1)}, bf16[2,4,256,256]{3,2,1,0:T(8,128)(2,1)}, bf16[2,128,128]{2,1,0:T(8,128...) custom-call(s32[2]{0:T(128)S(1)} %pad_add_fusion.info_ref, f32[4,512,128]{2,1,0:T(8,128)S(1)} %get-tuple-element.91.refs_0_, ...), custom_call_target="tpu_custom_call" | custom-call | bytes 70000 | tf_op jit(solution)/shard_map/pallas_call | solution.py:491
  35.2 4.4 %shard_map.61 = (bf16[4,512,512]{2,1,0:T(8,128)(2,1)}, bf16[384,512]{1,0:T(8,128)(2,1)}, bf16[2,4,256,256]{3,2,1,0:T(8,128)(2,1)}, bf16[2,128,128]{2,1,0:T(8,128...) custom-call(s32[2]{0:T(128)S(1)} %pad_add_fusion.info_ref, f32[4,512,128]{2,1,0:T(8,128)S(1)} %get-tuple-element.96.refs_0_, ...), custom_call_target="tpu_custom_call" | custom-call | bytes 70000 | tf_op jit(solution)/shard_map/pallas_call | solution.py:491
  39.6 1.0 %copy-done.25 = bf16[32,8,2048]{2,1,0:T(8,128)(2,1)} copy-done((bf16[32,8,2048]{2,1,0:T(8,128)(2,1)}, bf16[32,8,2048]{2,1,0:T(8,128)(2,1)S(1)}, u32[]{:S(2)}) %copy-start.25) | copy-done | bytes 1048600
  40.5 5.9 %shard_map.63 = (bf16[4,512,128]{2,1,0:T(8,128)(2,1)S(1)}, f32[4,512,128]{2,1,0:T(8,128)S(1)}, f32[4,2,64,128]{3,2,1,0:T(8,128)S(1)}, f32[656,128]{1,0:T(8,128)S(1)}) custom-call(s32[2]{0:T(128)S(1)} %pad_add_fusion.info_ref, bf16[128,256]{1,0:T(8,128)(2,1)} %shard_map.59.refs_0_, bf16[256,2048]{1,0:T(8,128)(2,1)} %bitcast.8, ...), custom_call_target="tpu_custom_call" | custom-call | bytes 70000 | tf_op jit(solution)/shard_map/pallas_call | solution.py:491
  46.5 2.4 %collective-permute-start.5 = (f16[656,128]{1,0:T(8,128)(2,1)S(1)}, f16[656,128]{1,0:T(8,128)(2,1)S(1)}, u32[]{:S(2)}, u32[]{:S(2)}) collective-permute-start(f16[656,128]{1,0:T(8,128)(2,1)S(1)} %convert_element_type.53), channel_id=1, source_target_pairs={{0,1},{1,0},{2,3},{3,2},{4,8},{5,9},{6,10},{7,11},{8,4},{9,5},{10,... | collective-permute-start | bytes 503816 | tf_op jit(solution)/shard_map/ppermute | solution.py:531
  49.0 1.7 %shard_map.65 = f32[656,128]{1,0:T(8,128)S(1)} custom-call(f32[4,512,128]{2,1,0:T(8,128)S(1)} %get-tuple-element.106.quotient_ref, f32[4,2,64,128]{3,2,1,0:T(8,128)S(1)} %get-tuple-element.107.edge_ref, bf16[4,512,512]{2,1,0:T(8,128)(2,1)S(1)} %copy-done.1, bf16[4,256,256]{2,1,0:T(8,128)(2,1)S(1)} %copy-done.10, bf16[2,4,256,256]{3,2,1,0:T(8,128)(2,1)S(1)} %copy-done.4, ...), custom_call_target="tpu_custom_call" | custom-call | bytes 70000 | tf_op jit(solution)/shard_map/pallas_call | solution.py:491
  50.9 1.6 %shard_map.64 = (f32[512,128]{1,0:T(8,128)S(1)}, f32[2,64,128]{2,1,0:T(8,128)S(1)}) custom-call(f32[4,512,128]{2,1,0:T(8,128)S(1)} %get-tuple-element.106.quotient_ref, f32[4,2,64,128]{3,2,1,0:T(8,128)S(1)} %get-tuple-element.107.edge_ref, bf16[4,512,512]{2,1,0:T(8,128)(2,1)S(1)} %copy-done, bf16[4,256,256]{2,1,0:T(8,128)(2,1)S(1)} %copy-done.6, ...), custom_call_target="tpu_custom_call" | custom-call | bytes 70000 | tf_op jit(solution)/shard_map/pallas_call | solution.py:491
  52.7 0.8 shard_map.66
  53.5 1.8 %collective-permute-start.6 = (f32[128,128]{1,0:T(8,128)S(1)}, f32[128,128]{1,0:T(8,128)S(1)}, u32[]{:S(2)}, u32[]{:S(2)}) collective-permute-start(f32[128,128]{1,0:T(8,128)S(1)} %get-tuple-element.120.up_ref), channel_id=1, source_target_pairs={{0,1},{1,0},{2,3},{3,2},{4,5},{5,4},{6,7},{7,6},{8,9},{9,8},{10,11... | collective-permute-start | bytes 196616 | tf_op jit(solution)/shard_map/ppermute | solution.py:527
  55.2 3.0 %collective-permute-done.6.up_in_ref = f32[128,128]{1,0:T(8,128)S(1)} collective-permute-done((f32[128,128]{1,0:T(8,128)S(1)}, f32[128,128]{1,0:T(8,128)S(1)}, u32[]{:S(2)}, u32[]{:S(2)}) %collective-permute-start.6) | collective-permute-done | bytes 65568 | tf_op jit(solution)/shard_map/ppermute | solution.py:527
  58.2 0.9 %shard_map.67 = (f32[640,128]{1,0:T(8,128)S(1)}, f32[656,128]{1,0:T(8,128)S(1)}) custom-call(s32[2]{0:T(128)S(1)} %pad_add_fusion.info_ref, f32[640,128]{1,0:T(8,128)S(1)} %copy-done.18, f32[512,128]{1,0:T(8,128)S(1)} %get-tuple-element.119.total_ref, f32[128,128]{1,0:T(8,128)S(1)} %get-tuple-element.120.up_ref, f32[128,128]{1,0:T(8,128)S(1)} %get-tuple-element.121.down_ref, ...), custom_call_target="tpu_custom_call" | custom-call | bytes 70000 | tf_op jit(solution)/shard_map/pallas_call | solution.py:491
  59.3 2.3 %collective-permute-start.9 = (f16[656,128]{1,0:T(8,128)(2,1)S(1)}, f16[656,128]{1,0:T(8,128)(2,1)S(1)}, u32[]{:S(2)}, u32[]{:S(2)}) collective-permute-start(f16[656,128]{1,0:T(8,128)(2,1)S(1)} %convert_element_type.55), channel_id=1, source_target_pairs={{0,1},{1,0},{2,3},{3,2},{4,8},{5,9},{6,10},{7,11},{8,4},{9,5},{10,... | collective-permute-start | bytes 503816 | tf_op jit(solution)/shard_map/ppermute | solution.py:531
  61.6 2.4 %shard_map.68.blurred_ref = f32[4,512,128]{2,1,0:T(8,128)S(1)} custom-call(s32[2]{0:T(128)S(1)} %pad_add_fusion.info_ref, f32[640,128]{1,0:T(8,128)S(1)} %get-tuple-element.122.own_ref.old_ref, bf16[4,512,512]{2,1,0:T(8,128)(2,1)S(1)} %copy-done.7, bf16[384,512]{1,0:T(8,128)(2,1)S(1)} %copy-done.16, bf16[2,4,256,256]{3,2,1,0:T(8,128)(2,1)S(1)} %copy-done.12, ...), custom_call_target="tpu_custom_call" | custom-call | bytes 70000 | tf_op jit(solution)/shard_map/pallas_call | solution.py:491
  64.2 2.4 %shard_map.69.blurred_ref = f32[4,512,128]{2,1,0:T(8,128)S(1)} custom-call(s32[2]{0:T(128)S(1)} %pad_add_fusion.info_ref, f32[4,512,128]{2,1,0:T(8,128)S(1)} %shard_map.68.blurred_ref, f32[656,128]{1,0:T(8,128)S(1)} %convert_element_type.56.near_ref, bf16[4,512,512]{2,1,0:T(8,128)(2,1)S(1)} %copy-done.8, bf16[384,512]{1,0:T(8,128)(2,1)S(1)} %copy-done.17, ...), custom_call_target="tpu_custom_call" | custom-call | bytes 70000 | tf_op jit(solution)/shard_map/pallas_call | solution.py:491
  66.7 0.3 copy-done.9
  67.0 3.8 %shard_map.70 = (f32[4,512,128]{2,1,0:T(8,128)S(1)}, f32[4,2,64,128]{3,2,1,0:T(8,128)S(1)}, f32[656,128]{1,0:T(8,128)S(1)}) custom-call(s32[2]{0:T(128)S(1)} %pad_add_fusion.info_ref, bf16[4,512,128]{2,1,0:T(8,128)(2,1)S(1)} %get-tuple-element.123.data_ref, f32[4,512,128]{2,1,0:T(8,128)S(1)} %shard_map.69.blurred_ref, ...), custom_call_target="tpu_custom_call" | custom-call | bytes 70000 | tf_op jit(solution)/shard_map/pallas_call | solution.py:491
  71.0 1.7 %shard_map.72 = f32[656,128]{1,0:T(8,128)S(1)} custom-call(f32[4,512,128]{2,1,0:T(8,128)S(1)} %get-tuple-element.137.quotient_ref, f32[4,2,64,128]{3,2,1,0:T(8,128)S(1)} %get-tuple-element.138.edge_ref, bf16[4,512,512]{2,1,0:T(8,128)(2,1)S(1)} %copy-done.1, bf16[4,256,256]{2,1,0:T(8,128)(2,1)S(1)} %copy-done.10, bf16[2,4,256,256]{3,2,1,0:T(8,128)(2,1)S(1)} %copy-done.4, ...), custom_call_target="tpu_custom_call" | custom-call | bytes 70000 | tf_op jit(solution)/shard_map/pallas_call | solution.py:491
  72.8 1.6 %shard_map.71 = (f32[512,128]{1,0:T(8,128)S(1)}, f32[2,64,128]{2,1,0:T(8,128)S(1)}) custom-call(f32[4,512,128]{2,1,0:T(8,128)S(1)} %get-tuple-element.137.quotient_ref, f32[4,2,64,128]{3,2,1,0:T(8,128)S(1)} %get-tuple-element.138.edge_ref, bf16[4,512,512]{2,1,0:T(8,128)(2,1)S(1)} %copy-done, bf16[4,256,256]{2,1,0:T(8,128)(2,1)S(1)} %copy-done.6, ...), custom_call_target="tpu_custom_call" | custom-call | bytes 70000 | tf_op jit(solution)/shard_map/pallas_call | solution.py:491
  74.4 1.9 %collective-permute-done.11 = f16[656,128]{1,0:T(8,128)(2,1)S(1)} collective-permute-done((f16[656,128]{1,0:T(8,128)(2,1)S(1)}, f16[656,128]{1,0:T(8,128)(2,1)S(1)}, u32[]{:S(2)}, u32[]{:S(2)}) %collective-permute-start.11) | collective-permute-done | bytes 167968 | tf_op jit(solution)/shard_map/ppermute | solution.py:531
  76.4 0.4 collective-permute-start.12
  76.9 3.5 %collective-permute-done.12.up_in_ref = f32[64,128]{1,0:T(8,128)S(1)} collective-permute-done((f32[64,128]{1,0:T(8,128)S(1)}, f32[64,128]{1,0:T(8,128)S(1)}, u32[]{:S(2)}, u32[]{:S(2)}) %collective-permute-start.12) | collective-permute-done | bytes 32800 | tf_op jit(solution)/shard_map/ppermute | solution.py:527
  80.4 1.6 %shard_map.74 = f32[32,16,128]{2,1,0:T(8,128)} custom-call(s32[2]{0:T(128)S(1)} %pad_add_fusion.info_ref, f32[640,128]{1,0:T(8,128)S(1)} %get-tuple-element.122.own_ref.old_ref, f32[512,128]{1,0:T(8,128)S(1)} %get-tuple-element.142.total_ref, f32[64,128]{1,0:T(8,128)S(1)} %collective-permute-done.12.up_in_ref, f32[64,128]{1,0:T(8,128)S(1)} %collective-permute-done.13.down_in_ref), custom_call_target="tpu_custom_call" | custom-call | bytes 70000 | tf_op jit(solution)/shard_map/pallas_call | solution.py:491
  (113 shorter events, 2.9 us)
Async XLA Ops:
  1.9 5.0 %collective-permute-start = (f32[64,128]{1,0:T(8,128)S(1)}, f32[64,128]{1,0:T(8,128)S(1)}, u32[]{:S(2)}, u32[]{:S(2)}) collective-permute-start(f32[64,128]{1,0:T(8,128)S(1)} %get-tuple-element.78), channel_id=1, source_target_pairs={{0,1},{1,0},{2,3},{3,2},{4,5},{5,4},{6,7},{7,6},{8,9},{9,8},{10,11... | collective-permute-start | bytes 98312 | tf_op jit(solution)/shard_map/ppermute | solution.py:527
  5.0 1.9 %collective-permute-start.1 = (f32[64,128]{1,0:T(8,128)S(1)}, f32[64,128]{1,0:T(8,128)S(1)}, u32[]{:S(2)}, u32[]{:S(2)}) collective-permute-start(f32[64,128]{1,0:T(8,128)S(1)} %get-tuple-element.79), channel_id=1, source_target_pairs={{0,4},{1,2},{2,1},{3,7},{4,0},{5,6},{6,5},{7,3},{8,12},{9,10},{10,... | collective-permute-start | bytes 98312 | tf_op jit(solution)/shard_map/ppermute | solution.py:531
  5.0 10.7 %copy-start.26 = (s32[8,4,4,3]{0,2,3,1:T(4,128)S(1)}, s32[8,4,4,3]{0,2,3,1:T(4,128)}, u32[]{:S(2)}) copy-start(s32[8,4,4,3]{0,2,3,1:T(4,128)} %param.9) | copy-start | bytes 4612
  5.1 11.3 %copy-start.28 = (f32[48,31]{0,1:T(8,128)S(1)}, f32[48,31]{0,1:T(8,128)}, u32[]{:S(2)}) copy-start(f32[48,31]{0,1:T(8,128)} %param.8) | copy-start | bytes 17860
  6.9 20.0 %copy-start.27 = (s32[4096]{0:T(1024)S(1)}, s32[4096]{0:T(1024)}, u32[]{:S(2)}) copy-start(s32[4096]{0:T(1024)} %param.7) | copy-start | bytes 49156
  6.9 32.7 %all-to-all-start = ((bf16[32,8,2048]{2,1,0:T(8,128)(2,1)}), bf16[32,8,2048]{2,1,0:T(8,128)(2,1)S(1)}, u32[]{:S(2)}, u32[]{:S(2)}) async-start(bf16[32,8,2048]{2,1,0:T(8,128)(2,1)} %bitcast.5), calls=%async_computation | async-start | bytes 2097152 | tf_op jit(solution)/shard_map/all_to_all | solution.py:608
  13.8 21.3 %collective-permute-start.3 = (f16[640,128]{1,0:T(8,128)(2,1)S(1)}, f16[640,128]{1,0:T(8,128)(2,1)S(1)}, u32[]{:S(2)}, u32[]{:S(2)}) collective-permute-start(f16[640,128]{1,0:T(8,128)(2,1)S(1)} %convert_element_type.48), channel_id=1, source_target_pairs={{0,1},{1,0},{2,3},{3,2},{4,8},{5,9},{6,10},{7,11},{8,4},{9,5},{10,... | collective-permute-start | bytes 491528 | tf_op jit(solution)/shard_map/ppermute | solution.py:531
  15.6 15.8 %collective-permute-start.2 = (f16[640,128]{1,0:T(8,128)(2,1)S(1)}, f16[640,128]{1,0:T(8,128)(2,1)S(1)}, u32[]{:S(2)}, u32[]{:S(2)}) collective-permute-start(f16[640,128]{1,0:T(8,128)(2,1)S(1)} %convert_element_type.48), channel_id=1, source_target_pairs={{0,4},{1,5},{2,6},{3,7},{4,0},{5,1},{6,2},{7,3},{8,12},{9,13},{10,... | collective-permute-start | bytes 491528 | tf_op jit(solution)/shard_map/ppermute | solution.py:527
  40.5 8.4 %copy-start.1 = (bf16[4,512,512]{2,1,0:T(8,128)(2,1)S(1)}, bf16[4,512,512]{2,1,0:T(8,128)(2,1)}, u32[]{:S(2)}) copy-start(bf16[4,512,512]{2,1,0:T(8,128)(2,1)} %get-tuple-element.114.k_ref) | copy-start | bytes 6291460
  40.5 8.4 %copy-start.4 = (bf16[2,4,256,256]{3,2,1,0:T(8,128)(2,1)S(1)}, bf16[2,4,256,256]{3,2,1,0:T(8,128)(2,1)}, u32[]{:S(2)}) copy-start(bf16[2,4,256,256]{3,2,1,0:T(8,128)(2,1)} %get-tuple-element.116.xy_ref) | copy-start | bytes 3145732
  40.5 8.4 %copy-start.10 = (bf16[4,256,256]{2,1,0:T(8,128)(2,1)S(1)}, bf16[4,256,256]{2,1,0:T(8,128)(2,1)}, u32[]{:S(2)}) copy-start(bf16[4,256,256]{2,1,0:T(8,128)(2,1)} %get-tuple-element.115.y_ref) | copy-start | bytes 1572868
  40.5 8.4 %copy-start.20 = (bf16[2,32,512]{2,1,0:T(8,128)(2,1)S(1)}, bf16[2,32,512]{2,1,0:T(8,128)(2,1)}, u32[]{:S(2)}) copy-start(bf16[2,32,512]{2,1,0:T(8,128)(2,1)} %get-tuple-element.117.z_ref) | copy-start | bytes 196612
  46.5 6.1 %collective-permute-start.5 = (f16[656,128]{1,0:T(8,128)(2,1)S(1)}, f16[656,128]{1,0:T(8,128)(2,1)S(1)}, u32[]{:S(2)}, u32[]{:S(2)}) collective-permute-start(f16[656,128]{1,0:T(8,128)(2,1)S(1)} %convert_element_type.53), channel_id=1, source_target_pairs={{0,1},{1,0},{2,3},{3,2},{4,8},{5,9},{6,10},{7,11},{8,4},{9,5},{10,... | collective-permute-start | bytes 503816 | tf_op jit(solution)/shard_map/ppermute | solution.py:531
  50.7 1.9 %collective-permute-start.4 = (f16[656,128]{1,0:T(8,128)(2,1)S(1)}, f16[656,128]{1,0:T(8,128)(2,1)S(1)}, u32[]{:S(2)}, u32[]{:S(2)}) collective-permute-start(f16[656,128]{1,0:T(8,128)(2,1)S(1)} %convert_element_type.51), channel_id=1, source_target_pairs={{0,4},{1,5},{2,6},{3,7},{4,0},{5,1},{6,2},{7,3},{8,12},{9,13},{10,... | collective-permute-start | bytes 503816 | tf_op jit(solution)/shard_map/ppermute | solution.py:527
  50.9 7.3 %copy-start.18 = (f32[640,128]{1,0:T(8,128)S(1)}, f32[640,128]{1,0:T(8,128)}, u32[]{:S(2)}) copy-start(f32[640,128]{1,0:T(8,128)} %get-tuple-element.88.old_ref) | copy-start | bytes 983044
  50.9 10.7 %copy-start.16 = (bf16[384,512]{1,0:T(8,128)(2,1)S(1)}, bf16[384,512]{1,0:T(8,128)(2,1)}, u32[]{:S(2)}) copy-start(bf16[384,512]{1,0:T(8,128)(2,1)} %get-tuple-element.125.y_ref) | copy-start | bytes 1179652
  52.5 9.1 %copy-start.7 = (bf16[4,512,512]{2,1,0:T(8,128)(2,1)S(1)}, bf16[4,512,512]{2,1,0:T(8,128)(2,1)}, u32[]{:S(2)}) copy-start(bf16[4,512,512]{2,1,0:T(8,128)(2,1)} %get-tuple-element.124.k_ref) | copy-start | bytes 6291460
  52.5 9.0 %copy-start.12 = (bf16[2,4,256,256]{3,2,1,0:T(8,128)(2,1)S(1)}, bf16[2,4,256,256]{3,2,1,0:T(8,128)(2,1)}, u32[]{:S(2)}) copy-start(bf16[2,4,256,256]{3,2,1,0:T(8,128)(2,1)} %get-tuple-element.126.xy_ref) | copy-start | bytes 3145732
  52.6 9.0 %copy-start.22 = (bf16[2,128,128]{2,1,0:T(8,128)(2,1)S(1)}, bf16[2,128,128]{2,1,0:T(8,128)(2,1)}, u32[]{:S(2)}) copy-start(bf16[2,128,128]{2,1,0:T(8,128)(2,1)} %get-tuple-element.127.z_ref) | copy-start | bytes 196612
  53.5 4.7 %collective-permute-start.6 = (f32[128,128]{1,0:T(8,128)S(1)}, f32[128,128]{1,0:T(8,128)S(1)}, u32[]{:S(2)}, u32[]{:S(2)}) collective-permute-start(f32[128,128]{1,0:T(8,128)S(1)} %get-tuple-element.120.up_ref), channel_id=1, source_target_pairs={{0,1},{1,0},{2,3},{3,2},{4,5},{5,4},{6,7},{7,6},{8,9},{9,8},{10,11... | collective-permute-start | bytes 196616 | tf_op jit(solution)/shard_map/ppermute | solution.py:527
  55.2 3.0 %collective-permute-start.7 = (f32[128,128]{1,0:T(8,128)S(1)}, f32[128,128]{1,0:T(8,128)S(1)}, u32[]{:S(2)}, u32[]{:S(2)}) collective-permute-start(f32[128,128]{1,0:T(8,128)S(1)} %get-tuple-element.121.down_ref), channel_id=1, source_target_pairs={{0,4},{1,2},{2,1},{3,7},{4,0},{5,6},{6,5},{7,3},{8,12},{9,10},{10,... | collective-permute-start | bytes 196616 | tf_op jit(solution)/shard_map/ppermute | solution.py:531
  59.1 4.9 %collective-permute-start.8 = (f16[656,128]{1,0:T(8,128)(2,1)S(1)}, f16[656,128]{1,0:T(8,128)(2,1)S(1)}, u32[]{:S(2)}, u32[]{:S(2)}) collective-permute-start(f16[656,128]{1,0:T(8,128)(2,1)S(1)} %convert_element_type.55), channel_id=1, source_target_pairs={{0,4},{1,5},{2,6},{3,7},{4,0},{5,1},{6,2},{7,3},{8,12},{9,13},{10,... | collective-permute-start | bytes 503816 | tf_op jit(solution)/shard_map/ppermute | solution.py:527
  59.3 7.3 %collective-permute-start.9 = (f16[656,128]{1,0:T(8,128)(2,1)S(1)}, f16[656,128]{1,0:T(8,128)(2,1)S(1)}, u32[]{:S(2)}, u32[]{:S(2)}) collective-permute-start(f16[656,128]{1,0:T(8,128)(2,1)S(1)} %convert_element_type.55), channel_id=1, source_target_pairs={{0,1},{1,0},{2,3},{3,2},{4,8},{5,9},{6,10},{7,11},{8,4},{9,5},{10,... | collective-permute-start | bytes 503816 | tf_op jit(solution)/shard_map/ppermute | solution.py:531
  61.6 5.0 %copy-start.15 = (bf16[384,512]{1,0:T(8,128)(2,1)S(1)}, bf16[384,512]{1,0:T(8,128)(2,1)}, u32[]{:S(2)}) copy-start(bf16[384,512]{1,0:T(8,128)(2,1)} %get-tuple-element.134.y_ref) | copy-start | bytes 1179652
  64.2 2.8 %copy-start.9 = (bf16[4,512,512]{2,1,0:T(8,128)(2,1)S(1)}, bf16[4,512,512]{2,1,0:T(8,128)(2,1)}, u32[]{:S(2)}) copy-start(bf16[4,512,512]{2,1,0:T(8,128)(2,1)} %get-tuple-element.133.k_ref) | copy-start | bytes 6291460
  64.2 2.8 %copy-start.11 = (bf16[4,256,256]{2,1,0:T(8,128)(2,1)S(1)}, bf16[4,256,256]{2,1,0:T(8,128)(2,1)}, u32[]{:S(2)}) copy-start(bf16[4,256,256]{2,1,0:T(8,128)(2,1)} %get-tuple-element.102.refs_3_.ya_ref) | copy-start | bytes 1572868
  64.2 2.8 %copy-start.21 = (bf16[2,32,512]{2,1,0:T(8,128)(2,1)S(1)}, bf16[2,32,512]{2,1,0:T(8,128)(2,1)}, u32[]{:S(2)}) copy-start(bf16[2,32,512]{2,1,0:T(8,128)(2,1)} %get-tuple-element.104.refs_5_.za_ref) | copy-start | bytes 196612
  64.2 2.8 %copy-start.23 = (bf16[2,128,128]{2,1,0:T(8,128)(2,1)S(1)}, bf16[2,128,128]{2,1,0:T(8,128)(2,1)}, u32[]{:S(2)}) copy-start(bf16[2,128,128]{2,1,0:T(8,128)(2,1)} %get-tuple-element.136.z_ref) | copy-start | bytes 196612
  70.8 5.4 %collective-permute-start.11 = (f16[656,128]{1,0:T(8,128)(2,1)S(1)}, f16[656,128]{1,0:T(8,128)(2,1)S(1)}, u32[]{:S(2)}, u32[]{:S(2)}) collective-permute-start(f16[656,128]{1,0:T(8,128)(2,1)S(1)} %convert_element_type.60), channel_id=1, source_target_pairs={{0,1},{1,0},{2,3},{3,2},{4,8},{5,9},{6,10},{7,11},{8,4},{9,5},{10,... | collective-permute-start | bytes 503816 | tf_op jit(solution)/shard_map/ppermute | solution.py:531
  72.7 3.5 %collective-permute-start.10 = (f16[656,128]{1,0:T(8,128)(2,1)S(1)}, f16[656,128]{1,0:T(8,128)(2,1)S(1)}, u32[]{:S(2)}, u32[]{:S(2)}) collective-permute-start(f16[656,128]{1,0:T(8,128)(2,1)S(1)} %convert_element_type.58), channel_id=1, source_target_pairs={{0,4},{1,5},{2,6},{3,7},{4,0},{5,1},{6,2},{7,3},{8,12},{9,13},{10,... | collective-permute-start | bytes 503816 | tf_op jit(solution)/shard_map/ppermute | solution.py:527
  76.4 4.0 %collective-permute-start.12 = (f32[64,128]{1,0:T(8,128)S(1)}, f32[64,128]{1,0:T(8,128)S(1)}, u32[]{:S(2)}, u32[]{:S(2)}) collective-permute-start(f32[64,128]{1,0:T(8,128)S(1)} %get-tuple-element.143), channel_id=1, source_target_pairs={{0,1},{1,0},{2,3},{3,2},{4,5},{5,4},{6,7},{7,6},{8,9},{9,8},{10,11... | collective-permute-start | bytes 98312 | tf_op jit(solution)/shard_map/ppermute | solution.py:527
  76.8 3.6 %collective-permute-start.13 = (f32[64,128]{1,0:T(8,128)S(1)}, f32[64,128]{1,0:T(8,128)S(1)}, u32[]{:S(2)}, u32[]{:S(2)}) collective-permute-start(f32[64,128]{1,0:T(8,128)S(1)} %get-tuple-element.144), channel_id=1, source_target_pairs={{0,4},{1,2},{2,1},{3,7},{4,0},{5,6},{6,5},{7,3},{8,12},{9,10},{10,... | collective-permute-start | bytes 98312 | tf_op jit(solution)/shard_map/ppermute | solution.py:531
  (12 other events, 26.4 us)

commit v3 on v2

--- a/solution.py
+++ b/solution.py
@@ -223,6 +223,23 @@
     return jnp.concatenate(rows, axis=0)
 
 
+def unpack_strips(up, down, shifts):
+    lane = iota((NZ, LANES), 1)
+    inside = []
+    for shift in shifts:
+        first = jnp.where(shift > 0, BY - STRIP, 0)
+        inside.append(jnp.logical_and(lane >= first, lane < first + STRIP))
+    rows = []
+    for x in range(BX):
+        half, j = x // 8, x % 8
+        moved = [
+            pltpu.roll(a[half * NZ : (half + 1) * NZ, :], 2 * LANES - shift - STRIP * j, 1)
+            for a, shift in zip((up, down), shifts)
+        ]
+        rows.append(jnp.where(inside[0], moved[0], jnp.where(inside[1], moved[1], 0.0)))
+    return jnp.concatenate(rows, axis=0)
+
+
 def wide(halves):
     return jnp.concatenate([halves[:NZ], halves[NZ:]], axis=1)
 
@@ -253,31 +270,27 @@
     return dot(jnp.concatenate([hi, lo, hi], axis=1), stacked)
 
 
-def forward_parts(sources, shifts, add):
-    for field, _, (k, y, _, _) in sources:
-        spread = three_lanes(field, y[...])
-        for v in range(V):
-            add(v, two_lanes(k[v], spread[:, v * BY : (v + 1) * BY]))
+def forward_parts(message, matrices, shifts, add):
+    k, y, xy, z = matrices
+    field, strips = message_parts(message)
+    totals = []
     for yr in range(2):
-        totals = [jnp.zeros((NZ, 2 * LANES), f32) for _ in range(V)]
-        for _, strips, (_, _, xy, z) in sources:
-            along = dot(z[yr], column3(wide(strips[yr])))
-            for v in range(V):
-                totals[v] += two_rows(along[v * NZ : (v + 1) * NZ], xy[yr, v])
-        for v in range(V):
-            add(v, unpack_strip(tall(totals[v]), shifts[yr]))
-
-
-def adjoint_parts(quotient_ref, edge_ref, refs, ready=lambda v: None):
+        along = dot(z[yr], column3(wide(strips[yr])))
+        totals.append([tall(two_rows(along[v * NZ : (v + 1) * NZ], xy[yr, v])) for v in range(V)])
+    spread = three_lanes(field, y[...])
+    for v in range(V):
+        center = two_lanes(k[v], spread[:, v * BY : (v + 1) * BY])
+        add(v, center + unpack_strips(totals[0][v], totals[1][v], shifts))
+
+
+def adjoint_parts(quotient_ref, edge_ref, refs):
     k_ref, y_ref, xy_ref, z_ref = refs
     total = jnp.zeros((FIELD, LANES), f32)
     for v in range(V):
         hi, lo = split(quotient_ref[v])
         both = dot(jnp.concatenate([hi, lo], axis=1), y_ref[v])
         spread = both[:, :BY] + both[:, BY:]
-        ready(v)
         total += two_lanes(k_ref[v], spread)
-    ready(V)
     strips = []
     for yr in range(2):
         parts = [column3(two_rows(wide(edge_ref[v, yr]), xy_ref[yr, v])) for v in range(V)]
@@ -326,67 +339,63 @@
         copy.wait()
 
 
-def forward_first_kernel(last, info_ref, *refs):
-    before = len(refs) - (13 if last else 12)
-    message_ref, matrices, kept = refs[before], refs[before + 1 : before + 5], refs[before + 5 : before + 10]
-    result_ref, out_ref, sems = refs[before + 10 :] if last else (None, *refs[before + 10 :])
-    copies = fetch((*matrices, message_ref), kept, sems)
+def forward_first_kernel(info_ref, *refs):
+    before = len(refs) - 6
+    message_ref, matrices, out_ref = refs[before], refs[before + 1 : before + 5], refs[-1]
     shifts = (info_ref[0], info_ref[1])
-    out_ref[...] = refs[0][...] if before else jnp.zeros_like(out_ref)
 
     def add(v, part):
-        out_ref[v] += part
-
-    forward_parts([(*message_parts(message_ref[...]), matrices)], shifts, add)
-    if last:
-        for v in range(V):
-            out_ref[v] = 1.0 / out_ref[v]
-        copies.append(pltpu.make_async_copy(out_ref, result_ref, sems.at[len(copies)]))
-        copies[-1].start()
-    for copy in copies:
-        copy.wait()
-
-
-def adjoint_far(quotient_ref, edge_ref, shifts, refs, far_ref, ready=lambda v: None):
+        out_ref[v] = part + refs[0][v] if before else part
+
+    forward_parts(message_ref[...], matrices, shifts, add)
+
+
+def forward_inverse_kernel(info_ref, blurred_ref, message_ref, k_ref, y_ref, xy_ref, z_ref, result_ref, out_ref, sem):
+    shifts = (info_ref[0], info_ref[1])
+
+    def add(v, part):
+        out_ref[v] = 1.0 / (blurred_ref[v] + part)
+
+    forward_parts(message_ref[...], (k_ref, y_ref, xy_ref, z_ref), shifts, add)
+    copy = pltpu.make_async_copy(out_ref, result_ref, sem)
+    copy.start()
+    copy.wait()
+
+
+def pack_edges(quotient_ref, edge_ref, shifts):
     for v in range(V):
         for yr in range(2):
             edge_ref[v, yr] = pack_strip(quotient_ref[v], shifts[yr])
-    write_scaled(far_ref, *adjoint_parts(quotient_ref, edge_ref, refs, ready))
-
-
-def quotient_first_kernel(info_ref, *refs):
+
+
+def quotient_first_kernel(info_ref, arrived_ref, *refs):
     outside, (data_ref, quotient_ref, edge_ref, far_ref), held, sems = (
-        refs[:7], refs[7:11], refs[11:18], refs[18],
-    )
-    pairs = list(zip(outside[:4], held[:4]))
-    pairs += [(outside[6].at[v], held[6].at[v]) for v in range(V)]
-    pairs += list(zip(outside[4:6], held[4:6]))
-    copies = [pltpu.make_async_copy(a, b, sems.at[n]) for n, (a, b) in enumerate(pairs)]
-    for copy in copies:
-        copy.start()
-    table_ref, arrived_ref, inverse_ref, y_ref, xy_ref, z_ref, k_ref = held
+        refs[:6], refs[6:10], refs[10:16], refs[16],
+    )
+    copies = fetch(outside, held, sems)
+    table_ref, inverse_ref, *matrices = held
     shifts = (info_ref[0], info_ref[1])
     copies[0].wait()
     copies[1].wait()
-    planes = dot(table_ref[...], arrived_ref[...])
-    copies[2].wait()
-    for v in range(V):
-        for x in range(BX):
-            rows = slice(x * NZ, (x + 1) * NZ)
-            piece = planes[v * NZ : (v + 1) * NZ, x * BY : (x + 1) * BY]
-            data_ref[v, rows, :] = piece.astype(bf16)
-            quotient_ref[v, rows, :] = piece * inverse_ref[v, rows, :]
-    copies[3].wait()
-
-    def ready(v):
-        for copy in copies[4 + v : 5 + v] if v < V else copies[4 + V :]:
-            copy.wait()
-
-    adjoint_far(quotient_ref, edge_ref, shifts, (k_ref, y_ref, xy_ref, z_ref), far_ref, ready)
-
-
-def adjoint_near_kernel(quotient_ref, edge_ref, k_ref, y_ref, xy_ref, z_ref, near_ref):
-    write_scaled(near_ref, *adjoint_parts(quotient_ref, edge_ref, (k_ref, y_ref, xy_ref, z_ref)))
+
+    @pl.when(shifts[0] >= 0)
+    def _():
+        planes = dot(table_ref[...], arrived_ref[...])
+        for v in range(V):
+            for x in range(BX):
+                rows = slice(x * NZ, (x + 1) * NZ)
+                piece = planes[v * NZ : (v + 1) * NZ, x * BY : (x + 1) * BY]
+                data_ref[v, rows, :] = piece.astype(bf16)
+                quotient_ref[v, rows, :] = piece * inverse_ref[v, rows, :]
+        pack_edges(quotient_ref, edge_ref, shifts)
+
+    for copy in copies[2:]:
+        copy.wait()
+    write_scaled(far_ref, *adjoint_parts(quotient_ref, edge_ref, matrices))
+
+
+def adjoint_side_kernel(quotient_ref, edge_ref, k_ref, y_ref, xy_ref, z_ref, message_ref):
+    write_scaled(message_ref, *adjoint_parts(quotient_ref, edge_ref, (k_ref, y_ref, xy_ref, z_ref)))
 
 
 def adjoint_center_kernel(quotient_ref, edge_ref, k_ref, y_ref, xy_ref, z_ref, field_ref, strips_ref):
@@ -432,22 +441,20 @@
 
 def forward_center_kernel(info_ref, own_ref, k_ref, y_ref, xy_ref, z_ref, out_ref):
     shifts = (info_ref[0], info_ref[1])
-    out_ref[...] = jnp.zeros_like(out_ref)
 
     def add(v, part):
-        out_ref[v] += part
-
-    forward_parts([(*message_parts(own_ref[...]), (k_ref, y_ref, xy_ref, z_ref))], shifts, add)
+        out_ref[v] = part
+
+    forward_parts(own_ref[...], (k_ref, y_ref, xy_ref, z_ref), shifts, add)
 
 
 def forward_near_kernel(info_ref, blurred_ref, near_ref, k_ref, y_ref, xy_ref, z_ref, out_ref):
     shifts = (info_ref[0], info_ref[1])
-    out_ref[...] = blurred_ref[...]
 
     def add(v, part):
-        out_ref[v] += part
-
-    forward_parts([(*message_parts(read_scaled(near_ref)), (k_ref, y_ref, xy_ref, z_ref))], shifts, add)
+        out_ref[v] = blurred_ref[v] + part
+
+    forward_parts(read_scaled(near_ref), (k_ref, y_ref, xy_ref, z_ref), shifts, add)
 
 
 def middle_kernel(
@@ -455,16 +462,13 @@
     ka_ref, ya_ref, xya_ref, za_ref, quotient_ref, edge_ref, far_ref,
 ):
     shifts = (info_ref[0], info_ref[1])
-    quotient_ref[...] = blurred_ref[...]
 
     def add(v, part):
-        quotient_ref[v] += part
-
-    sources = [(*message_parts(read_scaled(from_far_ref)), (k_ref, y_ref, xy_ref, z_ref))]
-    forward_parts(sources, shifts, add)
-    for v in range(V):
-        quotient_ref[v] = data_ref[v].astype(f32) / quotient_ref[v]
-    adjoint_far(quotient_ref, edge_ref, shifts, (ka_ref, ya_ref, xya_ref, za_ref), far_ref)
+        quotient_ref[v] = data_ref[v].astype(f32) / (blurred_ref[v] + part)
+
+    forward_parts(read_scaled(from_far_ref), (k_ref, y_ref, xy_ref, z_ref), shifts, add)
+    pack_edges(quotient_ref, edge_ref, shifts)
+    write_scaled(far_ref, *adjoint_parts(quotient_ref, edge_ref, (ka_ref, ya_ref, xya_ref, za_ref)))
 
 
 def final_kernel(info_ref, old_ref, total_ref, up_in_ref, down_in_ref, out_ref):
@@ -631,16 +635,15 @@
     )
     forward_far, forward_near, forward_center = forward[:4], forward[4:8], forward[8:]
 
-    def first_part(total, source, matrices, last=False):
-        return call(
-            functools.partial(forward_first_kernel, last), forward_shapes[:4] + [(message, f32), (every, f32)],
-            info, *total, source, *matrices, scalars=1, out_place=[HBM] * 5 + [HBM if last else VMEM],
-            scratch=[pltpu.VMEM(every, f32)] * last + [pltpu.SemaphoreType.DMA((6,))],
+    blurred = ()
+    for message_in, matrices in ((old, forward_center), (near, forward_near)):
+        blurred = call(
+            forward_first_kernel, [(every, f32)], info, *blurred, message_in, *matrices, scalars=1
         )
-
-    *forward_center, old, total = first_part((), old, forward_center)
-    *forward_near, _, total = first_part((total,), near, forward_near)
-    *forward_far, _, inverse = first_part((total,), far, forward_far, last=True)
+    (inverse,) = call(
+        forward_inverse_kernel, [(every, f32)], info, *blurred, far, *forward_far, scalars=1,
+        out_place=HBM, scratch=[pltpu.VMEM(every, f32), pltpu.SemaphoreType.DMA],
+    )
     adjoint_of_far, adjoint_near, adjoint_center = adjoint[:4], adjoint[4:8], adjoint[8:]
     (table,) = call(
         functools.partial(arrival_kernel, cap), [((slots, rows), bf16)],
@@ -649,17 +652,16 @@
     )
 
     edges = ((V, 2) + half, f32)
-    k, y, xy, z = adjoint_of_far
-    fetched = (table, arrived, inverse, y, xy, z, k)
+    fetched = (table, inverse, *adjoint_of_far)
     data, quotient, edge, far = call(
         quotient_first_kernel, [(every, bf16), (every, f32), edges, (scaled, f32)],
-        info, scalars=1, far=fetched, cost=QUICK,
-        scratch=held([(a.shape, a.dtype) for a in fetched]) + [pltpu.SemaphoreType.DMA((len(fetched) + V - 1,))],
+        info, arrived, scalars=1, far=fetched,
+        scratch=held([(a.shape, a.dtype) for a in fetched]) + [pltpu.SemaphoreType.DMA((len(fetched),))],
     )
 
     def sides(quotient, edge, far):
         far = swap_far("gx", far)
-        (near,) = call(adjoint_near_kernel, [(scaled, f32)], quotient, edge, *adjoint_near)
+        (near,) = call(adjoint_side_kernel, [(scaled, f32)], quotient, edge, *adjoint_near)
         near = swap_near("gx", near)
         center = [(one, f32), ((2,) + half, f32)]
         field, strips = call(adjoint_center_kernel, center, quotient, edge, *adjoint_center, cost=QUICK)
@@ -670,6 +672,10 @@
         gather_kernel, [(one, f32), (both, f32), (both, f32)], info, *sides(quotient, edge, far), scalars=1
     )
     up_in, down_in = swap("gy", up, down)
+    taps, backward, up, down = lax.optimization_barrier((taps, backward, up, down))
+    forward = call(build_forward_kernel, forward_shapes, taps, backward)
+    old, *forward = lax.optimization_barrier((old, *forward))
+    forward_far, forward_near, forward_center = forward[:4], forward[4:8], forward[8:]
     new, new_scaled = call(
         update_kernel, [(message, f32), (scaled, f32)],
         info, old, total, up, down, up_in, down_in, scalars=1,

time: 82.2 us -> 79.8 us (0.971); the launches traced: 82 us -> 78.6 us
  Pallas kernels: 50 us -> 46.3 us
  starting transfers between devices: 19.3 us -> 21.8 us
  local copies, waits for them, and re-layouts: 2.4 us -> 1.07 us
    pallas_call x20 -> x21, Pallas kernels: 50 us -> 46.3 us  [call(): pl.pallas_call(kernel, out_shape=[HBM(s, d) if where is HBM else jax.Shap...]
    ppermute x7, waiting for transfers between devices: 6.65 us -> 3.13 us  [swap_near(): lax.ppermute(narrow(axis, value), ('gx', 'gy'), partner_swaps(axis)[0])]
    all_to_all x1, waiting for transfers between devices: 0.01 us -> 2.62 us  [shards(): lax.all_to_all(outgoing.reshape(devices, cap, plane), ('gx', 'gy'), split...]
    ppermute x7, starting transfers between devices: 6.75 us -> 8.35 us  [swap_far(): lax.ppermute(narrow(axis, value), ('gx', 'gy'), partner_swaps(axis)[1])]
    unnamed x60 -> x32, local copies, waits for them, and re-layouts: 1.48 us -> 0.16 us
    ppermute x7, starting transfers between devices: 5.65 us -> 6.62 us  [swap_near(): lax.ppermute(narrow(axis, value), ('gx', 'gy'), partner_swaps(axis)[0])]
  transfers between devices with their start and end apart: 15 -> 15, of which waited for: 4 -> 6; matrix products, arithmetic and copies ran while one was open for 2% -> 2% of each run, Pallas kernels for 43% -> 41%
where the time goes in v3:
time: 79.8 us; the launch traced here: 78.6 us
  Pallas kernels  46.3 us (58%)
  starting transfers between devices  21.8 us (27%)
  waiting for transfers between devices  7.79 us (10%)
  local copies, waits for them, and re-layouts  1.07 us (1%)
    pallas_call x21, Pallas kernels, call(): pl.pallas_call(kernel, out_shape=[HBM(s, d) if where is HBM else jax.Shap...  46.3 us
    ppermute x7, starting transfers between devices, swap_far(): lax.ppermute(narrow(axis, value), ('gx', 'gy'), partner_swaps(axis)[1])  8.35 us
    all_to_all x1, starting transfers between devices, shards(): lax.all_to_all(outgoing.reshape(devices, cap, plane), ('gx', 'gy'), split...  6.85 us
    ppermute x7, starting transfers between devices, swap_near(): lax.ppermute(narrow(axis, value), ('gx', 'gy'), partner_swaps(axis)[0])  6.62 us
    ppermute x7, waiting for transfers between devices, swap_near(): lax.ppermute(narrow(axis, value), ('gx', 'gy'), partner_swaps(axis)[0])  3.13 us
    all_to_all x1, waiting for transfers between devices, shards(): lax.all_to_all(outgoing.reshape(devices, cap, plane), ('gx', 'gy'), split...  2.62 us
    ppermute x7, waiting for transfers between devices, swap_far(): lax.ppermute(narrow(axis, value), ('gx', 'gy'), partner_swaps(axis)[1])  2.04 us
  transfers between devices with their start and end apart: 15, of which 6 were waited for; matrix products, arithmetic and copies ran while one was open for 2% of the time, Pallas kernels for 41%

profile of v3, /device:TPU:0, one launch (start us, length us, event | category | flops | bytes accessed | tf_op | source)
XLA Modules:
  0.0 78.6 jit_solution(8065399419038877065)
XLA Ops:
  0.1 1.8 %shard_map.55 = (f32[512,128]{1,0:T(8,128)S(1)}, f32[64,128]{1,0:T(8,128)S(1)}, f32[64,128]{1,0:T(8,128)S(1)}, s32[32,128]{1,0:T(8,128)S(1)}, bf16[128,16,128]{2,1,0:T(8,128)(2,1)S(1)}) custom-call(s32[2]{0:T(128)S(1)} %pad_add_fusion.info_ref, f32[32,16,128]{2,1,0:T(8,128)} %refs_0_.1, s32[32,128]{1,0:T(8,128)} %bitcast.9, bf16[128,16,128]{2,1,0:T(8,128)(2,1)} %refs_2_.1), custom_call_target="tpu_custom_call" | custom-call | bytes 70000 | tf_op jit(solution)/shard_map/pallas_call | solution.py:495
  1.9 3.1 %collective-permute-start = (f32[64,128]{1,0:T(8,128)S(1)}, f32[64,128]{1,0:T(8,128)S(1)}, u32[]{:S(2)}, u32[]{:S(2)}) collective-permute-start(f32[64,128]{1,0:T(8,128)S(1)} %get-tuple-element.91), channel_id=1, source_target_pairs={{0,1},{1,0},{2,3},{3,2},{4,5},{5,4},{6,7},{7,6},{8,9},{9,8},{10,11... | collective-permute-start | bytes 98312 | tf_op jit(solution)/shard_map/ppermute | solution.py:531
  5.1 1.6 %shard_map.56 = bf16[256,2048]{1,0:T(8,128)(2,1)} custom-call(s32[1]{0:T(128)} %bitcast.3.me_ref, s32[32,128]{1,0:T(8,128)S(1)} %get-tuple-element.89.slots_ref, bf16[128,16,128]{2,1,0:T(8,128)(2,1)S(1)} %get-tuple-element.90.stored_ref), custom_call_target="tpu_custom_call" | custom-call | bytes 70000 | tf_op jit(solution)/shard_map/pallas_call | solution.py:495
  6.9 6.9 %all-to-all-start = ((bf16[32,8,2048]{2,1,0:T(8,128)(2,1)}), bf16[32,8,2048]{2,1,0:T(8,128)(2,1)S(1)}, u32[]{:S(2)}, u32[]{:S(2)}) async-start(bf16[32,8,2048]{2,1,0:T(8,128)(2,1)} %bitcast.4), calls=%async_computation | async-start | bytes 2097152 | tf_op jit(solution)/shard_map/all_to_all | solution.py:612
  13.8 1.8 %collective-permute-start.3 = (f16[640,128]{1,0:T(8,128)(2,1)S(1)}, f16[640,128]{1,0:T(8,128)(2,1)S(1)}, u32[]{:S(2)}, u32[]{:S(2)}) collective-permute-start(f16[640,128]{1,0:T(8,128)(2,1)S(1)} %convert_element_type.48), channel_id=1, source_target_pairs={{0,1},{1,0},{2,3},{3,2},{4,8},{5,9},{6,10},{7,11},{8,4},{9,5},{10,... | collective-permute-start | bytes 491528 | tf_op jit(solution)/shard_map/ppermute | solution.py:535
  17.3 2.5 %shard_map.58 = (bf16[4,512,512]{2,1,0:T(8,128)(2,1)S(1)}, bf16[384,512]{1,0:T(8,128)(2,1)S(1)}, bf16[2,4,256,256]{3,2,1,0:T(8,128)(2,1)S(1)}, bf16[2,128,128]{2...) custom-call(f32[108,128]{1,0:T(8,128)S(1)} %get-tuple-element.130.ta, ...), custom_call_target="tpu_custom_call" | custom-call | bytes 10500000 | tf_op jit(solution)/shard_map/pallas_call | solution.py:495
  19.8 7.0 %shard_map.62 = (bf16[4,512,512]{2,1,0:T(8,128)(2,1)}, bf16[4,256,256]{2,1,0:T(8,128)(2,1)}, bf16[2,4,256,256]{3,2,1,0:T(8,128)(2,1)}, bf16[2,32,512]{2,1,0:T(8,...) custom-call(f32[108,128]{1,0:T(8,128)S(1)} %get-tuple-element.130.ta, ...), custom_call_target="tpu_custom_call" | custom-call | bytes 14000000 | tf_op jit(solution)/shard_map/pallas_call | solution.py:495
  26.8 1.0 %shard_map.57.refs_0_ = bf16[128,256]{1,0:T(8,128)(2,1)} custom-call(s32[1]{0:T(128)} %bitcast.3.me_ref, s32[256,128]{1,0:T(8,128)S(1)} %broadcast_bitcast_fusion.slots_ref), custom_call_target="tpu_custom_call" | custom-call | bytes 70000 | tf_op jit(solution)/shard_map/pallas_call | solution.py:495
  27.8 2.0 %shard_map.59.refs_0_ = f32[4,512,128]{2,1,0:T(8,128)S(1)} custom-call(s32[2]{0:T(128)S(1)} %pad_add_fusion.info_ref, f32[640,128]{1,0:T(8,128)S(1)} %constant_dynamic-update-slice_fusion.refs_0_.old_ref, bf16[4,512,512]{2,1,0:T(8,128)(2,1)S(1)} %get-tuple-element.99.refs_1_, bf16[384,512]{1,0:T(8,128)(2,1)S(1)} %get-tuple-element.100.refs_2_, ...), custom_call_target="tpu_custom_call" | custom-call | bytes 70000 | tf_op jit(solution)/shard_map/pallas_call | solution.py:495
  29.9 2.0 %shard_map.60.blurred_ref = f32[4,512,128]{2,1,0:T(8,128)S(1)} custom-call(s32[2]{0:T(128)S(1)} %pad_add_fusion.info_ref, f32[4,512,128]{2,1,0:T(8,128)S(1)} %shard_map.59.refs_0_, f32[640,128]{1,0:T(8,128)S(1)} %convert_element_type.49.refs_1_, bf16[4,512,512]{2,1,0:T(8,128)(2,1)S(1)} %get-tuple-element.103.refs_2_, ...), custom_call_target="tpu_custom_call" | custom-call | bytes 70000 | tf_op jit(solution)/shard_map/pallas_call | solution.py:495
  31.9 1.2 %collective-permute-done.3 = f16[640,128]{1,0:T(8,128)(2,1)S(1)} collective-permute-done((f16[640,128]{1,0:T(8,128)(2,1)S(1)}, f16[640,128]{1,0:T(8,128)(2,1)S(1)}, u32[]{:S(2)}, u32[]{:S(2)}) %collective-permute-start.3) | collective-permute-done | bytes 163872 | tf_op jit(solution)/shard_map/ppermute | solution.py:535
  33.2 3.0 %shard_map.61.refs_1_ = f32[4,512,128]{2,1,0:T(8,128)} custom-call(s32[2]{0:T(128)S(1)} %pad_add_fusion.info_ref, f32[4,512,128]{2,1,0:T(8,128)S(1)} %shard_map.60.blurred_ref, f32[640,128]{1,0:T(8,128)S(1)} %convert_element_type.50.message_ref, bf16[4,512,512]{2,1,0:T(8,128)(2,1)S(1)} %get-tuple-element.107.k_ref, ...), custom_call_target="tpu_custom_call" | custom-call | bytes 70000 | tf_op jit(solution)/shard_map/pallas_call | solution.py:495
  36.2 2.6 %all-to-all-done = bf16[32,8,2048]{2,1,0:T(8,128)(2,1)S(1)} async-done(((bf16[32,8,2048]{2,1,0:T(8,128)(2,1)}), bf16[32,8,2048]{2,1,0:T(8,128)(2,1)S(1)}, u32[]{:S(2)}, u32[]{:S(2)}) %all-to-all-start) | async-done | bytes 1048608 | tf_op jit(solution)/shard_map/all_to_all | solution.py:612
  38.8 5.0 %shard_map.63 = (bf16[4,512,128]{2,1,0:T(8,128)(2,1)S(1)}, f32[4,512,128]{2,1,0:T(8,128)S(1)}, f32[4,2,64,128]{3,2,1,0:T(8,128)S(1)}, f32[656,128]{1,0:T(8,128)S(1)}) custom-call(s32[2]{0:T(128)S(1)} %pad_add_fusion.info_ref, bf16[256,2048]{1,0:T(8,128)(2,1)S(1)} %bitcast.8, bf16[128,256]{1,0:T(8,128)(2,1)} %shard_map.57.refs_0_, ...), custom_call_target="tpu_custom_call" | custom-call | bytes 70000 | tf_op jit(solution)/shard_map/pallas_call | solution.py:495
  43.8 3.2 %collective-permute-start.5 = (f16[656,128]{1,0:T(8,128)(2,1)S(1)}, f16[656,128]{1,0:T(8,128)(2,1)S(1)}, u32[]{:S(2)}, u32[]{:S(2)}) collective-permute-start(f16[656,128]{1,0:T(8,128)(2,1)S(1)} %convert_element_type.53), channel_id=1, source_target_pairs={{0,1},{1,0},{2,3},{3,2},{4,8},{5,9},{6,10},{7,11},{8,4},{9,5},{10,... | collective-permute-start | bytes 503816 | tf_op jit(solution)/shard_map/ppermute | solution.py:535
  47.0 1.7 %shard_map.65 = f32[656,128]{1,0:T(8,128)S(1)} custom-call(f32[4,512,128]{2,1,0:T(8,128)S(1)} %get-tuple-element.115.quotient_ref, f32[4,2,64,128]{3,2,1,0:T(8,128)S(1)} %get-tuple-element.116.edge_ref, bf16[4,512,512]{2,1,0:T(8,128)(2,1)S(1)} %copy-done.1, bf16[4,256,256]{2,1,0:T(8,128)(2,1)S(1)} %copy-done.7, bf16[2,4,256,256]{3,2,1,0:T(8,128)(2,1)S(1)} %copy-done.4, ...), custom_call_target="tpu_custom_call" | custom-call | bytes 70000 | tf_op jit(solution)/shard_map/pallas_call | solution.py:495
  49.0 1.6 %shard_map.64 = (f32[512,128]{1,0:T(8,128)S(1)}, f32[2,64,128]{2,1,0:T(8,128)S(1)}) custom-call(f32[4,512,128]{2,1,0:T(8,128)S(1)} %get-tuple-element.115.quotient_ref, f32[4,2,64,128]{3,2,1,0:T(8,128)S(1)} %get-tuple-element.116.edge_ref, bf16[4,512,512]{2,1,0:T(8,128)(2,1)S(1)} %copy-done, bf16[4,256,256]{2,1,0:T(8,128)(2,1)S(1)} %copy-done.6, ...), custom_call_target="tpu_custom_call" | custom-call | bytes 70000 | tf_op jit(solution)/shard_map/pallas_call | solution.py:495
  50.7 0.8 %shard_map.66 = (f32[512,128]{1,0:T(8,128)S(1)}, f32[128,128]{1,0:T(8,128)S(1)}, f32[128,128]{1,0:T(8,128)S(1)}) custom-call(s32[2]{0:T(128)S(1)} %pad_add_fusion.info_ref, f32[512,128]{1,0:T(8,128)S(1)} %get-tuple-element.121.field_ref, f32[2,64,128]{2,1,0:T(8,128)S(1)} %get-tuple-element.122.strips_ref, f32[656,128]{1,0:T(8,128)S(1)} %convert_element_type.52.near_ref, ...), custom_call_target="tpu_custom_call" | custom-call | bytes 70000 | tf_op jit(solution)/shard_map/pallas_call | solution.py:495
  51.5 1.8 %collective-permute-start.6 = (f32[128,128]{1,0:T(8,128)S(1)}, f32[128,128]{1,0:T(8,128)S(1)}, u32[]{:S(2)}, u32[]{:S(2)}) collective-permute-start(f32[128,128]{1,0:T(8,128)S(1)} %get-tuple-element.146.up_ref), channel_id=1, source_target_pairs={{0,1},{1,0},{2,3},{3,2},{4,5},{5,4},{6,7},{7,6},{8,9},{9,8},{10,11... | collective-permute-start | bytes 196616 | tf_op jit(solution)/shard_map/ppermute | solution.py:531
  53.3 2.5 %shard_map.67 = (bf16[4,512,512]{2,1,0:T(8,128)(2,1)S(1)}, bf16[384,512]{1,0:T(8,128)(2,1)S(1)}, bf16[2,4,256,256]{3,2,1,0:T(8,128)(2,1)S(1)}, bf16[2,128,128]{2...) custom-call(f32[108,128]{1,0:T(8,128)S(1)} %get-tuple-element.130.ta, ...), custom_call_target="tpu_custom_call" | custom-call | bytes 70000 | tf_op jit(solution)/shard_map/pallas_call | solution.py:495
  56.1 0.9 %shard_map.68 = (f32[640,128]{1,0:T(8,128)S(1)}, f32[656,128]{1,0:T(8,128)S(1)}) custom-call(s32[2]{0:T(128)S(1)} %pad_add_fusion.info_ref, f32[640,128]{1,0:T(8,128)S(1)} %constant_dynamic-update-slice_fusion.refs_0_.old_ref, f32[512,128]{1,0:T(8,128)S(1)} %get-tuple-element.145.total_ref, f32[128,128]{1,0:T(8,128)S(1)} %get-tuple-element.146.up_ref, ...), custom_call_target="tpu_custom_call" | custom-call | bytes 70000 | tf_op jit(solution)/shard_map/pallas_call | solution.py:495
  57.3 1.6 %collective-permute-start.9 = (f16[656,128]{1,0:T(8,128)(2,1)S(1)}, f16[656,128]{1,0:T(8,128)(2,1)S(1)}, u32[]{:S(2)}, u32[]{:S(2)}) collective-permute-start(f16[656,128]{1,0:T(8,128)(2,1)S(1)} %convert_element_type.55), channel_id=1, source_target_pairs={{0,1},{1,0},{2,3},{3,2},{4,8},{5,9},{6,10},{7,11},{8,4},{9,5},{10,... | collective-permute-start | bytes 503816 | tf_op jit(solution)/shard_map/ppermute | solution.py:535
  58.9 2.0 %shard_map.69.blurred_ref = f32[4,512,128]{2,1,0:T(8,128)S(1)} custom-call(s32[2]{0:T(128)S(1)} %pad_add_fusion.info_ref, f32[640,128]{1,0:T(8,128)S(1)} %get-tuple-element.148.own_ref.old_ref, bf16[4,512,512]{2,1,0:T(8,128)(2,1)S(1)} %get-tuple-element.150.k_ref, bf16[384,512]{1,0:T(8,128)(2,1)S(1)} %get-tuple-element.151.y_ref, ...), custom_call_target="tpu_custom_call" | custom-call | bytes 70000 | tf_op jit(solution)/shard_map/pallas_call | solution.py:495
  61.0 2.1 %shard_map.70.blurred_ref = f32[4,512,128]{2,1,0:T(8,128)S(1)} custom-call(s32[2]{0:T(128)S(1)} %pad_add_fusion.info_ref, f32[4,512,128]{2,1,0:T(8,128)S(1)} %shard_map.69.blurred_ref, f32[656,128]{1,0:T(8,128)S(1)} %convert_element_type.56.near_ref, bf16[4,512,512]{2,1,0:T(8,128)(2,1)S(1)} %get-tuple-element.155.k_ref, ...), custom_call_target="tpu_custom_call" | custom-call | bytes 70000 | tf_op jit(solution)/shard_map/pallas_call | solution.py:495
  63.2 3.8 %shard_map.71 = (f32[4,512,128]{2,1,0:T(8,128)S(1)}, f32[4,2,64,128]{3,2,1,0:T(8,128)S(1)}, f32[656,128]{1,0:T(8,128)S(1)}) custom-call(s32[2]{0:T(128)S(1)} %pad_add_fusion.info_ref, bf16[4,512,128]{2,1,0:T(8,128)(2,1)S(1)} %get-tuple-element.149.data_ref, f32[4,512,128]{2,1,0:T(8,128)S(1)} %shard_map.70.blurred_ref, ...), custom_call_target="tpu_custom_call" | custom-call | bytes 70000 | tf_op jit(solution)/shard_map/pallas_call | solution.py:495
  67.0 1.4 %collective-permute-start.11 = (f16[656,128]{1,0:T(8,128)(2,1)S(1)}, f16[656,128]{1,0:T(8,128)(2,1)S(1)}, u32[]{:S(2)}, u32[]{:S(2)}) collective-permute-start(f16[656,128]{1,0:T(8,128)(2,1)S(1)} %convert_element_type.60), channel_id=1, source_target_pairs={{0,1},{1,0},{2,3},{3,2},{4,8},{5,9},{6,10},{7,11},{8,4},{9,5},{10,... | collective-permute-start | bytes 503816 | tf_op jit(solution)/shard_map/ppermute | solution.py:535
  68.5 1.7 %shard_map.73 = f32[656,128]{1,0:T(8,128)S(1)} custom-call(f32[4,512,128]{2,1,0:T(8,128)S(1)} %get-tuple-element.163.quotient_ref, f32[4,2,64,128]{3,2,1,0:T(8,128)S(1)} %get-tuple-element.164.edge_ref, bf16[4,512,512]{2,1,0:T(8,128)(2,1)S(1)} %copy-done.1, bf16[4,256,256]{2,1,0:T(8,128)(2,1)S(1)} %copy-done.7, bf16[2,4,256,256]{3,2,1,0:T(8,128)(2,1)S(1)} %copy-done.4, ...), custom_call_target="tpu_custom_call" | custom-call | bytes 70000 | tf_op jit(solution)/shard_map/pallas_call | solution.py:495
  70.3 1.6 %shard_map.72 = (f32[512,128]{1,0:T(8,128)S(1)}, f32[2,64,128]{2,1,0:T(8,128)S(1)}) custom-call(f32[4,512,128]{2,1,0:T(8,128)S(1)} %get-tuple-element.163.quotient_ref, f32[4,2,64,128]{3,2,1,0:T(8,128)S(1)} %get-tuple-element.164.edge_ref, bf16[4,512,512]{2,1,0:T(8,128)(2,1)S(1)} %copy-done, bf16[4,256,256]{2,1,0:T(8,128)(2,1)S(1)} %copy-done.6, ...), custom_call_target="tpu_custom_call" | custom-call | bytes 70000 | tf_op jit(solution)/shard_map/pallas_call | solution.py:495
  71.9 0.8 collective-permute-done.11
  72.9 1.2 %collective-permute-start.12 = (f32[64,128]{1,0:T(8,128)S(1)}, f32[64,128]{1,0:T(8,128)S(1)}, u32[]{:S(2)}, u32[]{:S(2)}) collective-permute-start(f32[64,128]{1,0:T(8,128)S(1)} %get-tuple-element.169), channel_id=1, source_target_pairs={{0,1},{1,0},{2,3},{3,2},{4,5},{5,4},{6,7},{7,6},{8,9},{9,8},{10,11... | collective-permute-start | bytes 98312 | tf_op jit(solution)/shard_map/ppermute | solution.py:531
  74.4 2.6 %collective-permute-done.12.up_in_ref = f32[64,128]{1,0:T(8,128)S(1)} collective-permute-done((f32[64,128]{1,0:T(8,128)S(1)}, f32[64,128]{1,0:T(8,128)S(1)}, u32[]{:S(2)}, u32[]{:S(2)}) %collective-permute-start.12) | collective-permute-done | bytes 32800 | tf_op jit(solution)/shard_map/ppermute | solution.py:531
  77.1 1.6 %shard_map.75 = f32[32,16,128]{2,1,0:T(8,128)} custom-call(s32[2]{0:T(128)S(1)} %pad_add_fusion.info_ref, f32[640,128]{1,0:T(8,128)S(1)} %get-tuple-element.148.own_ref.old_ref, f32[512,128]{1,0:T(8,128)S(1)} %get-tuple-element.168.total_ref, f32[64,128]{1,0:T(8,128)S(1)} %collective-permute-done.12.up_in_ref, f32[64,128]{1,0:T(8,128)S(1)} %collective-permute-done.13.down_in_ref), custom_call_target="tpu_custom_call" | custom-call | bytes 70000 | tf_op jit(solution)/shard_map/pallas_call | solution.py:495
  (86 shorter events, 3.6 us)
Async XLA Ops:
  1.9 5.0 %collective-permute-start = (f32[64,128]{1,0:T(8,128)S(1)}, f32[64,128]{1,0:T(8,128)S(1)}, u32[]{:S(2)}, u32[]{:S(2)}) collective-permute-start(f32[64,128]{1,0:T(8,128)S(1)} %get-tuple-element.91), channel_id=1, source_target_pairs={{0,1},{1,0},{2,3},{3,2},{4,5},{5,4},{6,7},{7,6},{8,9},{9,8},{10,11... | collective-permute-start | bytes 98312 | tf_op jit(solution)/shard_map/ppermute | solution.py:531
  5.0 1.9 %collective-permute-start.1 = (f32[64,128]{1,0:T(8,128)S(1)}, f32[64,128]{1,0:T(8,128)S(1)}, u32[]{:S(2)}, u32[]{:S(2)}) collective-permute-start(f32[64,128]{1,0:T(8,128)S(1)} %get-tuple-element.92), channel_id=1, source_target_pairs={{0,4},{1,2},{2,1},{3,7},{4,0},{5,6},{6,5},{7,3},{8,12},{9,10},{10,... | collective-permute-start | bytes 98312 | tf_op jit(solution)/shard_map/ppermute | solution.py:535
  5.0 10.7 %copy-start.12 = (s32[8,4,4,3]{0,2,3,1:T(4,128)S(1)}, s32[8,4,4,3]{0,2,3,1:T(4,128)}, u32[]{:S(2)}) copy-start(s32[8,4,4,3]{0,2,3,1:T(4,128)} %param.9) | copy-start | bytes 4612
  5.1 11.3 %copy-start.14 = (f32[48,31]{0,1:T(8,128)S(1)}, f32[48,31]{0,1:T(8,128)}, u32[]{:S(2)}) copy-start(f32[48,31]{0,1:T(8,128)} %param.8) | copy-start | bytes 17860
  6.9 19.9 %copy-start.13 = (s32[4096]{0:T(1024)S(1)}, s32[4096]{0:T(1024)}, u32[]{:S(2)}) copy-start(s32[4096]{0:T(1024)} %param.7) | copy-start | bytes 49156
  6.9 31.9 %all-to-all-start = ((bf16[32,8,2048]{2,1,0:T(8,128)(2,1)}), bf16[32,8,2048]{2,1,0:T(8,128)(2,1)S(1)}, u32[]{:S(2)}, u32[]{:S(2)}) async-start(bf16[32,8,2048]{2,1,0:T(8,128)(2,1)} %bitcast.4), calls=%async_computation | async-start | bytes 2097152 | tf_op jit(solution)/shard_map/all_to_all | solution.py:612
  13.8 19.3 %collective-permute-start.3 = (f16[640,128]{1,0:T(8,128)(2,1)S(1)}, f16[640,128]{1,0:T(8,128)(2,1)S(1)}, u32[]{:S(2)}, u32[]{:S(2)}) collective-permute-start(f16[640,128]{1,0:T(8,128)(2,1)S(1)} %convert_element_type.48), channel_id=1, source_target_pairs={{0,1},{1,0},{2,3},{3,2},{4,8},{5,9},{6,10},{7,11},{8,4},{9,5},{10,... | collective-permute-start | bytes 491528 | tf_op jit(solution)/shard_map/ppermute | solution.py:535
  15.6 14.2 %collective-permute-start.2 = (f16[640,128]{1,0:T(8,128)(2,1)S(1)}, f16[640,128]{1,0:T(8,128)(2,1)S(1)}, u32[]{:S(2)}, u32[]{:S(2)}) collective-permute-start(f16[640,128]{1,0:T(8,128)(2,1)S(1)} %convert_element_type.48), channel_id=1, source_target_pairs={{0,4},{1,5},{2,6},{3,7},{4,0},{5,1},{6,2},{7,3},{8,12},{9,13},{10,... | collective-permute-start | bytes 491528 | tf_op jit(solution)/shard_map/ppermute | solution.py:531
  38.8 8.2 %copy-start.1 = (bf16[4,512,512]{2,1,0:T(8,128)(2,1)S(1)}, bf16[4,512,512]{2,1,0:T(8,128)(2,1)}, u32[]{:S(2)}) copy-start(bf16[4,512,512]{2,1,0:T(8,128)(2,1)} %get-tuple-element.123.k_ref) | copy-start | bytes 6291460
  38.8 8.2 %copy-start.4 = (bf16[2,4,256,256]{3,2,1,0:T(8,128)(2,1)S(1)}, bf16[2,4,256,256]{3,2,1,0:T(8,128)(2,1)}, u32[]{:S(2)}) copy-start(bf16[2,4,256,256]{3,2,1,0:T(8,128)(2,1)} %get-tuple-element.125.xy_ref) | copy-start | bytes 3145732
  38.8 8.2 %copy-start.7 = (bf16[4,256,256]{2,1,0:T(8,128)(2,1)S(1)}, bf16[4,256,256]{2,1,0:T(8,128)(2,1)}, u32[]{:S(2)}) copy-start(bf16[4,256,256]{2,1,0:T(8,128)(2,1)} %get-tuple-element.124.y_ref) | copy-start | bytes 1572868
  38.8 8.2 %copy-start.10 = (bf16[2,32,512]{2,1,0:T(8,128)(2,1)S(1)}, bf16[2,32,512]{2,1,0:T(8,128)(2,1)}, u32[]{:S(2)}) copy-start(bf16[2,32,512]{2,1,0:T(8,128)(2,1)} %get-tuple-element.126.z_ref) | copy-start | bytes 196612
  43.8 6.8 %collective-permute-start.5 = (f16[656,128]{1,0:T(8,128)(2,1)S(1)}, f16[656,128]{1,0:T(8,128)(2,1)S(1)}, u32[]{:S(2)}, u32[]{:S(2)}) collective-permute-start(f16[656,128]{1,0:T(8,128)(2,1)S(1)} %convert_element_type.53), channel_id=1, source_target_pairs={{0,1},{1,0},{2,3},{3,2},{4,8},{5,9},{6,10},{7,11},{8,4},{9,5},{10,... | collective-permute-start | bytes 503816 | tf_op jit(solution)/shard_map/ppermute | solution.py:535
  47.0 1.9 %copy-start = (bf16[4,512,512]{2,1,0:T(8,128)(2,1)S(1)}, bf16[4,512,512]{2,1,0:T(8,128)(2,1)}, u32[]{:S(2)}) copy-start(bf16[4,512,512]{2,1,0:T(8,128)(2,1)} %get-tuple-element.117.k_ref) | copy-start | bytes 6291460
  47.0 1.9 %copy-start.3 = (bf16[2,4,256,256]{3,2,1,0:T(8,128)(2,1)S(1)}, bf16[2,4,256,256]{3,2,1,0:T(8,128)(2,1)}, u32[]{:S(2)}) copy-start(bf16[2,4,256,256]{3,2,1,0:T(8,128)(2,1)} %get-tuple-element.119.xy_ref) | copy-start | bytes 3145732
  47.0 2.0 %copy-start.6 = (bf16[4,256,256]{2,1,0:T(8,128)(2,1)S(1)}, bf16[4,256,256]{2,1,0:T(8,128)(2,1)}, u32[]{:S(2)}) copy-start(bf16[4,256,256]{2,1,0:T(8,128)(2,1)} %get-tuple-element.118.y_ref) | copy-start | bytes 1572868
  47.0 2.0 %copy-start.9 = (bf16[2,32,512]{2,1,0:T(8,128)(2,1)S(1)}, bf16[2,32,512]{2,1,0:T(8,128)(2,1)}, u32[]{:S(2)}) copy-start(bf16[2,32,512]{2,1,0:T(8,128)(2,1)} %get-tuple-element.120.z_ref) | copy-start | bytes 196612
  48.8 1.8 %collective-permute-start.4 = (f16[656,128]{1,0:T(8,128)(2,1)S(1)}, f16[656,128]{1,0:T(8,128)(2,1)S(1)}, u32[]{:S(2)}, u32[]{:S(2)}) collective-permute-start(f16[656,128]{1,0:T(8,128)(2,1)S(1)} %convert_element_type.51), channel_id=1, source_target_pairs={{0,4},{1,5},{2,6},{3,7},{4,0},{5,1},{6,2},{7,3},{8,12},{9,13},{10,... | collective-permute-start | bytes 503816 | tf_op jit(solution)/shard_map/ppermute | solution.py:531
  51.5 4.7 %collective-permute-start.6 = (f32[128,128]{1,0:T(8,128)S(1)}, f32[128,128]{1,0:T(8,128)S(1)}, u32[]{:S(2)}, u32[]{:S(2)}) collective-permute-start(f32[128,128]{1,0:T(8,128)S(1)} %get-tuple-element.146.up_ref), channel_id=1, source_target_pairs={{0,1},{1,0},{2,3},{3,2},{4,5},{5,4},{6,7},{7,6},{8,9},{9,8},{10,11... | collective-permute-start | bytes 196616 | tf_op jit(solution)/shard_map/ppermute | solution.py:531
  53.3 2.9 %collective-permute-start.7 = (f32[128,128]{1,0:T(8,128)S(1)}, f32[128,128]{1,0:T(8,128)S(1)}, u32[]{:S(2)}, u32[]{:S(2)}) collective-permute-start(f32[128,128]{1,0:T(8,128)S(1)} %get-tuple-element.147.down_ref), channel_id=1, source_target_pairs={{0,4},{1,2},{2,1},{3,7},{4,0},{5,6},{6,5},{7,3},{8,12},{9,10},{10,... | collective-permute-start | bytes 196616 | tf_op jit(solution)/shard_map/ppermute | solution.py:535
  57.1 3.9 %collective-permute-start.8 = (f16[656,128]{1,0:T(8,128)(2,1)S(1)}, f16[656,128]{1,0:T(8,128)(2,1)S(1)}, u32[]{:S(2)}, u32[]{:S(2)}) collective-permute-start(f16[656,128]{1,0:T(8,128)(2,1)S(1)} %convert_element_type.55), channel_id=1, source_target_pairs={{0,4},{1,5},{2,6},{3,7},{4,0},{5,1},{6,2},{7,3},{8,12},{9,13},{10,... | collective-permute-start | bytes 503816 | tf_op jit(solution)/shard_map/ppermute | solution.py:531
  57.3 5.8 %collective-permute-start.9 = (f16[656,128]{1,0:T(8,128)(2,1)S(1)}, f16[656,128]{1,0:T(8,128)(2,1)S(1)}, u32[]{:S(2)}, u32[]{:S(2)}) collective-permute-start(f16[656,128]{1,0:T(8,128)(2,1)S(1)} %convert_element_type.55), channel_id=1, source_target_pairs={{0,1},{1,0},{2,3},{3,2},{4,8},{5,9},{6,10},{7,11},{8,4},{9,5},{10,... | collective-permute-start | bytes 503816 | tf_op jit(solution)/shard_map/ppermute | solution.py:535
  61.0 2.2 %copy-start.2 = (bf16[4,512,512]{2,1,0:T(8,128)(2,1)S(1)}, bf16[4,512,512]{2,1,0:T(8,128)(2,1)}, u32[]{:S(2)}) copy-start(bf16[4,512,512]{2,1,0:T(8,128)(2,1)} %get-tuple-element.111.refs_2_.ka_ref) | copy-start | bytes 6291460
  61.0 2.2 %copy-start.5 = (bf16[2,4,256,256]{3,2,1,0:T(8,128)(2,1)S(1)}, bf16[2,4,256,256]{3,2,1,0:T(8,128)(2,1)}, u32[]{:S(2)}) copy-start(bf16[2,4,256,256]{3,2,1,0:T(8,128)(2,1)} %get-tuple-element.113.refs_4_.xya_ref) | copy-start | bytes 3145732
  61.0 2.2 %copy-start.8 = (bf16[4,256,256]{2,1,0:T(8,128)(2,1)S(1)}, bf16[4,256,256]{2,1,0:T(8,128)(2,1)}, u32[]{:S(2)}) copy-start(bf16[4,256,256]{2,1,0:T(8,128)(2,1)} %get-tuple-element.112.refs_3_.ya_ref) | copy-start | bytes 1572868
  61.0 2.2 %copy-start.11 = (bf16[2,32,512]{2,1,0:T(8,128)(2,1)S(1)}, bf16[2,32,512]{2,1,0:T(8,128)(2,1)}, u32[]{:S(2)}) copy-start(bf16[2,32,512]{2,1,0:T(8,128)(2,1)} %get-tuple-element.114.refs_5_.za_ref) | copy-start | bytes 196612
  67.0 5.6 %collective-permute-start.11 = (f16[656,128]{1,0:T(8,128)(2,1)S(1)}, f16[656,128]{1,0:T(8,128)(2,1)S(1)}, u32[]{:S(2)}, u32[]{:S(2)}) collective-permute-start(f16[656,128]{1,0:T(8,128)(2,1)S(1)} %convert_element_type.60), channel_id=1, source_target_pairs={{0,1},{1,0},{2,3},{3,2},{4,8},{5,9},{6,10},{7,11},{8,4},{9,5},{10,... | collective-permute-start | bytes 503816 | tf_op jit(solution)/shard_map/ppermute | solution.py:535
  70.3 2.5 %collective-permute-start.10 = (f16[656,128]{1,0:T(8,128)(2,1)S(1)}, f16[656,128]{1,0:T(8,128)(2,1)S(1)}, u32[]{:S(2)}, u32[]{:S(2)}) collective-permute-start(f16[656,128]{1,0:T(8,128)(2,1)S(1)} %convert_element_type.58), channel_id=1, source_target_pairs={{0,4},{1,5},{2,6},{3,7},{4,0},{5,1},{6,2},{7,3},{8,12},{9,13},{10,... | collective-permute-start | bytes 503816 | tf_op jit(solution)/shard_map/ppermute | solution.py:531
  72.9 4.2 %collective-permute-start.12 = (f32[64,128]{1,0:T(8,128)S(1)}, f32[64,128]{1,0:T(8,128)S(1)}, u32[]{:S(2)}, u32[]{:S(2)}) collective-permute-start(f32[64,128]{1,0:T(8,128)S(1)} %get-tuple-element.169), channel_id=1, source_target_pairs={{0,1},{1,0},{2,3},{3,2},{4,5},{5,4},{6,7},{7,6},{8,9},{9,8},{10,11... | collective-permute-start | bytes 98312 | tf_op jit(solution)/shard_map/ppermute | solution.py:531
  74.1 2.9 %collective-permute-start.13 = (f32[64,128]{1,0:T(8,128)S(1)}, f32[64,128]{1,0:T(8,128)S(1)}, u32[]{:S(2)}, u32[]{:S(2)}) collective-permute-start(f32[64,128]{1,0:T(8,128)S(1)} %get-tuple-element.170), channel_id=1, source_target_pairs={{0,4},{1,2},{2,1},{3,7},{4,0},{5,6},{6,5},{7,3},{8,12},{9,10},{10,... | collective-permute-start | bytes 98312 | tf_op jit(solution)/shard_map/ppermute | solution.py:535

commit v4 on v3

--- a/solution.py
+++ b/solution.py
@@ -606,8 +606,8 @@
         functools.partial(route_kernel, cap), [((rows, plane), bf16)], me.reshape(1), slots_near, stored_near,
         scalars=1, scratch=[pltpu.VMEM((slots * BX, BY), f32)],
     )
-    outgoing, up_in, down_in, psf_taps, kernel_index, slots_of = lax.optimization_barrier(
-        (outgoing, up_in, down_in, psf_taps, kernel_index, slots_of)
+    outgoing, psf_taps, kernel_index, slots_of = lax.optimization_barrier(
+        (outgoing, psf_taps, kernel_index, slots_of)
     )
     arrived = lax.all_to_all(
         outgoing.reshape(devices, cap, plane), ("gx", "gy"), split_axis=0, concat_axis=0, tiled=True

time: 79.8 us -> 78 us (0.977)
  starting transfers between devices: 21.8 us -> 20.4 us
    all_to_all x1, starting transfers between devices: 6.85 us -> 5.4 us  [shards(): lax.all_to_all(outgoing.reshape(devices, cap, plane), ('gx', 'gy'), split...]
  transfers between devices with their start and end apart: 15 -> 15, of which waited for: 6 -> 5; matrix products, arithmetic and copies ran while one was open for 2% -> 2% of each run, Pallas kernels for 41% -> 42%
where the time goes in v4:
time: 78 us; the launch traced here: 76.9 us
  Pallas kernels  46.3 us (59%)
  starting transfers between devices  20.4 us (26%)
  waiting for transfers between devices  7.48 us (10%)
  local copies, waits for them, and re-layouts  1.06 us (1%)
  other arithmetic  0.8 us (1%)
    pallas_call x21, Pallas kernels, call(): pl.pallas_call(kernel, out_shape=[HBM(s, d) if where is HBM else jax.Shap...  46.3 us
    ppermute x7, starting transfers between devices, swap_far(): lax.ppermute(narrow(axis, value), ('gx', 'gy'), partner_swaps(axis)[1])  8.35 us
    ppermute x7, starting transfers between devices, swap_near(): lax.ppermute(narrow(axis, value), ('gx', 'gy'), partner_swaps(axis)[0])  6.62 us
    all_to_all x1, starting transfers between devices, shards(): lax.all_to_all(outgoing.reshape(devices, cap, plane), ('gx', 'gy'), split...  5.4 us
    ppermute x7, waiting for transfers between devices, swap_near(): lax.ppermute(narrow(axis, value), ('gx', 'gy'), partner_swaps(axis)[0])  2.96 us
    all_to_all x1, waiting for transfers between devices, shards(): lax.all_to_all(outgoing.reshape(devices, cap, plane), ('gx', 'gy'), split...  2.61 us
    ppermute x7, waiting for transfers between devices, swap_far(): lax.ppermute(narrow(axis, value), ('gx', 'gy'), partner_swaps(axis)[1])  1.9 us
  transfers between devices with their start and end apart: 15, of which 5 were waited for; matrix products, arithmetic and copies ran while one was open for 2% of the time, Pallas kernels for 42%

profile of v4, /device:TPU:0, one launch (start us, length us, event | category | flops | bytes accessed | tf_op | source)
XLA Modules:
  0.0 76.9 jit_solution(12364184518087657353)
XLA Ops:
  0.1 1.8 %shard_map.55 = (f32[512,128]{1,0:T(8,128)S(1)}, f32[64,128]{1,0:T(8,128)S(1)}, f32[64,128]{1,0:T(8,128)S(1)}, s32[32,128]{1,0:T(8,128)S(1)}, bf16[128,16,128]{2,1,0:T(8,128)(2,1)S(1)}) custom-call(s32[2]{0:T(128)S(1)} %pad_add_fusion.info_ref, f32[32,16,128]{2,1,0:T(8,128)} %refs_0_.1, s32[32,128]{1,0:T(8,128)} %bitcast.9, bf16[128,16,128]{2,1,0:T(8,128)(2,1)} %refs_2_.1), custom_call_target="tpu_custom_call" | custom-call | bytes 70000 | tf_op jit(solution)/shard_map/pallas_call | solution.py:495
  1.9 3.1 %collective-permute-start = (f32[64,128]{1,0:T(8,128)S(1)}, f32[64,128]{1,0:T(8,128)S(1)}, u32[]{:S(2)}, u32[]{:S(2)}) collective-permute-start(f32[64,128]{1,0:T(8,128)S(1)} %get-tuple-element.87), channel_id=1, source_target_pairs={{0,1},{1,0},{2,3},{3,2},{4,5},{5,4},{6,7},{7,6},{8,9},{9,8},{10,11... | collective-permute-start | bytes 98312 | tf_op jit(solution)/shard_map/ppermute | solution.py:531
  5.0 1.6 %shard_map.56 = bf16[256,2048]{1,0:T(8,128)(2,1)} custom-call(s32[1]{0:T(128)} %bitcast.3.me_ref, s32[32,128]{1,0:T(8,128)S(1)} %get-tuple-element.89.slots_ref, bf16[128,16,128]{2,1,0:T(8,128)(2,1)S(1)} %get-tuple-element.90.stored_ref), custom_call_target="tpu_custom_call" | custom-call | bytes 70000 | tf_op jit(solution)/shard_map/pallas_call | solution.py:495
  6.6 5.4 %all-to-all-start = ((bf16[32,8,2048]{2,1,0:T(8,128)(2,1)}), bf16[32,8,2048]{2,1,0:T(8,128)(2,1)S(1)}, u32[]{:S(2)}, u32[]{:S(2)}) async-start(bf16[32,8,2048]{2,1,0:T(8,128)(2,1)} %bitcast.4), calls=%async_computation | async-start | bytes 2097152 | tf_op jit(solution)/shard_map/all_to_all | solution.py:612
  13.7 2.5 %shard_map.58 = (bf16[4,512,512]{2,1,0:T(8,128)(2,1)S(1)}, bf16[384,512]{1,0:T(8,128)(2,1)S(1)}, bf16[2,4,256,256]{3,2,1,0:T(8,128)(2,1)S(1)}, bf16[2,128,128]{2...) custom-call(f32[108,128]{1,0:T(8,128)S(1)} %get-tuple-element.126.ta, ...), custom_call_target="tpu_custom_call" | custom-call | bytes 10500000 | tf_op jit(solution)/shard_map/pallas_call | solution.py:495
  16.2 7.0 %shard_map.62 = (bf16[4,512,512]{2,1,0:T(8,128)(2,1)}, bf16[4,256,256]{2,1,0:T(8,128)(2,1)}, bf16[2,4,256,256]{3,2,1,0:T(8,128)(2,1)}, bf16[2,32,512]{2,1,0:T(8,...) custom-call(f32[108,128]{1,0:T(8,128)S(1)} %get-tuple-element.126.ta, ...), custom_call_target="tpu_custom_call" | custom-call | bytes 14000000 | tf_op jit(solution)/shard_map/pallas_call | solution.py:495
  23.3 1.8 %collective-permute-start.3 = (f16[640,128]{1,0:T(8,128)(2,1)S(1)}, f16[640,128]{1,0:T(8,128)(2,1)S(1)}, u32[]{:S(2)}, u32[]{:S(2)}) collective-permute-start(f16[640,128]{1,0:T(8,128)(2,1)S(1)} %convert_element_type.48), channel_id=1, source_target_pairs={{0,1},{1,0},{2,3},{3,2},{4,8},{5,9},{6,10},{7,11},{8,4},{9,5},{10,... | collective-permute-start | bytes 491528 | tf_op jit(solution)/shard_map/ppermute | solution.py:535
  25.2 1.0 %shard_map.57.refs_0_ = bf16[128,256]{1,0:T(8,128)(2,1)} custom-call(s32[1]{0:T(128)} %bitcast.3.me_ref, s32[256,128]{1,0:T(8,128)S(1)} %broadcast_bitcast_fusion.slots_ref), custom_call_target="tpu_custom_call" | custom-call | bytes 70000 | tf_op jit(solution)/shard_map/pallas_call | solution.py:495
  26.2 2.0 %shard_map.59.refs_0_ = f32[4,512,128]{2,1,0:T(8,128)S(1)} custom-call(s32[2]{0:T(128)S(1)} %pad_add_fusion.info_ref, f32[640,128]{1,0:T(8,128)S(1)} %constant_dynamic-update-slice_fusion.refs_0_.old_ref, bf16[4,512,512]{2,1,0:T(8,128)(2,1)S(1)} %get-tuple-element.95.refs_1_, bf16[384,512]{1,0:T(8,128)(2,1)S(1)} %get-tuple-element.96.refs_2_, ...), custom_call_target="tpu_custom_call" | custom-call | bytes 70000 | tf_op jit(solution)/shard_map/pallas_call | solution.py:495
  28.3 2.0 %shard_map.60.blurred_ref = f32[4,512,128]{2,1,0:T(8,128)S(1)} custom-call(s32[2]{0:T(128)S(1)} %pad_add_fusion.info_ref, f32[4,512,128]{2,1,0:T(8,128)S(1)} %shard_map.59.refs_0_, f32[640,128]{1,0:T(8,128)S(1)} %convert_element_type.49.refs_1_, bf16[4,512,512]{2,1,0:T(8,128)(2,1)S(1)} %get-tuple-element.99.refs_2_, ...), custom_call_target="tpu_custom_call" | custom-call | bytes 70000 | tf_op jit(solution)/shard_map/pallas_call | solution.py:495
  30.3 1.1 %collective-permute-done.3 = f16[640,128]{1,0:T(8,128)(2,1)S(1)} collective-permute-done((f16[640,128]{1,0:T(8,128)(2,1)S(1)}, f16[640,128]{1,0:T(8,128)(2,1)S(1)}, u32[]{:S(2)}, u32[]{:S(2)}) %collective-permute-start.3) | collective-permute-done | bytes 163872 | tf_op jit(solution)/shard_map/ppermute | solution.py:535
  31.4 3.0 %shard_map.61.refs_1_ = f32[4,512,128]{2,1,0:T(8,128)} custom-call(s32[2]{0:T(128)S(1)} %pad_add_fusion.info_ref, f32[4,512,128]{2,1,0:T(8,128)S(1)} %shard_map.60.blurred_ref, f32[640,128]{1,0:T(8,128)S(1)} %convert_element_type.50.message_ref, bf16[4,512,512]{2,1,0:T(8,128)(2,1)S(1)} %get-tuple-element.103.k_ref, ...), custom_call_target="tpu_custom_call" | custom-call | bytes 70000 | tf_op jit(solution)/shard_map/pallas_call | solution.py:495
  34.5 2.6 %all-to-all-done = bf16[32,8,2048]{2,1,0:T(8,128)(2,1)S(1)} async-done(((bf16[32,8,2048]{2,1,0:T(8,128)(2,1)}), bf16[32,8,2048]{2,1,0:T(8,128)(2,1)S(1)}, u32[]{:S(2)}, u32[]{:S(2)}) %all-to-all-start) | async-done | bytes 1048608 | tf_op jit(solution)/shard_map/all_to_all | solution.py:612
  37.1 5.0 %shard_map.63 = (bf16[4,512,128]{2,1,0:T(8,128)(2,1)S(1)}, f32[4,512,128]{2,1,0:T(8,128)S(1)}, f32[4,2,64,128]{3,2,1,0:T(8,128)S(1)}, f32[656,128]{1,0:T(8,128)S(1)}) custom-call(s32[2]{0:T(128)S(1)} %pad_add_fusion.info_ref, bf16[256,2048]{1,0:T(8,128)(2,1)S(1)} %bitcast.8, bf16[128,256]{1,0:T(8,128)(2,1)} %shard_map.57.refs_0_, ...), custom_call_target="tpu_custom_call" | custom-call | bytes 70000 | tf_op jit(solution)/shard_map/pallas_call | solution.py:495
  42.1 3.2 %collective-permute-start.5 = (f16[656,128]{1,0:T(8,128)(2,1)S(1)}, f16[656,128]{1,0:T(8,128)(2,1)S(1)}, u32[]{:S(2)}, u32[]{:S(2)}) collective-permute-start(f16[656,128]{1,0:T(8,128)(2,1)S(1)} %convert_element_type.53), channel_id=1, source_target_pairs={{0,1},{1,0},{2,3},{3,2},{4,8},{5,9},{6,10},{7,11},{8,4},{9,5},{10,... | collective-permute-start | bytes 503816 | tf_op jit(solution)/shard_map/ppermute | solution.py:535
  45.3 1.7 %shard_map.65 = f32[656,128]{1,0:T(8,128)S(1)} custom-call(f32[4,512,128]{2,1,0:T(8,128)S(1)} %get-tuple-element.111.quotient_ref, f32[4,2,64,128]{3,2,1,0:T(8,128)S(1)} %get-tuple-element.112.edge_ref, bf16[4,512,512]{2,1,0:T(8,128)(2,1)S(1)} %copy-done.1, bf16[4,256,256]{2,1,0:T(8,128)(2,1)S(1)} %copy-done.7, bf16[2,4,256,256]{3,2,1,0:T(8,128)(2,1)S(1)} %copy-done.4, ...), custom_call_target="tpu_custom_call" | custom-call | bytes 70000 | tf_op jit(solution)/shard_map/pallas_call | solution.py:495
  47.2 1.6 %shard_map.64 = (f32[512,128]{1,0:T(8,128)S(1)}, f32[2,64,128]{2,1,0:T(8,128)S(1)}) custom-call(f32[4,512,128]{2,1,0:T(8,128)S(1)} %get-tuple-element.111.quotient_ref, f32[4,2,64,128]{3,2,1,0:T(8,128)S(1)} %get-tuple-element.112.edge_ref, bf16[4,512,512]{2,1,0:T(8,128)(2,1)S(1)} %copy-done, bf16[4,256,256]{2,1,0:T(8,128)(2,1)S(1)} %copy-done.6, ...), custom_call_target="tpu_custom_call" | custom-call | bytes 70000 | tf_op jit(solution)/shard_map/pallas_call | solution.py:495
  48.9 0.8 %shard_map.66 = (f32[512,128]{1,0:T(8,128)S(1)}, f32[128,128]{1,0:T(8,128)S(1)}, f32[128,128]{1,0:T(8,128)S(1)}) custom-call(s32[2]{0:T(128)S(1)} %pad_add_fusion.info_ref, f32[512,128]{1,0:T(8,128)S(1)} %get-tuple-element.117.field_ref, f32[2,64,128]{2,1,0:T(8,128)S(1)} %get-tuple-element.118.strips_ref, f32[656,128]{1,0:T(8,128)S(1)} %convert_element_type.52.near_ref, ...), custom_call_target="tpu_custom_call" | custom-call | bytes 70000 | tf_op jit(solution)/shard_map/pallas_call | solution.py:495
  49.8 1.8 %collective-permute-start.6 = (f32[128,128]{1,0:T(8,128)S(1)}, f32[128,128]{1,0:T(8,128)S(1)}, u32[]{:S(2)}, u32[]{:S(2)}) collective-permute-start(f32[128,128]{1,0:T(8,128)S(1)} %get-tuple-element.142.up_ref), channel_id=1, source_target_pairs={{0,1},{1,0},{2,3},{3,2},{4,5},{5,4},{6,7},{7,6},{8,9},{9,8},{10,11... | collective-permute-start | bytes 196616 | tf_op jit(solution)/shard_map/ppermute | solution.py:531
  51.6 2.5 %shard_map.67 = (bf16[4,512,512]{2,1,0:T(8,128)(2,1)S(1)}, bf16[384,512]{1,0:T(8,128)(2,1)S(1)}, bf16[2,4,256,256]{3,2,1,0:T(8,128)(2,1)S(1)}, bf16[2,128,128]{2...) custom-call(f32[108,128]{1,0:T(8,128)S(1)} %get-tuple-element.126.ta, ...), custom_call_target="tpu_custom_call" | custom-call | bytes 70000 | tf_op jit(solution)/shard_map/pallas_call | solution.py:495
  54.4 0.9 %shard_map.68 = (f32[640,128]{1,0:T(8,128)S(1)}, f32[656,128]{1,0:T(8,128)S(1)}) custom-call(s32[2]{0:T(128)S(1)} %pad_add_fusion.info_ref, f32[640,128]{1,0:T(8,128)S(1)} %constant_dynamic-update-slice_fusion.refs_0_.old_ref, f32[512,128]{1,0:T(8,128)S(1)} %get-tuple-element.141.total_ref, f32[128,128]{1,0:T(8,128)S(1)} %get-tuple-element.142.up_ref, ...), custom_call_target="tpu_custom_call" | custom-call | bytes 70000 | tf_op jit(solution)/shard_map/pallas_call | solution.py:495
  55.6 1.6 %collective-permute-start.9 = (f16[656,128]{1,0:T(8,128)(2,1)S(1)}, f16[656,128]{1,0:T(8,128)(2,1)S(1)}, u32[]{:S(2)}, u32[]{:S(2)}) collective-permute-start(f16[656,128]{1,0:T(8,128)(2,1)S(1)} %convert_element_type.55), channel_id=1, source_target_pairs={{0,1},{1,0},{2,3},{3,2},{4,8},{5,9},{6,10},{7,11},{8,4},{9,5},{10,... | collective-permute-start | bytes 503816 | tf_op jit(solution)/shard_map/ppermute | solution.py:535
  57.2 2.0 %shard_map.69.blurred_ref = f32[4,512,128]{2,1,0:T(8,128)S(1)} custom-call(s32[2]{0:T(128)S(1)} %pad_add_fusion.info_ref, f32[640,128]{1,0:T(8,128)S(1)} %get-tuple-element.144.own_ref.old_ref, bf16[4,512,512]{2,1,0:T(8,128)(2,1)S(1)} %get-tuple-element.146.k_ref, bf16[384,512]{1,0:T(8,128)(2,1)S(1)} %get-tuple-element.147.y_ref, ...), custom_call_target="tpu_custom_call" | custom-call | bytes 70000 | tf_op jit(solution)/shard_map/pallas_call | solution.py:495
  59.3 2.1 %shard_map.70.blurred_ref = f32[4,512,128]{2,1,0:T(8,128)S(1)} custom-call(s32[2]{0:T(128)S(1)} %pad_add_fusion.info_ref, f32[4,512,128]{2,1,0:T(8,128)S(1)} %shard_map.69.blurred_ref, f32[656,128]{1,0:T(8,128)S(1)} %convert_element_type.56.near_ref, bf16[4,512,512]{2,1,0:T(8,128)(2,1)S(1)} %get-tuple-element.151.k_ref, ...), custom_call_target="tpu_custom_call" | custom-call | bytes 70000 | tf_op jit(solution)/shard_map/pallas_call | solution.py:495
  61.5 3.8 %shard_map.71 = (f32[4,512,128]{2,1,0:T(8,128)S(1)}, f32[4,2,64,128]{3,2,1,0:T(8,128)S(1)}, f32[656,128]{1,0:T(8,128)S(1)}) custom-call(s32[2]{0:T(128)S(1)} %pad_add_fusion.info_ref, bf16[4,512,128]{2,1,0:T(8,128)(2,1)S(1)} %get-tuple-element.145.data_ref, f32[4,512,128]{2,1,0:T(8,128)S(1)} %shard_map.70.blurred_ref, ...), custom_call_target="tpu_custom_call" | custom-call | bytes 70000 | tf_op jit(solution)/shard_map/pallas_call | solution.py:495
  65.3 1.4 %collective-permute-start.11 = (f16[656,128]{1,0:T(8,128)(2,1)S(1)}, f16[656,128]{1,0:T(8,128)(2,1)S(1)}, u32[]{:S(2)}, u32[]{:S(2)}) collective-permute-start(f16[656,128]{1,0:T(8,128)(2,1)S(1)} %convert_element_type.60), channel_id=1, source_target_pairs={{0,1},{1,0},{2,3},{3,2},{4,8},{5,9},{6,10},{7,11},{8,4},{9,5},{10,... | collective-permute-start | bytes 503816 | tf_op jit(solution)/shard_map/ppermute | solution.py:535
  66.8 1.7 %shard_map.73 = f32[656,128]{1,0:T(8,128)S(1)} custom-call(f32[4,512,128]{2,1,0:T(8,128)S(1)} %get-tuple-element.159.quotient_ref, f32[4,2,64,128]{3,2,1,0:T(8,128)S(1)} %get-tuple-element.160.edge_ref, bf16[4,512,512]{2,1,0:T(8,128)(2,1)S(1)} %copy-done.1, bf16[4,256,256]{2,1,0:T(8,128)(2,1)S(1)} %copy-done.7, bf16[2,4,256,256]{3,2,1,0:T(8,128)(2,1)S(1)} %copy-done.4, ...), custom_call_target="tpu_custom_call" | custom-call | bytes 70000 | tf_op jit(solution)/shard_map/pallas_call | solution.py:495
  68.6 1.6 %shard_map.72 = (f32[512,128]{1,0:T(8,128)S(1)}, f32[2,64,128]{2,1,0:T(8,128)S(1)}) custom-call(f32[4,512,128]{2,1,0:T(8,128)S(1)} %get-tuple-element.159.quotient_ref, f32[4,2,64,128]{3,2,1,0:T(8,128)S(1)} %get-tuple-element.160.edge_ref, bf16[4,512,512]{2,1,0:T(8,128)(2,1)S(1)} %copy-done, bf16[4,256,256]{2,1,0:T(8,128)(2,1)S(1)} %copy-done.6, ...), custom_call_target="tpu_custom_call" | custom-call | bytes 70000 | tf_op jit(solution)/shard_map/pallas_call | solution.py:495
  70.2 0.8 %collective-permute-done.11 = f16[656,128]{1,0:T(8,128)(2,1)S(1)} collective-permute-done((f16[656,128]{1,0:T(8,128)(2,1)S(1)}, f16[656,128]{1,0:T(8,128)(2,1)S(1)}, u32[]{:S(2)}, u32[]{:S(2)}) %collective-permute-start.11) | collective-permute-done | bytes 167968 | tf_op jit(solution)/shard_map/ppermute | solution.py:535
  71.2 1.2 %collective-permute-start.12 = (f32[64,128]{1,0:T(8,128)S(1)}, f32[64,128]{1,0:T(8,128)S(1)}, u32[]{:S(2)}, u32[]{:S(2)}) collective-permute-start(f32[64,128]{1,0:T(8,128)S(1)} %get-tuple-element.165), channel_id=1, source_target_pairs={{0,1},{1,0},{2,3},{3,2},{4,5},{5,4},{6,7},{7,6},{8,9},{9,8},{10,11... | collective-permute-start | bytes 98312 | tf_op jit(solution)/shard_map/ppermute | solution.py:531
  72.7 2.6 %collective-permute-done.12.up_in_ref = f32[64,128]{1,0:T(8,128)S(1)} collective-permute-done((f32[64,128]{1,0:T(8,128)S(1)}, f32[64,128]{1,0:T(8,128)S(1)}, u32[]{:S(2)}, u32[]{:S(2)}) %collective-permute-start.12) | collective-permute-done | bytes 32800 | tf_op jit(solution)/shard_map/ppermute | solution.py:531
  75.3 1.6 %shard_map.75 = f32[32,16,128]{2,1,0:T(8,128)} custom-call(s32[2]{0:T(128)S(1)} %pad_add_fusion.info_ref, f32[640,128]{1,0:T(8,128)S(1)} %get-tuple-element.144.own_ref.old_ref, f32[512,128]{1,0:T(8,128)S(1)} %get-tuple-element.164.total_ref, f32[64,128]{1,0:T(8,128)S(1)} %collective-permute-done.12.up_in_ref, f32[64,128]{1,0:T(8,128)S(1)} %collective-permute-done.13.down_in_ref), custom_call_target="tpu_custom_call" | custom-call | bytes 70000 | tf_op jit(solution)/shard_map/pallas_call | solution.py:495
  (86 shorter events, 3.4 us)
Async XLA Ops:
  0.1 12.0 %copy-start.12 = (s32[8,4,4,3]{0,2,3,1:T(4,128)S(1)}, s32[8,4,4,3]{0,2,3,1:T(4,128)}, u32[]{:S(2)}) copy-start(s32[8,4,4,3]{0,2,3,1:T(4,128)} %param.9) | copy-start | bytes 4612
  1.9 10.8 %copy-start.14 = (f32[48,31]{0,1:T(8,128)S(1)}, f32[48,31]{0,1:T(8,128)}, u32[]{:S(2)}) copy-start(f32[48,31]{0,1:T(8,128)} %param.8) | copy-start | bytes 17860
  1.9 21.3 %collective-permute-start = (f32[64,128]{1,0:T(8,128)S(1)}, f32[64,128]{1,0:T(8,128)S(1)}, u32[]{:S(2)}, u32[]{:S(2)}) collective-permute-start(f32[64,128]{1,0:T(8,128)S(1)} %get-tuple-element.87), channel_id=1, source_target_pairs={{0,1},{1,0},{2,3},{3,2},{4,5},{5,4},{6,7},{7,6},{8,9},{9,8},{10,11... | collective-permute-start | bytes 98312 | tf_op jit(solution)/shard_map/ppermute | solution.py:531
  5.0 18.2 %collective-permute-start.1 = (f32[64,128]{1,0:T(8,128)S(1)}, f32[64,128]{1,0:T(8,128)S(1)}, u32[]{:S(2)}, u32[]{:S(2)}) collective-permute-start(f32[64,128]{1,0:T(8,128)S(1)} %get-tuple-element.88), channel_id=1, source_target_pairs={{0,4},{1,2},{2,1},{3,7},{4,0},{5,6},{6,5},{7,3},{8,12},{9,10},{10,... | collective-permute-start | bytes 98312 | tf_op jit(solution)/shard_map/ppermute | solution.py:535
  6.6 30.5 %all-to-all-start = ((bf16[32,8,2048]{2,1,0:T(8,128)(2,1)}), bf16[32,8,2048]{2,1,0:T(8,128)(2,1)S(1)}, u32[]{:S(2)}, u32[]{:S(2)}) async-start(bf16[32,8,2048]{2,1,0:T(8,128)(2,1)} %bitcast.4), calls=%async_computation | async-start | bytes 2097152 | tf_op jit(solution)/shard_map/all_to_all | solution.py:612
  12.0 13.2 %copy-start.13 = (s32[4096]{0:T(1024)S(1)}, s32[4096]{0:T(1024)}, u32[]{:S(2)}) copy-start(s32[4096]{0:T(1024)} %param.7) | copy-start | bytes 49156
  23.3 8.1 %collective-permute-start.3 = (f16[640,128]{1,0:T(8,128)(2,1)S(1)}, f16[640,128]{1,0:T(8,128)(2,1)S(1)}, u32[]{:S(2)}, u32[]{:S(2)}) collective-permute-start(f16[640,128]{1,0:T(8,128)(2,1)S(1)} %convert_element_type.48), channel_id=1, source_target_pairs={{0,1},{1,0},{2,3},{3,2},{4,8},{5,9},{6,10},{7,11},{8,4},{9,5},{10,... | collective-permute-start | bytes 491528 | tf_op jit(solution)/shard_map/ppermute | solution.py:535
  25.1 3.1 %collective-permute-start.2 = (f16[640,128]{1,0:T(8,128)(2,1)S(1)}, f16[640,128]{1,0:T(8,128)(2,1)S(1)}, u32[]{:S(2)}, u32[]{:S(2)}) collective-permute-start(f16[640,128]{1,0:T(8,128)(2,1)S(1)} %convert_element_type.48), channel_id=1, source_target_pairs={{0,4},{1,5},{2,6},{3,7},{4,0},{5,1},{6,2},{7,3},{8,12},{9,13},{10,... | collective-permute-start | bytes 491528 | tf_op jit(solution)/shard_map/ppermute | solution.py:531
  37.1 8.2 %copy-start.1 = (bf16[4,512,512]{2,1,0:T(8,128)(2,1)S(1)}, bf16[4,512,512]{2,1,0:T(8,128)(2,1)}, u32[]{:S(2)}) copy-start(bf16[4,512,512]{2,1,0:T(8,128)(2,1)} %get-tuple-element.119.k_ref) | copy-start | bytes 6291460
  37.1 8.2 %copy-start.4 = (bf16[2,4,256,256]{3,2,1,0:T(8,128)(2,1)S(1)}, bf16[2,4,256,256]{3,2,1,0:T(8,128)(2,1)}, u32[]{:S(2)}) copy-start(bf16[2,4,256,256]{3,2,1,0:T(8,128)(2,1)} %get-tuple-element.121.xy_ref) | copy-start | bytes 3145732
  37.1 8.2 %copy-start.7 = (bf16[4,256,256]{2,1,0:T(8,128)(2,1)S(1)}, bf16[4,256,256]{2,1,0:T(8,128)(2,1)}, u32[]{:S(2)}) copy-start(bf16[4,256,256]{2,1,0:T(8,128)(2,1)} %get-tuple-element.120.y_ref) | copy-start | bytes 1572868
  37.1 8.2 %copy-start.10 = (bf16[2,32,512]{2,1,0:T(8,128)(2,1)S(1)}, bf16[2,32,512]{2,1,0:T(8,128)(2,1)}, u32[]{:S(2)}) copy-start(bf16[2,32,512]{2,1,0:T(8,128)(2,1)} %get-tuple-element.122.z_ref) | copy-start | bytes 196612
  42.1 6.8 %collective-permute-start.5 = (f16[656,128]{1,0:T(8,128)(2,1)S(1)}, f16[656,128]{1,0:T(8,128)(2,1)S(1)}, u32[]{:S(2)}, u32[]{:S(2)}) collective-permute-start(f16[656,128]{1,0:T(8,128)(2,1)S(1)} %convert_element_type.53), channel_id=1, source_target_pairs={{0,1},{1,0},{2,3},{3,2},{4,8},{5,9},{6,10},{7,11},{8,4},{9,5},{10,... | collective-permute-start | bytes 503816 | tf_op jit(solution)/shard_map/ppermute | solution.py:535
  45.3 1.9 %copy-start = (bf16[4,512,512]{2,1,0:T(8,128)(2,1)S(1)}, bf16[4,512,512]{2,1,0:T(8,128)(2,1)}, u32[]{:S(2)}) copy-start(bf16[4,512,512]{2,1,0:T(8,128)(2,1)} %get-tuple-element.113.k_ref) | copy-start | bytes 6291460
  45.3 1.9 %copy-start.3 = (bf16[2,4,256,256]{3,2,1,0:T(8,128)(2,1)S(1)}, bf16[2,4,256,256]{3,2,1,0:T(8,128)(2,1)}, u32[]{:S(2)}) copy-start(bf16[2,4,256,256]{3,2,1,0:T(8,128)(2,1)} %get-tuple-element.115.xy_ref) | copy-start | bytes 3145732
  45.3 2.0 %copy-start.6 = (bf16[4,256,256]{2,1,0:T(8,128)(2,1)S(1)}, bf16[4,256,256]{2,1,0:T(8,128)(2,1)}, u32[]{:S(2)}) copy-start(bf16[4,256,256]{2,1,0:T(8,128)(2,1)} %get-tuple-element.114.y_ref) | copy-start | bytes 1572868
  45.3 2.0 %copy-start.9 = (bf16[2,32,512]{2,1,0:T(8,128)(2,1)S(1)}, bf16[2,32,512]{2,1,0:T(8,128)(2,1)}, u32[]{:S(2)}) copy-start(bf16[2,32,512]{2,1,0:T(8,128)(2,1)} %get-tuple-element.116.z_ref) | copy-start | bytes 196612
  47.1 1.8 %collective-permute-start.4 = (f16[656,128]{1,0:T(8,128)(2,1)S(1)}, f16[656,128]{1,0:T(8,128)(2,1)S(1)}, u32[]{:S(2)}, u32[]{:S(2)}) collective-permute-start(f16[656,128]{1,0:T(8,128)(2,1)S(1)} %convert_element_type.51), channel_id=1, source_target_pairs={{0,4},{1,5},{2,6},{3,7},{4,0},{5,1},{6,2},{7,3},{8,12},{9,13},{10,... | collective-permute-start | bytes 503816 | tf_op jit(solution)/shard_map/ppermute | solution.py:531
  49.8 4.7 %collective-permute-start.6 = (f32[128,128]{1,0:T(8,128)S(1)}, f32[128,128]{1,0:T(8,128)S(1)}, u32[]{:S(2)}, u32[]{:S(2)}) collective-permute-start(f32[128,128]{1,0:T(8,128)S(1)} %get-tuple-element.142.up_ref), channel_id=1, source_target_pairs={{0,1},{1,0},{2,3},{3,2},{4,5},{5,4},{6,7},{7,6},{8,9},{9,8},{10,11... | collective-permute-start | bytes 196616 | tf_op jit(solution)/shard_map/ppermute | solution.py:531
  51.6 2.9 %collective-permute-start.7 = (f32[128,128]{1,0:T(8,128)S(1)}, f32[128,128]{1,0:T(8,128)S(1)}, u32[]{:S(2)}, u32[]{:S(2)}) collective-permute-start(f32[128,128]{1,0:T(8,128)S(1)} %get-tuple-element.143.down_ref), channel_id=1, source_target_pairs={{0,4},{1,2},{2,1},{3,7},{4,0},{5,6},{6,5},{7,3},{8,12},{9,10},{10,... | collective-permute-start | bytes 196616 | tf_op jit(solution)/shard_map/ppermute | solution.py:535
  55.3 3.9 %collective-permute-start.8 = (f16[656,128]{1,0:T(8,128)(2,1)S(1)}, f16[656,128]{1,0:T(8,128)(2,1)S(1)}, u32[]{:S(2)}, u32[]{:S(2)}) collective-permute-start(f16[656,128]{1,0:T(8,128)(2,1)S(1)} %convert_element_type.55), channel_id=1, source_target_pairs={{0,4},{1,5},{2,6},{3,7},{4,0},{5,1},{6,2},{7,3},{8,12},{9,13},{10,... | collective-permute-start | bytes 503816 | tf_op jit(solution)/shard_map/ppermute | solution.py:531
  55.6 5.8 %collective-permute-start.9 = (f16[656,128]{1,0:T(8,128)(2,1)S(1)}, f16[656,128]{1,0:T(8,128)(2,1)S(1)}, u32[]{:S(2)}, u32[]{:S(2)}) collective-permute-start(f16[656,128]{1,0:T(8,128)(2,1)S(1)} %convert_element_type.55), channel_id=1, source_target_pairs={{0,1},{1,0},{2,3},{3,2},{4,8},{5,9},{6,10},{7,11},{8,4},{9,5},{10,... | collective-permute-start | bytes 503816 | tf_op jit(solution)/shard_map/ppermute | solution.py:535
  59.3 2.2 %copy-start.2 = (bf16[4,512,512]{2,1,0:T(8,128)(2,1)S(1)}, bf16[4,512,512]{2,1,0:T(8,128)(2,1)}, u32[]{:S(2)}) copy-start(bf16[4,512,512]{2,1,0:T(8,128)(2,1)} %get-tuple-element.107.refs_2_.ka_ref) | copy-start | bytes 6291460
  59.3 2.2 %copy-start.5 = (bf16[2,4,256,256]{3,2,1,0:T(8,128)(2,1)S(1)}, bf16[2,4,256,256]{3,2,1,0:T(8,128)(2,1)}, u32[]{:S(2)}) copy-start(bf16[2,4,256,256]{3,2,1,0:T(8,128)(2,1)} %get-tuple-element.109.refs_4_.xya_ref) | copy-start | bytes 3145732
  59.3 2.2 %copy-start.8 = (bf16[4,256,256]{2,1,0:T(8,128)(2,1)S(1)}, bf16[4,256,256]{2,1,0:T(8,128)(2,1)}, u32[]{:S(2)}) copy-start(bf16[4,256,256]{2,1,0:T(8,128)(2,1)} %get-tuple-element.108.refs_3_.ya_ref) | copy-start | bytes 1572868
  59.3 2.2 %copy-start.11 = (bf16[2,32,512]{2,1,0:T(8,128)(2,1)S(1)}, bf16[2,32,512]{2,1,0:T(8,128)(2,1)}, u32[]{:S(2)}) copy-start(bf16[2,32,512]{2,1,0:T(8,128)(2,1)} %get-tuple-element.110.refs_5_.za_ref) | copy-start | bytes 196612
  65.3 5.6 %collective-permute-start.11 = (f16[656,128]{1,0:T(8,128)(2,1)S(1)}, f16[656,128]{1,0:T(8,128)(2,1)S(1)}, u32[]{:S(2)}, u32[]{:S(2)}) collective-permute-start(f16[656,128]{1,0:T(8,128)(2,1)S(1)} %convert_element_type.60), channel_id=1, source_target_pairs={{0,1},{1,0},{2,3},{3,2},{4,8},{5,9},{6,10},{7,11},{8,4},{9,5},{10,... | collective-permute-start | bytes 503816 | tf_op jit(solution)/shard_map/ppermute | solution.py:535
  68.5 2.5 %collective-permute-start.10 = (f16[656,128]{1,0:T(8,128)(2,1)S(1)}, f16[656,128]{1,0:T(8,128)(2,1)S(1)}, u32[]{:S(2)}, u32[]{:S(2)}) collective-permute-start(f16[656,128]{1,0:T(8,128)(2,1)S(1)} %convert_element_type.58), channel_id=1, source_target_pairs={{0,4},{1,5},{2,6},{3,7},{4,0},{5,1},{6,2},{7,3},{8,12},{9,13},{10,... | collective-permute-start | bytes 503816 | tf_op jit(solution)/shard_map/ppermute | solution.py:531
  71.2 4.1 %collective-permute-start.12 = (f32[64,128]{1,0:T(8,128)S(1)}, f32[64,128]{1,0:T(8,128)S(1)}, u32[]{:S(2)}, u32[]{:S(2)}) collective-permute-start(f32[64,128]{1,0:T(8,128)S(1)} %get-tuple-element.165), channel_id=1, source_target_pairs={{0,1},{1,0},{2,3},{3,2},{4,5},{5,4},{6,7},{7,6},{8,9},{9,8},{10,11... | collective-permute-start | bytes 98312 | tf_op jit(solution)/shard_map/ppermute | solution.py:531
  72.4 2.9 %collective-permute-start.13 = (f32[64,128]{1,0:T(8,128)S(1)}, f32[64,128]{1,0:T(8,128)S(1)}, u32[]{:S(2)}, u32[]{:S(2)}) collective-permute-start(f32[64,128]{1,0:T(8,128)S(1)} %get-tuple-element.166), channel_id=1, source_target_pairs={{0,4},{1,2},{2,1},{3,7},{4,0},{5,6},{6,5},{7,3},{8,12},{9,10},{10,... | collective-permute-start | bytes 98312 | tf_op jit(solution)/shard_map/ppermute | solution.py:535

commit v5 on v4

--- a/solution.py
+++ b/solution.py
@@ -211,29 +211,18 @@
     return jnp.concatenate(halves, axis=0)
 
 
-def unpack_strip(halves, shift):
-    lane = iota((NZ, LANES), 1)
-    first = jnp.where(shift > 0, BY - STRIP, 0)
-    inside = jnp.logical_and(lane >= first, lane < first + STRIP)
-    rows = []
-    for x in range(BX):
-        half, j = x // 8, x % 8
-        moved = pltpu.roll(halves[half * NZ : (half + 1) * NZ, :], 2 * LANES - shift - STRIP * j, 1)
-        rows.append(jnp.where(inside, moved, 0.0))
-    return jnp.concatenate(rows, axis=0)
-
-
-def unpack_strips(up, down, shifts):
-    lane = iota((NZ, LANES), 1)
+def unpack_strips(up, down, shifts, planes=slice(0, NZ)):
+    first, last = planes.start, planes.stop
+    lane = iota((last - first, LANES), 1)
     inside = []
     for shift in shifts:
-        first = jnp.where(shift > 0, BY - STRIP, 0)
-        inside.append(jnp.logical_and(lane >= first, lane < first + STRIP))
+        edge = jnp.where(shift > 0, BY - STRIP, 0)
+        inside.append(jnp.logical_and(lane >= edge, lane < edge + STRIP))
     rows = []
     for x in range(BX):
         half, j = x // 8, x % 8
         moved = [
-            pltpu.roll(a[half * NZ : (half + 1) * NZ, :], 2 * LANES - shift - STRIP * j, 1)
+            pltpu.roll(a[half * NZ + first : half * NZ + last, :], 2 * LANES - shift - STRIP * j, 1)
             for a, shift in zip((up, down), shifts)
         ]
         rows.append(jnp.where(inside[0], moved[0], jnp.where(inside[1], moved[1], 0.0)))
@@ -273,29 +262,30 @@
 def forward_parts(message, matrices, shifts, add):
     k, y, xy, z = matrices
     field, strips = message_parts(message)
-    totals = []
-    for yr in range(2):
-        along = dot(z[yr], column3(wide(strips[yr])))
-        totals.append([tall(two_rows(along[v * NZ : (v + 1) * NZ], xy[yr, v])) for v in range(V)])
     spread = three_lanes(field, y[...])
+    alongs = [dot(z[yr], column3(wide(strips[yr]))) for yr in range(2)]
     for v in range(V):
         center = two_lanes(k[v], spread[:, v * BY : (v + 1) * BY])
-        add(v, center + unpack_strips(totals[0][v], totals[1][v], shifts))
+        rows = slice(v * NZ, (v + 1) * NZ)
+        up, down = [tall(two_rows(alongs[yr][rows], xy[yr, v])) for yr in range(2)]
+        add(v, center + unpack_strips(up, down, shifts))
 
 
 def adjoint_parts(quotient_ref, edge_ref, refs):
     k_ref, y_ref, xy_ref, z_ref = refs
-    total = jnp.zeros((FIELD, LANES), f32)
+    columns = []
     for v in range(V):
         hi, lo = split(quotient_ref[v])
         both = dot(jnp.concatenate([hi, lo], axis=1), y_ref[v])
-        spread = both[:, :BY] + both[:, BY:]
-        total += two_lanes(k_ref[v], spread)
+        columns.append(jnp.concatenate(split(both[:, :BY] + both[:, BY:]), axis=1))
+    both = dot(
+        jnp.concatenate([k_ref[v] for v in range(V)], axis=1), jnp.concatenate(columns, axis=0)
+    )
     strips = []
     for yr in range(2):
         parts = [column3(two_rows(wide(edge_ref[v, yr]), xy_ref[yr, v])) for v in range(V)]
         strips.append(tall(dot(z_ref[yr], jnp.concatenate(parts, axis=0))))
-    return total, strips
+    return both[:, :BY] + both[:, BY:], strips
 
 
 def write_message(ref, field, strips):
@@ -330,11 +320,15 @@
     )
     copies = fetch(outside, (estimate_ref, *held), sems)
     copies[0].wait()
-    for x in range(BX):
-        field_ref[x * NZ : (x + 1) * NZ, :] = estimate_ref[:, x, :]
-    field = field_ref[...]
-    first_ref[...] = pack_strip(field, info_ref[0])
-    second_ref[...] = pack_strip(field, info_ref[1])
+
+    @pl.when(info_ref[0] >= 0)
+    def _():
+        for x in range(BX):
+            field_ref[x * NZ : (x + 1) * NZ, :] = estimate_ref[:, x, :]
+        field = field_ref[...]
+        first_ref[...] = pack_strip(field, info_ref[0])
+        second_ref[...] = pack_strip(field, info_ref[1])
+
     for copy in copies[1:]:
         copy.wait()
 
@@ -369,27 +363,34 @@
 
 
 def quotient_first_kernel(info_ref, arrived_ref, *refs):
-    outside, (data_ref, quotient_ref, edge_ref, far_ref), held, sems = (
-        refs[:6], refs[6:10], refs[10:16], refs[16],
-    )
-    copies = fetch(outside, held, sems)
+    outside, (data_ref, quotient_ref, edge_ref, far_ref), held, planes_ref, sems = (
+        refs[:6], refs[6:10], refs[10:16], refs[16], refs[17],
+    )
+    parts = [(outside[0], held[0])] + [(outside[1].at[v], held[1].at[v]) for v in range(V)]
+    parts += list(zip(outside[2:], held[2:]))
+    copies = fetch(*zip(*parts), sems)
     table_ref, inverse_ref, *matrices = held
     shifts = (info_ref[0], info_ref[1])
     copies[0].wait()
-    copies[1].wait()
 
     @pl.when(shifts[0] >= 0)
     def _():
-        planes = dot(table_ref[...], arrived_ref[...])
-        for v in range(V):
+        planes_ref[...] = dot(table_ref[...], arrived_ref[...])
+
+    for v in range(V):
+        copies[1 + v].wait()
+
+        @pl.when(shifts[0] >= 0)
+        def _():
             for x in range(BX):
                 rows = slice(x * NZ, (x + 1) * NZ)
-                piece = planes[v * NZ : (v + 1) * NZ, x * BY : (x + 1) * BY]
+                piece = planes_ref[v * NZ : (v + 1) * NZ, x * BY : (x + 1) * BY]
                 data_ref[v, rows, :] = piece.astype(bf16)
                 quotient_ref[v, rows, :] = piece * inverse_ref[v, rows, :]
-        pack_edges(quotient_ref, edge_ref, shifts)
-
-    for copy in copies[2:]:
+            for yr in range(2):
+                edge_ref[v, yr] = pack_strip(quotient_ref[v], shifts[yr])
+
+    for copy in copies[1 + V :]:
         copy.wait()
     write_scaled(far_ref, *adjoint_parts(quotient_ref, edge_ref, matrices))
 
@@ -427,10 +428,8 @@
     info_ref, old_ref, total_ref, up_ref, down_ref, up_in_ref, down_in_ref, new_ref, scaled_ref
 ):
     half = 2 * NZ
-    correction = total_ref[...]
-    for n, ref in enumerate((up_in_ref, down_in_ref)):
-        correction += unpack_strip(ref[:half], info_ref[n])
-    field = old_ref[:FIELD] * correction
+    shifts = (info_ref[0], info_ref[1])
+    field = old_ref[:FIELD] * (total_ref[...] + unpack_strips(up_in_ref[:half], down_in_ref[:half], shifts))
     strips = []
     for n, (ref, own) in enumerate(((up_in_ref, up_ref), (down_in_ref, down_ref))):
         rows = slice(FIELD + n * half, FIELD + (n + 1) * half)
@@ -471,13 +470,25 @@
     write_scaled(far_ref, *adjoint_parts(quotient_ref, edge_ref, (ka_ref, ya_ref, xya_ref, za_ref)))
 
 
-def final_kernel(info_ref, old_ref, total_ref, up_in_ref, down_in_ref, out_ref):
-    correction = total_ref[...]
-    for n, ref in enumerate((up_in_ref, down_in_ref)):
-        correction += unpack_strip(ref[...], info_ref[n])
-    result = old_ref[:FIELD] * correction
-    for x in range(BX):
-        out_ref[:, x, :] = result[x * NZ : (x + 1) * NZ]
+def final_kernel(info_ref, old_ref, total_ref, up_in_ref, down_in_ref, out_ref, held_ref, sems):
+    shifts = (info_ref[0], info_ref[1])
+    half = NZ // 2
+    copies = []
+    for n in range(2):
+
+        @pl.when(shifts[0] >= 0)
+        def _():
+            edges = unpack_strips(up_in_ref[...], down_in_ref[...], shifts, slice(n * half, (n + 1) * half))
+            for x in range(BX):
+                rows = slice(x * NZ + n * half, x * NZ + (n + 1) * half)
+                correction = total_ref[rows] + edges[x * half : (x + 1) * half]
+                held_ref[n * half : (n + 1) * half, x, :] = old_ref[rows] * correction
+
+        part = slice(n * half, (n + 1) * half)
+        copies.append(pltpu.make_async_copy(held_ref.at[part], out_ref.at[part], sems.at[n]))
+        copies[-1].start()
+    for copy in copies:
+        copy.wait()
 
 
 SMEM, VMEM, HBM = pltpu.SMEM, pltpu.VMEM, pltpu.HBM
@@ -656,7 +667,8 @@
     data, quotient, edge, far = call(
         quotient_first_kernel, [(every, bf16), (every, f32), edges, (scaled, f32)],
         info, arrived, scalars=1, far=fetched,
-        scratch=held([(a.shape, a.dtype) for a in fetched]) + [pltpu.SemaphoreType.DMA((len(fetched),))],
+        scratch=held([(a.shape, a.dtype) for a in fetched])
+        + [pltpu.VMEM((slots, plane), f32), pltpu.SemaphoreType.DMA((len(fetched) + V - 1,))],
     )
 
     def sides(quotient, edge, far):
@@ -694,7 +706,10 @@
         gather_last_kernel, [(one, f32), (half, f32), (half, f32)], *sides(quotient, edge, far)
     )
     up_in, down_in = swap("gy", up, down)
-    (refined,) = call(final_kernel, [(estimate.shape, f32)], info, new, total, up_in, down_in, scalars=1)
+    (refined,) = call(
+        final_kernel, [(estimate.shape, f32)], info, new, total, up_in, down_in, scalars=1, out_place=HBM,
+        scratch=[pltpu.VMEM(estimate.shape, f32), pltpu.SemaphoreType.DMA((2,))],
+    )
     return refined
 
 

time: 78 us -> 77.5 us (level)
  Pallas kernels: 46.3 us -> 44.9 us
    pallas_call x21, Pallas kernels: 46.3 us -> 44.9 us  [call(): pl.pallas_call(kernel, out_shape=[HBM(s, d) if where is HBM else jax.Shap...]
  transfers between devices with their start and end apart: 15 -> 15, of which waited for: 5 -> 5; matrix products, arithmetic and copies ran while one was open for 2% -> 2% of each run, Pallas kernels for 42% -> 41%
where the time goes in v5:
time: 77.5 us; the launch traced here: 76.3 us
  Pallas kernels  44.9 us (58%)
  starting transfers between devices  20.8 us (27%)
  waiting for transfers between devices  7.61 us (10%)
  local copies, waits for them, and re-layouts  1.28 us (2%)
  other arithmetic  0.8 us (1%)
  between operations  0.79 us (1%)
    pallas_call x21, Pallas kernels, call(): pl.pallas_call(kernel, out_shape=[HBM(s, d) if where is HBM else jax.Shap...  44.9 us
    ppermute x7, starting transfers between devices, swap_far(): lax.ppermute(narrow(axis, value), ('gx', 'gy'), partner_swaps(axis)[1])  8.33 us
    ppermute x7, starting transfers between devices, swap_near(): lax.ppermute(narrow(axis, value), ('gx', 'gy'), partner_swaps(axis)[0])  7.02 us
    all_to_all x1, starting transfers between devices, shards(): lax.all_to_all(outgoing.reshape(devices, cap, plane), ('gx', 'gy'), split...  5.4 us
    ppermute x7, waiting for transfers between devices, swap_near(): lax.ppermute(narrow(axis, value), ('gx', 'gy'), partner_swaps(axis)[0])  2.94 us
    all_to_all x1, waiting for transfers between devices, shards(): lax.all_to_all(outgoing.reshape(devices, cap, plane), ('gx', 'gy'), split...  2.68 us
    ppermute x7, waiting for transfers between devices, swap_far(): lax.ppermute(narrow(axis, value), ('gx', 'gy'), partner_swaps(axis)[1])  1.98 us
  transfers between devices with their start and end apart: 15, of which 5 were waited for; matrix products, arithmetic and copies ran while one was open for 2% of the time, Pallas kernels for 41%

profile of v5, /device:TPU:0, one launch (start us, length us, event | category | flops | bytes accessed | tf_op | source)
XLA Modules:
  0.0 76.3 jit_solution(11855619634879075961)
XLA Ops:
  0.1 1.8 %shard_map.55 = (f32[512,128]{1,0:T(8,128)S(1)}, f32[64,128]{1,0:T(8,128)S(1)}, f32[64,128]{1,0:T(8,128)S(1)}, s32[32,128]{1,0:T(8,128)S(1)}, bf16[128,16,128]{2,1,0:T(8,128)(2,1)S(1)}) custom-call(s32[2]{0:T(128)S(1)} %pad_add_fusion.info_ref, f32[32,16,128]{2,1,0:T(8,128)} %refs_0_.1, s32[32,128]{1,0:T(8,128)} %bitcast.9, bf16[128,16,128]{2,1,0:T(8,128)(2,1)} %refs_2_.1), custom_call_target="tpu_custom_call" | custom-call | bytes 70000 | tf_op jit(solution)/shard_map/pallas_call | solution.py:506
  1.9 3.1 %collective-permute-start = (f32[64,128]{1,0:T(8,128)S(1)}, f32[64,128]{1,0:T(8,128)S(1)}, u32[]{:S(2)}, u32[]{:S(2)}) collective-permute-start(f32[64,128]{1,0:T(8,128)S(1)} %get-tuple-element.87), channel_id=1, source_target_pairs={{0,1},{1,0},{2,3},{3,2},{4,5},{5,4},{6,7},{7,6},{8,9},{9,8},{10,11... | collective-permute-start | bytes 98312 | tf_op jit(solution)/shard_map/ppermute | solution.py:542
  5.0 1.6 %shard_map.56 = bf16[256,2048]{1,0:T(8,128)(2,1)} custom-call(s32[1]{0:T(128)} %bitcast.3.me_ref, s32[32,128]{1,0:T(8,128)S(1)} %get-tuple-element.89.slots_ref, bf16[128,16,128]{2,1,0:T(8,128)(2,1)S(1)} %get-tuple-element.90.stored_ref), custom_call_target="tpu_custom_call" | custom-call | bytes 70000 | tf_op jit(solution)/shard_map/pallas_call | solution.py:506
  6.6 5.4 %all-to-all-start = ((bf16[32,8,2048]{2,1,0:T(8,128)(2,1)}), bf16[32,8,2048]{2,1,0:T(8,128)(2,1)S(1)}, u32[]{:S(2)}, u32[]{:S(2)}) async-start(bf16[32,8,2048]{2,1,0:T(8,128)(2,1)} %bitcast.4), calls=%async_computation | async-start | bytes 2097152 | tf_op jit(solution)/shard_map/all_to_all | solution.py:623
  13.7 2.5 %shard_map.58 = (bf16[4,512,512]{2,1,0:T(8,128)(2,1)S(1)}, bf16[384,512]{1,0:T(8,128)(2,1)S(1)}, bf16[2,4,256,256]{3,2,1,0:T(8,128)(2,1)S(1)}, bf16[2,128,128]{2...) custom-call(f32[108,128]{1,0:T(8,128)S(1)} %get-tuple-element.126.ta, ...), custom_call_target="tpu_custom_call" | custom-call | bytes 10500000 | tf_op jit(solution)/shard_map/pallas_call | solution.py:506
  16.2 7.0 %shard_map.62 = (bf16[4,512,512]{2,1,0:T(8,128)(2,1)}, bf16[4,256,256]{2,1,0:T(8,128)(2,1)}, bf16[2,4,256,256]{3,2,1,0:T(8,128)(2,1)}, bf16[2,32,512]{2,1,0:T(8,...) custom-call(f32[108,128]{1,0:T(8,128)S(1)} %get-tuple-element.126.ta, ...), custom_call_target="tpu_custom_call" | custom-call | bytes 14000000 | tf_op jit(solution)/shard_map/pallas_call | solution.py:506
  23.3 1.8 %collective-permute-start.3 = (f16[640,128]{1,0:T(8,128)(2,1)S(1)}, f16[640,128]{1,0:T(8,128)(2,1)S(1)}, u32[]{:S(2)}, u32[]{:S(2)}) collective-permute-start(f16[640,128]{1,0:T(8,128)(2,1)S(1)} %convert_element_type.48), channel_id=1, source_target_pairs={{0,1},{1,0},{2,3},{3,2},{4,8},{5,9},{6,10},{7,11},{8,4},{9,5},{10,... | collective-permute-start | bytes 491528 | tf_op jit(solution)/shard_map/ppermute | solution.py:546
  25.2 1.0 %shard_map.57.refs_0_ = bf16[128,256]{1,0:T(8,128)(2,1)} custom-call(s32[1]{0:T(128)} %bitcast.3.me_ref, s32[256,128]{1,0:T(8,128)S(1)} %broadcast_bitcast_fusion.slots_ref), custom_call_target="tpu_custom_call" | custom-call | bytes 70000 | tf_op jit(solution)/shard_map/pallas_call | solution.py:506
  26.2 1.9 %shard_map.59.refs_0_ = f32[4,512,128]{2,1,0:T(8,128)S(1)} custom-call(s32[2]{0:T(128)S(1)} %pad_add_fusion.info_ref, f32[640,128]{1,0:T(8,128)S(1)} %constant_dynamic-update-slice_fusion.refs_0_.old_ref, bf16[4,512,512]{2,1,0:T(8,128)(2,1)S(1)} %get-tuple-element.95.refs_1_, bf16[384,512]{1,0:T(8,128)(2,1)S(1)} %get-tuple-element.96.refs_2_, ...), custom_call_target="tpu_custom_call" | custom-call | bytes 70000 | tf_op jit(solution)/shard_map/pallas_call | solution.py:506
  28.2 2.0 %shard_map.60.blurred_ref = f32[4,512,128]{2,1,0:T(8,128)S(1)} custom-call(s32[2]{0:T(128)S(1)} %pad_add_fusion.info_ref, f32[4,512,128]{2,1,0:T(8,128)S(1)} %shard_map.59.refs_0_, f32[640,128]{1,0:T(8,128)S(1)} %convert_element_type.49.refs_1_, bf16[4,512,512]{2,1,0:T(8,128)(2,1)S(1)} %get-tuple-element.99.refs_2_, ...), custom_call_target="tpu_custom_call" | custom-call | bytes 70000 | tf_op jit(solution)/shard_map/pallas_call | solution.py:506
  30.2 1.2 %collective-permute-done.3 = f16[640,128]{1,0:T(8,128)(2,1)S(1)} collective-permute-done((f16[640,128]{1,0:T(8,128)(2,1)S(1)}, f16[640,128]{1,0:T(8,128)(2,1)S(1)}, u32[]{:S(2)}, u32[]{:S(2)}) %collective-permute-start.3) | collective-permute-done | bytes 163872 | tf_op jit(solution)/shard_map/ppermute | solution.py:546
  31.4 2.9 %shard_map.61.refs_1_ = f32[4,512,128]{2,1,0:T(8,128)} custom-call(s32[2]{0:T(128)S(1)} %pad_add_fusion.info_ref, f32[4,512,128]{2,1,0:T(8,128)S(1)} %shard_map.60.blurred_ref, f32[640,128]{1,0:T(8,128)S(1)} %convert_element_type.50.message_ref, bf16[4,512,512]{2,1,0:T(8,128)(2,1)S(1)} %get-tuple-element.103.k_ref, ...), custom_call_target="tpu_custom_call" | custom-call | bytes 70000 | tf_op jit(solution)/shard_map/pallas_call | solution.py:506
  34.4 2.7 %all-to-all-done = bf16[32,8,2048]{2,1,0:T(8,128)(2,1)S(1)} async-done(((bf16[32,8,2048]{2,1,0:T(8,128)(2,1)}), bf16[32,8,2048]{2,1,0:T(8,128)(2,1)S(1)}, u32[]{:S(2)}, u32[]{:S(2)}) %all-to-all-start) | async-done | bytes 1048608 | tf_op jit(solution)/shard_map/all_to_all | solution.py:623
  37.1 4.8 %shard_map.63 = (bf16[4,512,128]{2,1,0:T(8,128)(2,1)S(1)}, f32[4,512,128]{2,1,0:T(8,128)S(1)}, f32[4,2,64,128]{3,2,1,0:T(8,128)S(1)}, f32[656,128]{1,0:T(8,128)S(1)}) custom-call(s32[2]{0:T(128)S(1)} %pad_add_fusion.info_ref, bf16[256,2048]{1,0:T(8,128)(2,1)S(1)} %bitcast.8, bf16[128,256]{1,0:T(8,128)(2,1)} %shard_map.57.refs_0_, ...), custom_call_target="tpu_custom_call" | custom-call | bytes 70000 | tf_op jit(solution)/shard_map/pallas_call | solution.py:506
  41.9 3.2 %collective-permute-start.5 = (f16[656,128]{1,0:T(8,128)(2,1)S(1)}, f16[656,128]{1,0:T(8,128)(2,1)S(1)}, u32[]{:S(2)}, u32[]{:S(2)}) collective-permute-start(f16[656,128]{1,0:T(8,128)(2,1)S(1)} %convert_element_type.53), channel_id=1, source_target_pairs={{0,1},{1,0},{2,3},{3,2},{4,8},{5,9},{6,10},{7,11},{8,4},{9,5},{10,... | collective-permute-start | bytes 503816 | tf_op jit(solution)/shard_map/ppermute | solution.py:546
  45.1 1.5 %shard_map.65 = f32[656,128]{1,0:T(8,128)S(1)} custom-call(f32[4,512,128]{2,1,0:T(8,128)S(1)} %get-tuple-element.111.quotient_ref, f32[4,2,64,128]{3,2,1,0:T(8,128)S(1)} %get-tuple-element.112.edge_ref, bf16[4,512,512]{2,1,0:T(8,128)(2,1)S(1)} %copy-done.1, bf16[4,256,256]{2,1,0:T(8,128)(2,1)S(1)} %copy-done.7, bf16[2,4,256,256]{3,2,1,0:T(8,128)(2,1)S(1)} %copy-done.4, ...), custom_call_target="tpu_custom_call" | custom-call | bytes 70000 | tf_op jit(solution)/shard_map/pallas_call | solution.py:506
  47.1 1.4 %shard_map.64 = (f32[512,128]{1,0:T(8,128)S(1)}, f32[2,64,128]{2,1,0:T(8,128)S(1)}) custom-call(f32[4,512,128]{2,1,0:T(8,128)S(1)} %get-tuple-element.111.quotient_ref, f32[4,2,64,128]{3,2,1,0:T(8,128)S(1)} %get-tuple-element.112.edge_ref, bf16[4,512,512]{2,1,0:T(8,128)(2,1)S(1)} %copy-done, bf16[4,256,256]{2,1,0:T(8,128)(2,1)S(1)} %copy-done.6, ...), custom_call_target="tpu_custom_call" | custom-call | bytes 70000 | tf_op jit(solution)/shard_map/pallas_call | solution.py:506
  48.5 0.8 %shard_map.66 = (f32[512,128]{1,0:T(8,128)S(1)}, f32[128,128]{1,0:T(8,128)S(1)}, f32[128,128]{1,0:T(8,128)S(1)}) custom-call(s32[2]{0:T(128)S(1)} %pad_add_fusion.info_ref, f32[512,128]{1,0:T(8,128)S(1)} %get-tuple-element.117.field_ref, f32[2,64,128]{2,1,0:T(8,128)S(1)} %get-tuple-element.118.strips_ref, f32[656,128]{1,0:T(8,128)S(1)} %convert_element_type.52.near_ref, ...), custom_call_target="tpu_custom_call" | custom-call | bytes 70000 | tf_op jit(solution)/shard_map/pallas_call | solution.py:506
  49.4 2.0 %collective-permute-start.6 = (f32[128,128]{1,0:T(8,128)S(1)}, f32[128,128]{1,0:T(8,128)S(1)}, u32[]{:S(2)}, u32[]{:S(2)}) collective-permute-start(f32[128,128]{1,0:T(8,128)S(1)} %get-tuple-element.142.up_ref), channel_id=1, source_target_pairs={{0,1},{1,0},{2,3},{3,2},{4,5},{5,4},{6,7},{7,6},{8,9},{9,8},{10,11... | collective-permute-start | bytes 196616 | tf_op jit(solution)/shard_map/ppermute | solution.py:542
  51.4 2.5 %shard_map.67 = (bf16[4,512,512]{2,1,0:T(8,128)(2,1)S(1)}, bf16[384,512]{1,0:T(8,128)(2,1)S(1)}, bf16[2,4,256,256]{3,2,1,0:T(8,128)(2,1)S(1)}, bf16[2,128,128]{2...) custom-call(f32[108,128]{1,0:T(8,128)S(1)} %get-tuple-element.126.ta, ...), custom_call_target="tpu_custom_call" | custom-call | bytes 70000 | tf_op jit(solution)/shard_map/pallas_call | solution.py:506
  54.2 0.9 %shard_map.68 = (f32[640,128]{1,0:T(8,128)S(1)}, f32[656,128]{1,0:T(8,128)S(1)}) custom-call(s32[2]{0:T(128)S(1)} %pad_add_fusion.info_ref, f32[640,128]{1,0:T(8,128)S(1)} %constant_dynamic-update-slice_fusion.refs_0_.old_ref, f32[512,128]{1,0:T(8,128)S(1)} %get-tuple-element.141.total_ref, f32[128,128]{1,0:T(8,128)S(1)} %get-tuple-element.142.up_ref, ...), custom_call_target="tpu_custom_call" | custom-call | bytes 70000 | tf_op jit(solution)/shard_map/pallas_call | solution.py:506
  55.4 1.6 %collective-permute-start.9 = (f16[656,128]{1,0:T(8,128)(2,1)S(1)}, f16[656,128]{1,0:T(8,128)(2,1)S(1)}, u32[]{:S(2)}, u32[]{:S(2)}) collective-permute-start(f16[656,128]{1,0:T(8,128)(2,1)S(1)} %convert_element_type.55), channel_id=1, source_target_pairs={{0,1},{1,0},{2,3},{3,2},{4,8},{5,9},{6,10},{7,11},{8,4},{9,5},{10,... | collective-permute-start | bytes 503816 | tf_op jit(solution)/shard_map/ppermute | solution.py:546
  57.0 1.9 %shard_map.69.blurred_ref = f32[4,512,128]{2,1,0:T(8,128)S(1)} custom-call(s32[2]{0:T(128)S(1)} %pad_add_fusion.info_ref, f32[640,128]{1,0:T(8,128)S(1)} %get-tuple-element.144.own_ref.old_ref, bf16[4,512,512]{2,1,0:T(8,128)(2,1)S(1)} %get-tuple-element.146.k_ref, bf16[384,512]{1,0:T(8,128)(2,1)S(1)} %get-tuple-element.147.y_ref, ...), custom_call_target="tpu_custom_call" | custom-call | bytes 70000 | tf_op jit(solution)/shard_map/pallas_call | solution.py:506
  59.1 2.0 %shard_map.70.blurred_ref = f32[4,512,128]{2,1,0:T(8,128)S(1)} custom-call(s32[2]{0:T(128)S(1)} %pad_add_fusion.info_ref, f32[4,512,128]{2,1,0:T(8,128)S(1)} %shard_map.69.blurred_ref, f32[656,128]{1,0:T(8,128)S(1)} %convert_element_type.56.near_ref, bf16[4,512,512]{2,1,0:T(8,128)(2,1)S(1)} %get-tuple-element.151.k_ref, ...), custom_call_target="tpu_custom_call" | custom-call | bytes 70000 | tf_op jit(solution)/shard_map/pallas_call | solution.py:506
  61.1 3.5 %shard_map.71 = (f32[4,512,128]{2,1,0:T(8,128)S(1)}, f32[4,2,64,128]{3,2,1,0:T(8,128)S(1)}, f32[656,128]{1,0:T(8,128)S(1)}) custom-call(s32[2]{0:T(128)S(1)} %pad_add_fusion.info_ref, bf16[4,512,128]{2,1,0:T(8,128)(2,1)S(1)} %get-tuple-element.145.data_ref, f32[4,512,128]{2,1,0:T(8,128)S(1)} %shard_map.70.blurred_ref, ...), custom_call_target="tpu_custom_call" | custom-call | bytes 70000 | tf_op jit(solution)/shard_map/pallas_call | solution.py:506
  64.6 1.4 %collective-permute-start.11 = (f16[656,128]{1,0:T(8,128)(2,1)S(1)}, f16[656,128]{1,0:T(8,128)(2,1)S(1)}, u32[]{:S(2)}, u32[]{:S(2)}) collective-permute-start(f16[656,128]{1,0:T(8,128)(2,1)S(1)} %convert_element_type.60), channel_id=1, source_target_pairs={{0,1},{1,0},{2,3},{3,2},{4,8},{5,9},{6,10},{7,11},{8,4},{9,5},{10,... | collective-permute-start | bytes 503816 | tf_op jit(solution)/shard_map/ppermute | solution.py:546
  66.0 1.7 %shard_map.73 = f32[656,128]{1,0:T(8,128)S(1)} custom-call(f32[4,512,128]{2,1,0:T(8,128)S(1)} %get-tuple-element.159.quotient_ref, f32[4,2,64,128]{3,2,1,0:T(8,128)S(1)} %get-tuple-element.160.edge_ref, bf16[4,512,512]{2,1,0:T(8,128)(2,1)S(1)} %copy-done.1, bf16[4,256,256]{2,1,0:T(8,128)(2,1)S(1)} %copy-done.7, bf16[2,4,256,256]{3,2,1,0:T(8,128)(2,1)S(1)} %copy-done.4, ...), custom_call_target="tpu_custom_call" | custom-call | bytes 70000 | tf_op jit(solution)/shard_map/pallas_call | solution.py:506
  67.9 1.4 %shard_map.72 = (f32[512,128]{1,0:T(8,128)S(1)}, f32[2,64,128]{2,1,0:T(8,128)S(1)}) custom-call(f32[4,512,128]{2,1,0:T(8,128)S(1)} %get-tuple-element.159.quotient_ref, f32[4,2,64,128]{3,2,1,0:T(8,128)S(1)} %get-tuple-element.160.edge_ref, bf16[4,512,512]{2,1,0:T(8,128)(2,1)S(1)} %copy-done, bf16[4,256,256]{2,1,0:T(8,128)(2,1)S(1)} %copy-done.6, ...), custom_call_target="tpu_custom_call" | custom-call | bytes 70000 | tf_op jit(solution)/shard_map/pallas_call | solution.py:506
  69.3 0.8 collective-permute-done.11
  70.2 1.4 %collective-permute-start.12 = (f32[64,128]{1,0:T(8,128)S(1)}, f32[64,128]{1,0:T(8,128)S(1)}, u32[]{:S(2)}, u32[]{:S(2)}) collective-permute-start(f32[64,128]{1,0:T(8,128)S(1)} %get-tuple-element.165), channel_id=1, source_target_pairs={{0,1},{1,0},{2,3},{3,2},{4,5},{5,4},{6,7},{7,6},{8,9},{9,8},{10,11... | collective-permute-start | bytes 98312 | tf_op jit(solution)/shard_map/ppermute | solution.py:542
  72.0 2.6 %collective-permute-done.12.up_in_ref = f32[64,128]{1,0:T(8,128)S(1)} collective-permute-done((f32[64,128]{1,0:T(8,128)S(1)}, f32[64,128]{1,0:T(8,128)S(1)}, u32[]{:S(2)}, u32[]{:S(2)}) %collective-permute-start.12) | collective-permute-done | bytes 32800 | tf_op jit(solution)/shard_map/ppermute | solution.py:542
  74.6 1.6 %shard_map.75 = f32[32,16,128]{2,1,0:T(8,128)} custom-call(s32[2]{0:T(128)S(1)} %pad_add_fusion.info_ref, f32[640,128]{1,0:T(8,128)S(1)} %get-tuple-element.144.own_ref.old_ref, f32[512,128]{1,0:T(8,128)S(1)} %get-tuple-element.164.total_ref, f32[64,128]{1,0:T(8,128)S(1)} %collective-permute-done.12.up_in_ref, f32[64,128]{1,0:T(8,128)S(1)} %collective-permute-done.13.down_in_ref), custom_call_target="tpu_custom_call" | custom-call | bytes 70000 | tf_op jit(solution)/shard_map/pallas_call | solution.py:506
  (86 shorter events, 3.6 us)
Async XLA Ops:
  0.1 12.0 %copy-start.12 = (s32[8,4,4,3]{0,2,3,1:T(4,128)S(1)}, s32[8,4,4,3]{0,2,3,1:T(4,128)}, u32[]{:S(2)}) copy-start(s32[8,4,4,3]{0,2,3,1:T(4,128)} %param.9) | copy-start | bytes 4612
  1.9 10.8 %copy-start.14 = (f32[48,31]{0,1:T(8,128)S(1)}, f32[48,31]{0,1:T(8,128)}, u32[]{:S(2)}) copy-start(f32[48,31]{0,1:T(8,128)} %param.8) | copy-start | bytes 17860
  1.9 21.3 %collective-permute-start = (f32[64,128]{1,0:T(8,128)S(1)}, f32[64,128]{1,0:T(8,128)S(1)}, u32[]{:S(2)}, u32[]{:S(2)}) collective-permute-start(f32[64,128]{1,0:T(8,128)S(1)} %get-tuple-element.87), channel_id=1, source_target_pairs={{0,1},{1,0},{2,3},{3,2},{4,5},{5,4},{6,7},{7,6},{8,9},{9,8},{10,11... | collective-permute-start | bytes 98312 | tf_op jit(solution)/shard_map/ppermute | solution.py:542
  5.0 18.2 %collective-permute-start.1 = (f32[64,128]{1,0:T(8,128)S(1)}, f32[64,128]{1,0:T(8,128)S(1)}, u32[]{:S(2)}, u32[]{:S(2)}) collective-permute-start(f32[64,128]{1,0:T(8,128)S(1)} %get-tuple-element.88), channel_id=1, source_target_pairs={{0,4},{1,2},{2,1},{3,7},{4,0},{5,6},{6,5},{7,3},{8,12},{9,10},{10,... | collective-permute-start | bytes 98312 | tf_op jit(solution)/shard_map/ppermute | solution.py:546
  6.6 30.5 %all-to-all-start = ((bf16[32,8,2048]{2,1,0:T(8,128)(2,1)}), bf16[32,8,2048]{2,1,0:T(8,128)(2,1)S(1)}, u32[]{:S(2)}, u32[]{:S(2)}) async-start(bf16[32,8,2048]{2,1,0:T(8,128)(2,1)} %bitcast.4), calls=%async_computation | async-start | bytes 2097152 | tf_op jit(solution)/shard_map/all_to_all | solution.py:623
  12.0 13.2 %copy-start.13 = (s32[4096]{0:T(1024)S(1)}, s32[4096]{0:T(1024)}, u32[]{:S(2)}) copy-start(s32[4096]{0:T(1024)} %param.7) | copy-start | bytes 49156
  23.3 8.1 %collective-permute-start.3 = (f16[640,128]{1,0:T(8,128)(2,1)S(1)}, f16[640,128]{1,0:T(8,128)(2,1)S(1)}, u32[]{:S(2)}, u32[]{:S(2)}) collective-permute-start(f16[640,128]{1,0:T(8,128)(2,1)S(1)} %convert_element_type.48), channel_id=1, source_target_pairs={{0,1},{1,0},{2,3},{3,2},{4,8},{5,9},{6,10},{7,11},{8,4},{9,5},{10,... | collective-permute-start | bytes 491528 | tf_op jit(solution)/shard_map/ppermute | solution.py:546
  25.1 3.1 %collective-permute-start.2 = (f16[640,128]{1,0:T(8,128)(2,1)S(1)}, f16[640,128]{1,0:T(8,128)(2,1)S(1)}, u32[]{:S(2)}, u32[]{:S(2)}) collective-permute-start(f16[640,128]{1,0:T(8,128)(2,1)S(1)} %convert_element_type.48), channel_id=1, source_target_pairs={{0,4},{1,5},{2,6},{3,7},{4,0},{5,1},{6,2},{7,3},{8,12},{9,13},{10,... | collective-permute-start | bytes 491528 | tf_op jit(solution)/shard_map/ppermute | solution.py:542
  37.1 8.0 %copy-start.1 = (bf16[4,512,512]{2,1,0:T(8,128)(2,1)S(1)}, bf16[4,512,512]{2,1,0:T(8,128)(2,1)}, u32[]{:S(2)}) copy-start(bf16[4,512,512]{2,1,0:T(8,128)(2,1)} %get-tuple-element.119.k_ref) | copy-start | bytes 6291460
  37.1 8.0 %copy-start.4 = (bf16[2,4,256,256]{3,2,1,0:T(8,128)(2,1)S(1)}, bf16[2,4,256,256]{3,2,1,0:T(8,128)(2,1)}, u32[]{:S(2)}) copy-start(bf16[2,4,256,256]{3,2,1,0:T(8,128)(2,1)} %get-tuple-element.121.xy_ref) | copy-start | bytes 3145732
  37.1 8.0 %copy-start.7 = (bf16[4,256,256]{2,1,0:T(8,128)(2,1)S(1)}, bf16[4,256,256]{2,1,0:T(8,128)(2,1)}, u32[]{:S(2)}) copy-start(bf16[4,256,256]{2,1,0:T(8,128)(2,1)} %get-tuple-element.120.y_ref) | copy-start | bytes 1572868
  37.1 8.0 %copy-start.10 = (bf16[2,32,512]{2,1,0:T(8,128)(2,1)S(1)}, bf16[2,32,512]{2,1,0:T(8,128)(2,1)}, u32[]{:S(2)}) copy-start(bf16[2,32,512]{2,1,0:T(8,128)(2,1)} %get-tuple-element.122.z_ref) | copy-start | bytes 196612
  41.9 6.6 %collective-permute-start.5 = (f16[656,128]{1,0:T(8,128)(2,1)S(1)}, f16[656,128]{1,0:T(8,128)(2,1)S(1)}, u32[]{:S(2)}, u32[]{:S(2)}) collective-permute-start(f16[656,128]{1,0:T(8,128)(2,1)S(1)} %convert_element_type.53), channel_id=1, source_target_pairs={{0,1},{1,0},{2,3},{3,2},{4,8},{5,9},{6,10},{7,11},{8,4},{9,5},{10,... | collective-permute-start | bytes 503816 | tf_op jit(solution)/shard_map/ppermute | solution.py:546
  45.1 1.7 %copy-start = (bf16[4,512,512]{2,1,0:T(8,128)(2,1)S(1)}, bf16[4,512,512]{2,1,0:T(8,128)(2,1)}, u32[]{:S(2)}) copy-start(bf16[4,512,512]{2,1,0:T(8,128)(2,1)} %get-tuple-element.113.k_ref) | copy-start | bytes 6291460
  45.1 1.8 %copy-start.3 = (bf16[2,4,256,256]{3,2,1,0:T(8,128)(2,1)S(1)}, bf16[2,4,256,256]{3,2,1,0:T(8,128)(2,1)}, u32[]{:S(2)}) copy-start(bf16[2,4,256,256]{3,2,1,0:T(8,128)(2,1)} %get-tuple-element.115.xy_ref) | copy-start | bytes 3145732
  45.1 2.0 %copy-start.6 = (bf16[4,256,256]{2,1,0:T(8,128)(2,1)S(1)}, bf16[4,256,256]{2,1,0:T(8,128)(2,1)}, u32[]{:S(2)}) copy-start(bf16[4,256,256]{2,1,0:T(8,128)(2,1)} %get-tuple-element.114.y_ref) | copy-start | bytes 1572868
  45.1 2.0 %copy-start.9 = (bf16[2,32,512]{2,1,0:T(8,128)(2,1)S(1)}, bf16[2,32,512]{2,1,0:T(8,128)(2,1)}, u32[]{:S(2)}) copy-start(bf16[2,32,512]{2,1,0:T(8,128)(2,1)} %get-tuple-element.116.z_ref) | copy-start | bytes 196612
  46.7 1.8 %collective-permute-start.4 = (f16[656,128]{1,0:T(8,128)(2,1)S(1)}, f16[656,128]{1,0:T(8,128)(2,1)S(1)}, u32[]{:S(2)}, u32[]{:S(2)}) collective-permute-start(f16[656,128]{1,0:T(8,128)(2,1)S(1)} %convert_element_type.51), channel_id=1, source_target_pairs={{0,4},{1,5},{2,6},{3,7},{4,0},{5,1},{6,2},{7,3},{8,12},{9,13},{10,... | collective-permute-start | bytes 503816 | tf_op jit(solution)/shard_map/ppermute | solution.py:542
  49.4 4.9 %collective-permute-start.6 = (f32[128,128]{1,0:T(8,128)S(1)}, f32[128,128]{1,0:T(8,128)S(1)}, u32[]{:S(2)}, u32[]{:S(2)}) collective-permute-start(f32[128,128]{1,0:T(8,128)S(1)} %get-tuple-element.142.up_ref), channel_id=1, source_target_pairs={{0,1},{1,0},{2,3},{3,2},{4,5},{5,4},{6,7},{7,6},{8,9},{9,8},{10,11... | collective-permute-start | bytes 196616 | tf_op jit(solution)/shard_map/ppermute | solution.py:542
  51.4 2.9 %collective-permute-start.7 = (f32[128,128]{1,0:T(8,128)S(1)}, f32[128,128]{1,0:T(8,128)S(1)}, u32[]{:S(2)}, u32[]{:S(2)}) collective-permute-start(f32[128,128]{1,0:T(8,128)S(1)} %get-tuple-element.143.down_ref), channel_id=1, source_target_pairs={{0,4},{1,2},{2,1},{3,7},{4,0},{5,6},{6,5},{7,3},{8,12},{9,10},{10,... | collective-permute-start | bytes 196616 | tf_op jit(solution)/shard_map/ppermute | solution.py:546
  55.1 3.8 %collective-permute-start.8 = (f16[656,128]{1,0:T(8,128)(2,1)S(1)}, f16[656,128]{1,0:T(8,128)(2,1)S(1)}, u32[]{:S(2)}, u32[]{:S(2)}) collective-permute-start(f16[656,128]{1,0:T(8,128)(2,1)S(1)} %convert_element_type.55), channel_id=1, source_target_pairs={{0,4},{1,5},{2,6},{3,7},{4,0},{5,1},{6,2},{7,3},{8,12},{9,13},{10,... | collective-permute-start | bytes 503816 | tf_op jit(solution)/shard_map/ppermute | solution.py:542
  55.4 5.6 %collective-permute-start.9 = (f16[656,128]{1,0:T(8,128)(2,1)S(1)}, f16[656,128]{1,0:T(8,128)(2,1)S(1)}, u32[]{:S(2)}, u32[]{:S(2)}) collective-permute-start(f16[656,128]{1,0:T(8,128)(2,1)S(1)} %convert_element_type.55), channel_id=1, source_target_pairs={{0,1},{1,0},{2,3},{3,2},{4,8},{5,9},{6,10},{7,11},{8,4},{9,5},{10,... | collective-permute-start | bytes 503816 | tf_op jit(solution)/shard_map/ppermute | solution.py:546
  59.0 2.1 %copy-start.2 = (bf16[4,512,512]{2,1,0:T(8,128)(2,1)S(1)}, bf16[4,512,512]{2,1,0:T(8,128)(2,1)}, u32[]{:S(2)}) copy-start(bf16[4,512,512]{2,1,0:T(8,128)(2,1)} %get-tuple-element.107.refs_2_.ka_ref) | copy-start | bytes 6291460
  59.0 2.1 %copy-start.5 = (bf16[2,4,256,256]{3,2,1,0:T(8,128)(2,1)S(1)}, bf16[2,4,256,256]{3,2,1,0:T(8,128)(2,1)}, u32[]{:S(2)}) copy-start(bf16[2,4,256,256]{3,2,1,0:T(8,128)(2,1)} %get-tuple-element.109.refs_4_.xya_ref) | copy-start | bytes 3145732
  59.0 2.1 %copy-start.8 = (bf16[4,256,256]{2,1,0:T(8,128)(2,1)S(1)}, bf16[4,256,256]{2,1,0:T(8,128)(2,1)}, u32[]{:S(2)}) copy-start(bf16[4,256,256]{2,1,0:T(8,128)(2,1)} %get-tuple-element.108.refs_3_.ya_ref) | copy-start | bytes 1572868
  59.1 2.1 %copy-start.11 = (bf16[2,32,512]{2,1,0:T(8,128)(2,1)S(1)}, bf16[2,32,512]{2,1,0:T(8,128)(2,1)}, u32[]{:S(2)}) copy-start(bf16[2,32,512]{2,1,0:T(8,128)(2,1)} %get-tuple-element.110.refs_5_.za_ref) | copy-start | bytes 196612
  64.6 5.4 %collective-permute-start.11 = (f16[656,128]{1,0:T(8,128)(2,1)S(1)}, f16[656,128]{1,0:T(8,128)(2,1)S(1)}, u32[]{:S(2)}, u32[]{:S(2)}) collective-permute-start(f16[656,128]{1,0:T(8,128)(2,1)S(1)} %convert_element_type.60), channel_id=1, source_target_pairs={{0,1},{1,0},{2,3},{3,2},{4,8},{5,9},{6,10},{7,11},{8,4},{9,5},{10,... | collective-permute-start | bytes 503816 | tf_op jit(solution)/shard_map/ppermute | solution.py:546
  67.8 2.3 %collective-permute-start.10 = (f16[656,128]{1,0:T(8,128)(2,1)S(1)}, f16[656,128]{1,0:T(8,128)(2,1)S(1)}, u32[]{:S(2)}, u32[]{:S(2)}) collective-permute-start(f16[656,128]{1,0:T(8,128)(2,1)S(1)} %convert_element_type.58), channel_id=1, source_target_pairs={{0,4},{1,5},{2,6},{3,7},{4,0},{5,1},{6,2},{7,3},{8,12},{9,13},{10,... | collective-permute-start | bytes 503816 | tf_op jit(solution)/shard_map/ppermute | solution.py:542
  70.2 4.3 %collective-permute-start.12 = (f32[64,128]{1,0:T(8,128)S(1)}, f32[64,128]{1,0:T(8,128)S(1)}, u32[]{:S(2)}, u32[]{:S(2)}) collective-permute-start(f32[64,128]{1,0:T(8,128)S(1)} %get-tuple-element.165), channel_id=1, source_target_pairs={{0,1},{1,0},{2,3},{3,2},{4,5},{5,4},{6,7},{7,6},{8,9},{9,8},{10,11... | collective-permute-start | bytes 98312 | tf_op jit(solution)/shard_map/ppermute | solution.py:542
  71.6 2.9 %collective-permute-start.13 = (f32[64,128]{1,0:T(8,128)S(1)}, f32[64,128]{1,0:T(8,128)S(1)}, u32[]{:S(2)}, u32[]{:S(2)}) collective-permute-start(f32[64,128]{1,0:T(8,128)S(1)} %get-tuple-element.166), channel_id=1, source_target_pairs={{0,4},{1,2},{2,1},{3,7},{4,0},{5,6},{6,5},{7,3},{8,12},{9,10},{10,... | collective-permute-start | bytes 98312 | tf_op jit(solution)/shard_map/ppermute | solution.py:546

commit v6 on v5

--- a/solution.py
+++ b/solution.py
@@ -135,10 +135,10 @@
     return jnp.where(jnp.abs(off) <= RADIUS, table, 0.0)
 
 
-def build_forward_kernel(taps_ref, back_ref, *held):
+def build_forward_kernel(order, taps_ref, back_ref, *held):
     each, tiled = selectors(NZ, BX)
     each16, tiled16 = selectors(STRIP, BX)
-    for n, xr in enumerate(ORDER):
+    for n, xr in enumerate(order):
         k_ref, y_ref, xy_ref, z_ref = held[4 * n : 4 * n + 4]
         for v in range(V):
             def fwd(yr, e):
@@ -639,7 +639,7 @@
     forward_shapes = shapes((3 * BY, V * BY), (V * NZ, LANES))
     adjoint_shapes = shapes((V, 2 * BY, 2 * BY), (NZ, V * LANES))
     sems = [pltpu.SemaphoreType.DMA((4 * ROLES,))]
-    forward = call(build_forward_kernel, forward_shapes, taps, backward, cost=3.0)
+    forward = call(functools.partial(build_forward_kernel, ORDER), forward_shapes, taps, backward, cost=3.0)
     adjoint = call(
         build_adjoint_kernel, adjoint_shapes, taps, backward,
         out_place=HBM, scratch=held(adjoint_shapes) + sems, cost=4.0,
@@ -685,9 +685,11 @@
     )
     up_in, down_in = swap("gy", up, down)
     taps, backward, up, down = lax.optimization_barrier((taps, backward, up, down))
-    forward = call(build_forward_kernel, forward_shapes, taps, backward)
+    forward = call(
+        functools.partial(build_forward_kernel, ORDER[1:]), forward_shapes[4:], taps, backward
+    )
     old, *forward = lax.optimization_barrier((old, *forward))
-    forward_far, forward_near, forward_center = forward[:4], forward[4:8], forward[8:]
+    forward_near, forward_center = forward[:4], forward[4:]
     new, new_scaled = call(
         update_kernel, [(message, f32), (scaled, f32)],
         info, old, total, up, down, up_in, down_in, scalars=1,
@@ -697,6 +699,10 @@
     (blurred,) = call(forward_center_kernel, [(every, f32)], info, new, *forward_center, scalars=1, cost=QUICK)
     (blurred,) = call(
         forward_near_kernel, [(every, f32)], info, blurred, near.astype(f32), *forward_near, scalars=1, cost=QUICK
+    )
+    taps, backward, blurred = lax.optimization_barrier((taps, backward, blurred))
+    forward_far = call(
+        functools.partial(build_forward_kernel, ORDER[:1]), forward_shapes[:4], taps, backward
     )
     quotient, edge, far = call(
         middle_kernel, [(every, f32), edges, (scaled, f32)],

time: 77.5 us -> 77.7 us (level)
  waiting for transfers between devices: 7.61 us -> 9.24 us
  starting transfers between devices: 20.8 us -> 19.7 us
    ppermute x7, starting transfers between devices: 7.02 us -> 5.93 us  [swap_near(): lax.ppermute(narrow(axis, value), ('gx', 'gy'), partner_swaps(axis)[0])]
    ppermute x7, waiting for transfers between devices: 1.98 us -> 2.86 us  [swap_far(): lax.ppermute(narrow(axis, value), ('gx', 'gy'), partner_swaps(axis)[1])]
    ppermute x7, waiting for transfers between devices: 2.94 us -> 3.72 us  [swap_near(): lax.ppermute(narrow(axis, value), ('gx', 'gy'), partner_swaps(axis)[0])]
    pallas_call x21 -> x22, Pallas kernels: 44.9 us -> 44.9 us  [call(): pl.pallas_call(kernel, out_shape=[HBM(s, d) if where is HBM else jax.Shap...]
where the time goes in v6:
time: 77.7 us; the launch traced here: 77 us
  Pallas kernels  44.9 us (58%)
  starting transfers between devices  19.7 us (25%)
  waiting for transfers between devices  9.24 us (12%)
  local copies, waits for them, and re-layouts  1.28 us (2%)
  other arithmetic  0.8 us (1%)
  between operations  0.79 us (1%)
    pallas_call x22, Pallas kernels, call(): pl.pallas_call(kernel, out_shape=[HBM(s, d) if where is HBM else jax.Shap...  44.9 us
    ppermute x7, starting transfers between devices, swap_far(): lax.ppermute(narrow(axis, value), ('gx', 'gy'), partner_swaps(axis)[1])  8.36 us
    ppermute x7, starting transfers between devices, swap_near(): lax.ppermute(narrow(axis, value), ('gx', 'gy'), partner_swaps(axis)[0])  5.93 us
    all_to_all x1, starting transfers between devices, shards(): lax.all_to_all(outgoing.reshape(devices, cap, plane), ('gx', 'gy'), split...  5.4 us
    ppermute x7, waiting for transfers between devices, swap_near(): lax.ppermute(narrow(axis, value), ('gx', 'gy'), partner_swaps(axis)[0])  3.72 us
    ppermute x7, waiting for transfers between devices, swap_far(): lax.ppermute(narrow(axis, value), ('gx', 'gy'), partner_swaps(axis)[1])  2.86 us
    all_to_all x1, waiting for transfers between devices, shards(): lax.all_to_all(outgoing.reshape(devices, cap, plane), ('gx', 'gy'), split...  2.66 us
  transfers between devices with their start and end apart: 15, of which 5 were waited for; matrix products, arithmetic and copies ran while one was open for 2% of the time, Pallas kernels for 41%

profile of v6, /device:TPU:0, one launch (start us, length us, event | category | flops | bytes accessed | tf_op | source)
XLA Modules:
  0.0 77.0 jit_solution(9944537520787255083)
XLA Ops:
  0.1 1.8 %shard_map.55 = (f32[512,128]{1,0:T(8,128)S(1)}, f32[64,128]{1,0:T(8,128)S(1)}, f32[64,128]{1,0:T(8,128)S(1)}, s32[32,128]{1,0:T(8,128)S(1)}, bf16[128,16,128]{2,1,0:T(8,128)(2,1)S(1)}) custom-call(s32[2]{0:T(128)S(1)} %pad_add_fusion.info_ref, f32[32,16,128]{2,1,0:T(8,128)} %refs_0_.1, s32[32,128]{1,0:T(8,128)} %bitcast.9, bf16[128,16,128]{2,1,0:T(8,128)(2,1)} %refs_2_.1), custom_call_target="tpu_custom_call" | custom-call | bytes 70000 | tf_op jit(solution)/shard_map/pallas_call | solution.py:506
  1.9 3.1 %collective-permute-start = (f32[64,128]{1,0:T(8,128)S(1)}, f32[64,128]{1,0:T(8,128)S(1)}, u32[]{:S(2)}, u32[]{:S(2)}) collective-permute-start(f32[64,128]{1,0:T(8,128)S(1)} %get-tuple-element.86), channel_id=1, source_target_pairs={{0,1},{1,0},{2,3},{3,2},{4,5},{5,4},{6,7},{7,6},{8,9},{9,8},{10,11... | collective-permute-start | bytes 98312 | tf_op jit(solution)/shard_map/ppermute | solution.py:542
  5.0 1.6 %shard_map.56 = bf16[256,2048]{1,0:T(8,128)(2,1)} custom-call(s32[1]{0:T(128)} %bitcast.3.me_ref, s32[32,128]{1,0:T(8,128)S(1)} %get-tuple-element.88.slots_ref, bf16[128,16,128]{2,1,0:T(8,128)(2,1)S(1)} %get-tuple-element.89.stored_ref), custom_call_target="tpu_custom_call" | custom-call | bytes 70000 | tf_op jit(solution)/shard_map/pallas_call | solution.py:506
  6.6 5.4 %all-to-all-start = ((bf16[32,8,2048]{2,1,0:T(8,128)(2,1)}), bf16[32,8,2048]{2,1,0:T(8,128)(2,1)S(1)}, u32[]{:S(2)}, u32[]{:S(2)}) async-start(bf16[32,8,2048]{2,1,0:T(8,128)(2,1)} %bitcast.4), calls=%async_computation | async-start | bytes 2097152 | tf_op jit(solution)/shard_map/all_to_all | solution.py:623
  13.7 2.5 %shard_map.58 = (bf16[4,512,512]{2,1,0:T(8,128)(2,1)S(1)}, bf16[384,512]{1,0:T(8,128)(2,1)S(1)}, bf16[2,4,256,256]{3,2,1,0:T(8,128)(2,1)S(1)}, bf16[2,128,128]{2...) custom-call(f32[108,128]{1,0:T(8,128)S(1)} %get-tuple-element.151.ta, ...), custom_call_target="tpu_custom_call" | custom-call | bytes 10500000 | tf_op jit(solution)/shard_map/pallas_call | solution.py:506
  16.2 7.0 %shard_map.62 = (bf16[4,512,512]{2,1,0:T(8,128)(2,1)}, bf16[4,256,256]{2,1,0:T(8,128)(2,1)}, bf16[2,4,256,256]{3,2,1,0:T(8,128)(2,1)}, bf16[2,32,512]{2,1,0:T(8,...) custom-call(f32[108,128]{1,0:T(8,128)S(1)} %get-tuple-element.151.ta, ...), custom_call_target="tpu_custom_call" | custom-call | bytes 14000000 | tf_op jit(solution)/shard_map/pallas_call | solution.py:506
  23.3 1.8 %collective-permute-start.3 = (f16[640,128]{1,0:T(8,128)(2,1)S(1)}, f16[640,128]{1,0:T(8,128)(2,1)S(1)}, u32[]{:S(2)}, u32[]{:S(2)}) collective-permute-start(f16[640,128]{1,0:T(8,128)(2,1)S(1)} %convert_element_type.48), channel_id=1, source_target_pairs={{0,1},{1,0},{2,3},{3,2},{4,8},{5,9},{6,10},{7,11},{8,4},{9,5},{10,... | collective-permute-start | bytes 491528 | tf_op jit(solution)/shard_map/ppermute | solution.py:546
  25.3 1.0 %shard_map.57.refs_0_ = bf16[128,256]{1,0:T(8,128)(2,1)} custom-call(s32[1]{0:T(128)} %bitcast.3.me_ref, s32[256,128]{1,0:T(8,128)S(1)} %broadcast_bitcast_fusion.slots_ref), custom_call_target="tpu_custom_call" | custom-call | bytes 70000 | tf_op jit(solution)/shard_map/pallas_call | solution.py:506
  26.2 1.9 %shard_map.59.refs_0_ = f32[4,512,128]{2,1,0:T(8,128)S(1)} custom-call(s32[2]{0:T(128)S(1)} %pad_add_fusion.info_ref, f32[640,128]{1,0:T(8,128)S(1)} %constant_dynamic-update-slice_fusion.refs_0_.old_ref, bf16[4,512,512]{2,1,0:T(8,128)(2,1)S(1)} %get-tuple-element.94.refs_1_, bf16[384,512]{1,0:T(8,128)(2,1)S(1)} %get-tuple-element.95.refs_2_, ...), custom_call_target="tpu_custom_call" | custom-call | bytes 70000 | tf_op jit(solution)/shard_map/pallas_call | solution.py:506
  28.2 2.0 %shard_map.60.blurred_ref = f32[4,512,128]{2,1,0:T(8,128)S(1)} custom-call(s32[2]{0:T(128)S(1)} %pad_add_fusion.info_ref, f32[4,512,128]{2,1,0:T(8,128)S(1)} %shard_map.59.refs_0_, f32[640,128]{1,0:T(8,128)S(1)} %convert_element_type.49.refs_1_, bf16[4,512,512]{2,1,0:T(8,128)(2,1)S(1)} %get-tuple-element.98.refs_2_, ...), custom_call_target="tpu_custom_call" | custom-call | bytes 70000 | tf_op jit(solution)/shard_map/pallas_call | solution.py:506
  30.2 1.2 %collective-permute-done.3 = f16[640,128]{1,0:T(8,128)(2,1)S(1)} collective-permute-done((f16[640,128]{1,0:T(8,128)(2,1)S(1)}, f16[640,128]{1,0:T(8,128)(2,1)S(1)}, u32[]{:S(2)}, u32[]{:S(2)}) %collective-permute-start.3) | collective-permute-done | bytes 163872 | tf_op jit(solution)/shard_map/ppermute | solution.py:546
  31.4 3.0 %shard_map.61.refs_1_ = f32[4,512,128]{2,1,0:T(8,128)} custom-call(s32[2]{0:T(128)S(1)} %pad_add_fusion.info_ref, f32[4,512,128]{2,1,0:T(8,128)S(1)} %shard_map.60.blurred_ref, f32[640,128]{1,0:T(8,128)S(1)} %convert_element_type.50.message_ref, bf16[4,512,512]{2,1,0:T(8,128)(2,1)S(1)} %get-tuple-element.102.k_ref, ...), custom_call_target="tpu_custom_call" | custom-call | bytes 70000 | tf_op jit(solution)/shard_map/pallas_call | solution.py:506
  34.4 2.7 %all-to-all-done = bf16[32,8,2048]{2,1,0:T(8,128)(2,1)S(1)} async-done(((bf16[32,8,2048]{2,1,0:T(8,128)(2,1)}), bf16[32,8,2048]{2,1,0:T(8,128)(2,1)S(1)}, u32[]{:S(2)}, u32[]{:S(2)}) %all-to-all-start) | async-done | bytes 1048608 | tf_op jit(solution)/shard_map/all_to_all | solution.py:623
  37.1 4.8 %shard_map.63 = (bf16[4,512,128]{2,1,0:T(8,128)(2,1)S(1)}, f32[4,512,128]{2,1,0:T(8,128)S(1)}, f32[4,2,64,128]{3,2,1,0:T(8,128)S(1)}, f32[656,128]{1,0:T(8,128)S(1)}) custom-call(s32[2]{0:T(128)S(1)} %pad_add_fusion.info_ref, bf16[256,2048]{1,0:T(8,128)(2,1)S(1)} %bitcast.8, bf16[128,256]{1,0:T(8,128)(2,1)} %shard_map.57.refs_0_, ...), custom_call_target="tpu_custom_call" | custom-call | bytes 70000 | tf_op jit(solution)/shard_map/pallas_call | solution.py:506
  41.9 3.2 %collective-permute-start.5 = (f16[656,128]{1,0:T(8,128)(2,1)S(1)}, f16[656,128]{1,0:T(8,128)(2,1)S(1)}, u32[]{:S(2)}, u32[]{:S(2)}) collective-permute-start(f16[656,128]{1,0:T(8,128)(2,1)S(1)} %convert_element_type.53), channel_id=1, source_target_pairs={{0,1},{1,0},{2,3},{3,2},{4,8},{5,9},{6,10},{7,11},{8,4},{9,5},{10,... | collective-permute-start | bytes 503816 | tf_op jit(solution)/shard_map/ppermute | solution.py:546
  45.1 1.5 %shard_map.65 = f32[656,128]{1,0:T(8,128)S(1)} custom-call(f32[4,512,128]{2,1,0:T(8,128)S(1)} %get-tuple-element.110.quotient_ref, f32[4,2,64,128]{3,2,1,0:T(8,128)S(1)} %get-tuple-element.111.edge_ref, bf16[4,512,512]{2,1,0:T(8,128)(2,1)S(1)} %copy-done.1, bf16[4,256,256]{2,1,0:T(8,128)(2,1)S(1)} %copy-done.7, bf16[2,4,256,256]{3,2,1,0:T(8,128)(2,1)S(1)} %copy-done.4, ...), custom_call_target="tpu_custom_call" | custom-call | bytes 70000 | tf_op jit(solution)/shard_map/pallas_call | solution.py:506
  47.1 1.4 %shard_map.64 = (f32[512,128]{1,0:T(8,128)S(1)}, f32[2,64,128]{2,1,0:T(8,128)S(1)}) custom-call(f32[4,512,128]{2,1,0:T(8,128)S(1)} %get-tuple-element.110.quotient_ref, f32[4,2,64,128]{3,2,1,0:T(8,128)S(1)} %get-tuple-element.111.edge_ref, bf16[4,512,512]{2,1,0:T(8,128)(2,1)S(1)} %copy-done, bf16[4,256,256]{2,1,0:T(8,128)(2,1)S(1)} %copy-done.6, ...), custom_call_target="tpu_custom_call" | custom-call | bytes 70000 | tf_op jit(solution)/shard_map/pallas_call | solution.py:506
  49.4 2.0 %collective-permute-start.6 = (f32[128,128]{1,0:T(8,128)S(1)}, f32[128,128]{1,0:T(8,128)S(1)}, u32[]{:S(2)}, u32[]{:S(2)}) collective-permute-start(f32[128,128]{1,0:T(8,128)S(1)} %get-tuple-element.137.up_ref), channel_id=1, source_target_pairs={{0,1},{1,0},{2,3},{3,2},{4,5},{5,4},{6,7},{7,6},{8,9},{9,8},{10,11... | collective-permute-start | bytes 196616 | tf_op jit(solution)/shard_map/ppermute | solution.py:542
  51.4 1.6 %shard_map.67 = (bf16[4,512,512]{2,1,0:T(8,128)(2,1)S(1)}, bf16[384,512]{1,0:T(8,128)(2,1)S(1)}, bf16[2,4,256,256]{3,2,1,0:T(8,128)(2,1)S(1)}, bf16[2,128,128]{2...) custom-call(f32[108,128]{1,0:T(8,128)S(1)} %get-tuple-element.151.ta, ...), custom_call_target="tpu_custom_call" | custom-call | bytes 70000 | tf_op jit(solution)/shard_map/pallas_call | solution.py:506
  53.0 1.2 %collective-permute-done.6.up_in_ref = f32[128,128]{1,0:T(8,128)S(1)} collective-permute-done((f32[128,128]{1,0:T(8,128)S(1)}, f32[128,128]{1,0:T(8,128)S(1)}, u32[]{:S(2)}, u32[]{:S(2)}) %collective-permute-start.6) | collective-permute-done | bytes 65568 | tf_op jit(solution)/shard_map/ppermute | solution.py:542
  54.2 0.9 %shard_map.68 = (f32[640,128]{1,0:T(8,128)S(1)}, f32[656,128]{1,0:T(8,128)S(1)}) custom-call(s32[2]{0:T(128)S(1)} %pad_add_fusion.info_ref, f32[640,128]{1,0:T(8,128)S(1)} %constant_dynamic-update-slice_fusion.refs_0_.old_ref, f32[512,128]{1,0:T(8,128)S(1)} %get-tuple-element.136.total_ref, f32[128,128]{1,0:T(8,128)S(1)} %get-tuple-element.137.up_ref, ...), custom_call_target="tpu_custom_call" | custom-call | bytes 70000 | tf_op jit(solution)/shard_map/pallas_call | solution.py:506
  55.2 1.8 %collective-permute-start.9 = (f16[656,128]{1,0:T(8,128)(2,1)S(1)}, f16[656,128]{1,0:T(8,128)(2,1)S(1)}, u32[]{:S(2)}, u32[]{:S(2)}) collective-permute-start(f16[656,128]{1,0:T(8,128)(2,1)S(1)} %convert_element_type.55), channel_id=1, source_target_pairs={{0,1},{1,0},{2,3},{3,2},{4,8},{5,9},{6,10},{7,11},{8,4},{9,5},{10,... | collective-permute-start | bytes 503816 | tf_op jit(solution)/shard_map/ppermute | solution.py:546
  57.0 1.9 %shard_map.69.blurred_ref = f32[4,512,128]{2,1,0:T(8,128)S(1)} custom-call(s32[2]{0:T(128)S(1)} %pad_add_fusion.info_ref, f32[640,128]{1,0:T(8,128)S(1)} %get-tuple-element.139.own_ref.old_ref, bf16[4,512,512]{2,1,0:T(8,128)(2,1)S(1)} %get-tuple-element.141.k_ref, bf16[384,512]{1,0:T(8,128)(2,1)S(1)} %get-tuple-element.142.y_ref, ...), custom_call_target="tpu_custom_call" | custom-call | bytes 70000 | tf_op jit(solution)/shard_map/pallas_call | solution.py:506
  59.1 2.0 %shard_map.70.blurred_ref = f32[4,512,128]{2,1,0:T(8,128)S(1)} custom-call(s32[2]{0:T(128)S(1)} %pad_add_fusion.info_ref, f32[4,512,128]{2,1,0:T(8,128)S(1)} %shard_map.69.blurred_ref, f32[656,128]{1,0:T(8,128)S(1)} %convert_element_type.56.near_ref, bf16[4,512,512]{2,1,0:T(8,128)(2,1)S(1)} %get-tuple-element.146.k_ref, ...), custom_call_target="tpu_custom_call" | custom-call | bytes 70000 | tf_op jit(solution)/shard_map/pallas_call | solution.py:506
  61.0 0.9 %shard_map.71 = (bf16[4,512,512]{2,1,0:T(8,128)(2,1)S(1)}, bf16[384,512]{1,0:T(8,128)(2,1)S(1)}, bf16[2,4,256,256]{3,2,1,0:T(8,128)(2,1)S(1)}, bf16[2,128,128]{2,1,0:T(8,128)(2,1)S(1)}) custom-call(f32[108,128]{1,0:T(8,128)S(1)} %get-tuple-element.151.taps_ref, f32[108,128]{1,0:T(8,128)S(1)} %get-tuple-element.152.back_ref), custom_call_target="tpu_custom_call" | custom-call | bytes 70000 | tf_op jit(solution)/shard_map/pallas_call | solution.py:506
  62.1 3.4 %shard_map.72 = (f32[4,512,128]{2,1,0:T(8,128)S(1)}, f32[4,2,64,128]{3,2,1,0:T(8,128)S(1)}, f32[656,128]{1,0:T(8,128)S(1)}) custom-call(s32[2]{0:T(128)S(1)} %pad_add_fusion.info_ref, bf16[4,512,128]{2,1,0:T(8,128)(2,1)S(1)} %get-tuple-element.140.data_ref, f32[4,512,128]{2,1,0:T(8,128)S(1)} %shard_map.70.blurred_ref, ...), custom_call_target="tpu_custom_call" | custom-call | bytes 70000 | tf_op jit(solution)/shard_map/pallas_call | solution.py:506
  66.0 1.7 %shard_map.74 = f32[656,128]{1,0:T(8,128)S(1)} custom-call(f32[4,512,128]{2,1,0:T(8,128)S(1)} %get-tuple-element.157.quotient_ref, f32[4,2,64,128]{3,2,1,0:T(8,128)S(1)} %get-tuple-element.158.edge_ref, bf16[4,512,512]{2,1,0:T(8,128)(2,1)S(1)} %copy-done.1, bf16[4,256,256]{2,1,0:T(8,128)(2,1)S(1)} %copy-done.7, bf16[2,4,256,256]{3,2,1,0:T(8,128)(2,1)S(1)} %copy-done.4, ...), custom_call_target="tpu_custom_call" | custom-call | bytes 70000 | tf_op jit(solution)/shard_map/pallas_call | solution.py:506
  67.9 1.4 %shard_map.73 = (f32[512,128]{1,0:T(8,128)S(1)}, f32[2,64,128]{2,1,0:T(8,128)S(1)}) custom-call(f32[4,512,128]{2,1,0:T(8,128)S(1)} %get-tuple-element.157.quotient_ref, f32[4,2,64,128]{3,2,1,0:T(8,128)S(1)} %get-tuple-element.158.edge_ref, bf16[4,512,512]{2,1,0:T(8,128)(2,1)S(1)} %copy-done, bf16[4,256,256]{2,1,0:T(8,128)(2,1)S(1)} %copy-done.6, ...), custom_call_target="tpu_custom_call" | custom-call | bytes 70000 | tf_op jit(solution)/shard_map/pallas_call | solution.py:506
  69.3 1.6 %collective-permute-done.11 = f16[656,128]{1,0:T(8,128)(2,1)S(1)} collective-permute-done((f16[656,128]{1,0:T(8,128)(2,1)S(1)}, f16[656,128]{1,0:T(8,128)(2,1)S(1)}, u32[]{:S(2)}, u32[]{:S(2)}) %collective-permute-start.11) | collective-permute-done | bytes 167968 | tf_op jit(solution)/shard_map/ppermute | solution.py:546
  71.6 1.1 %collective-permute-start.13 = (f32[64,128]{1,0:T(8,128)S(1)}, f32[64,128]{1,0:T(8,128)S(1)}, u32[]{:S(2)}, u32[]{:S(2)}) collective-permute-start(f32[64,128]{1,0:T(8,128)S(1)} %get-tuple-element.164), channel_id=1, source_target_pairs={{0,4},{1,2},{2,1},{3,7},{4,0},{5,6},{6,5},{7,3},{8,12},{9,10},{10,... | collective-permute-start | bytes 98312 | tf_op jit(solution)/shard_map/ppermute | solution.py:546
  72.7 2.5 %collective-permute-done.12.up_in_ref = f32[64,128]{1,0:T(8,128)S(1)} collective-permute-done((f32[64,128]{1,0:T(8,128)S(1)}, f32[64,128]{1,0:T(8,128)S(1)}, u32[]{:S(2)}, u32[]{:S(2)}) %collective-permute-start.12) | collective-permute-done | bytes 32800 | tf_op jit(solution)/shard_map/ppermute | solution.py:542
  75.2 1.6 %shard_map.76 = f32[32,16,128]{2,1,0:T(8,128)} custom-call(s32[2]{0:T(128)S(1)} %pad_add_fusion.info_ref, f32[640,128]{1,0:T(8,128)S(1)} %get-tuple-element.139.own_ref.old_ref, f32[512,128]{1,0:T(8,128)S(1)} %get-tuple-element.162.total_ref, f32[64,128]{1,0:T(8,128)S(1)} %collective-permute-done.12.up_in_ref, f32[64,128]{1,0:T(8,128)S(1)} %collective-permute-done.13.down_in_ref), custom_call_target="tpu_custom_call" | custom-call | bytes 70000 | tf_op jit(solution)/shard_map/pallas_call | solution.py:506
  (87 shorter events, 4.6 us)
Async XLA Ops:
  0.1 12.0 %copy-start.12 = (s32[8,4,4,3]{0,2,3,1:T(4,128)S(1)}, s32[8,4,4,3]{0,2,3,1:T(4,128)}, u32[]{:S(2)}) copy-start(s32[8,4,4,3]{0,2,3,1:T(4,128)} %param.9) | copy-start | bytes 4612
  1.9 10.8 %copy-start.14 = (f32[48,31]{0,1:T(8,128)S(1)}, f32[48,31]{0,1:T(8,128)}, u32[]{:S(2)}) copy-start(f32[48,31]{0,1:T(8,128)} %param.8) | copy-start | bytes 17860
  1.9 21.3 %collective-permute-start = (f32[64,128]{1,0:T(8,128)S(1)}, f32[64,128]{1,0:T(8,128)S(1)}, u32[]{:S(2)}, u32[]{:S(2)}) collective-permute-start(f32[64,128]{1,0:T(8,128)S(1)} %get-tuple-element.86), channel_id=1, source_target_pairs={{0,1},{1,0},{2,3},{3,2},{4,5},{5,4},{6,7},{7,6},{8,9},{9,8},{10,11... | collective-permute-start | bytes 98312 | tf_op jit(solution)/shard_map/ppermute | solution.py:542
  5.0 18.3 %collective-permute-start.1 = (f32[64,128]{1,0:T(8,128)S(1)}, f32[64,128]{1,0:T(8,128)S(1)}, u32[]{:S(2)}, u32[]{:S(2)}) collective-permute-start(f32[64,128]{1,0:T(8,128)S(1)} %get-tuple-element.87), channel_id=1, source_target_pairs={{0,4},{1,2},{2,1},{3,7},{4,0},{5,6},{6,5},{7,3},{8,12},{9,10},{10,... | collective-permute-start | bytes 98312 | tf_op jit(solution)/shard_map/ppermute | solution.py:546
  6.6 30.5 %all-to-all-start = ((bf16[32,8,2048]{2,1,0:T(8,128)(2,1)}), bf16[32,8,2048]{2,1,0:T(8,128)(2,1)S(1)}, u32[]{:S(2)}, u32[]{:S(2)}) async-start(bf16[32,8,2048]{2,1,0:T(8,128)(2,1)} %bitcast.4), calls=%async_computation | async-start | bytes 2097152 | tf_op jit(solution)/shard_map/all_to_all | solution.py:623
  12.0 13.2 %copy-start.13 = (s32[4096]{0:T(1024)S(1)}, s32[4096]{0:T(1024)}, u32[]{:S(2)}) copy-start(s32[4096]{0:T(1024)} %param.7) | copy-start | bytes 49156
  23.3 8.1 %collective-permute-start.3 = (f16[640,128]{1,0:T(8,128)(2,1)S(1)}, f16[640,128]{1,0:T(8,128)(2,1)S(1)}, u32[]{:S(2)}, u32[]{:S(2)}) collective-permute-start(f16[640,128]{1,0:T(8,128)(2,1)S(1)} %convert_element_type.48), channel_id=1, source_target_pairs={{0,1},{1,0},{2,3},{3,2},{4,8},{5,9},{6,10},{7,11},{8,4},{9,5},{10,... | collective-permute-start | bytes 491528 | tf_op jit(solution)/shard_map/ppermute | solution.py:546
  25.1 3.1 %collective-permute-start.2 = (f16[640,128]{1,0:T(8,128)(2,1)S(1)}, f16[640,128]{1,0:T(8,128)(2,1)S(1)}, u32[]{:S(2)}, u32[]{:S(2)}) collective-permute-start(f16[640,128]{1,0:T(8,128)(2,1)S(1)} %convert_element_type.48), channel_id=1, source_target_pairs={{0,4},{1,5},{2,6},{3,7},{4,0},{5,1},{6,2},{7,3},{8,12},{9,13},{10,... | collective-permute-start | bytes 491528 | tf_op jit(solution)/shard_map/ppermute | solution.py:542
  37.1 8.0 %copy-start.1 = (bf16[4,512,512]{2,1,0:T(8,128)(2,1)S(1)}, bf16[4,512,512]{2,1,0:T(8,128)(2,1)}, u32[]{:S(2)}) copy-start(bf16[4,512,512]{2,1,0:T(8,128)(2,1)} %get-tuple-element.118.k_ref) | copy-start | bytes 6291460
  37.1 8.0 %copy-start.4 = (bf16[2,4,256,256]{3,2,1,0:T(8,128)(2,1)S(1)}, bf16[2,4,256,256]{3,2,1,0:T(8,128)(2,1)}, u32[]{:S(2)}) copy-start(bf16[2,4,256,256]{3,2,1,0:T(8,128)(2,1)} %get-tuple-element.120.xy_ref) | copy-start | bytes 3145732
  37.1 8.0 %copy-start.7 = (bf16[4,256,256]{2,1,0:T(8,128)(2,1)S(1)}, bf16[4,256,256]{2,1,0:T(8,128)(2,1)}, u32[]{:S(2)}) copy-start(bf16[4,256,256]{2,1,0:T(8,128)(2,1)} %get-tuple-element.119.y_ref) | copy-start | bytes 1572868
  37.1 8.0 %copy-start.10 = (bf16[2,32,512]{2,1,0:T(8,128)(2,1)S(1)}, bf16[2,32,512]{2,1,0:T(8,128)(2,1)}, u32[]{:S(2)}) copy-start(bf16[2,32,512]{2,1,0:T(8,128)(2,1)} %get-tuple-element.121.z_ref) | copy-start | bytes 196612
  41.9 6.6 %collective-permute-start.5 = (f16[656,128]{1,0:T(8,128)(2,1)S(1)}, f16[656,128]{1,0:T(8,128)(2,1)S(1)}, u32[]{:S(2)}, u32[]{:S(2)}) collective-permute-start(f16[656,128]{1,0:T(8,128)(2,1)S(1)} %convert_element_type.53), channel_id=1, source_target_pairs={{0,1},{1,0},{2,3},{3,2},{4,8},{5,9},{6,10},{7,11},{8,4},{9,5},{10,... | collective-permute-start | bytes 503816 | tf_op jit(solution)/shard_map/ppermute | solution.py:546
  45.1 1.7 %copy-start = (bf16[4,512,512]{2,1,0:T(8,128)(2,1)S(1)}, bf16[4,512,512]{2,1,0:T(8,128)(2,1)}, u32[]{:S(2)}) copy-start(bf16[4,512,512]{2,1,0:T(8,128)(2,1)} %get-tuple-element.112.k_ref) | copy-start | bytes 6291460
  45.1 1.8 %copy-start.3 = (bf16[2,4,256,256]{3,2,1,0:T(8,128)(2,1)S(1)}, bf16[2,4,256,256]{3,2,1,0:T(8,128)(2,1)}, u32[]{:S(2)}) copy-start(bf16[2,4,256,256]{3,2,1,0:T(8,128)(2,1)} %get-tuple-element.114.xy_ref) | copy-start | bytes 3145732
  45.1 2.0 %copy-start.6 = (bf16[4,256,256]{2,1,0:T(8,128)(2,1)S(1)}, bf16[4,256,256]{2,1,0:T(8,128)(2,1)}, u32[]{:S(2)}) copy-start(bf16[4,256,256]{2,1,0:T(8,128)(2,1)} %get-tuple-element.113.y_ref) | copy-start | bytes 1572868
  45.1 2.0 %copy-start.9 = (bf16[2,32,512]{2,1,0:T(8,128)(2,1)S(1)}, bf16[2,32,512]{2,1,0:T(8,128)(2,1)}, u32[]{:S(2)}) copy-start(bf16[2,32,512]{2,1,0:T(8,128)(2,1)} %get-tuple-element.115.z_ref) | copy-start | bytes 196612
  46.7 1.8 %collective-permute-start.4 = (f16[656,128]{1,0:T(8,128)(2,1)S(1)}, f16[656,128]{1,0:T(8,128)(2,1)S(1)}, u32[]{:S(2)}, u32[]{:S(2)}) collective-permute-start(f16[656,128]{1,0:T(8,128)(2,1)S(1)} %convert_element_type.51), channel_id=1, source_target_pairs={{0,4},{1,5},{2,6},{3,7},{4,0},{5,1},{6,2},{7,3},{8,12},{9,13},{10,... | collective-permute-start | bytes 503816 | tf_op jit(solution)/shard_map/ppermute | solution.py:542
  49.4 4.9 %collective-permute-start.6 = (f32[128,128]{1,0:T(8,128)S(1)}, f32[128,128]{1,0:T(8,128)S(1)}, u32[]{:S(2)}, u32[]{:S(2)}) collective-permute-start(f32[128,128]{1,0:T(8,128)S(1)} %get-tuple-element.137.up_ref), channel_id=1, source_target_pairs={{0,1},{1,0},{2,3},{3,2},{4,5},{5,4},{6,7},{7,6},{8,9},{9,8},{10,11... | collective-permute-start | bytes 196616 | tf_op jit(solution)/shard_map/ppermute | solution.py:542
  51.4 2.9 %collective-permute-start.7 = (f32[128,128]{1,0:T(8,128)S(1)}, f32[128,128]{1,0:T(8,128)S(1)}, u32[]{:S(2)}, u32[]{:S(2)}) collective-permute-start(f32[128,128]{1,0:T(8,128)S(1)} %get-tuple-element.138.down_ref), channel_id=1, source_target_pairs={{0,4},{1,2},{2,1},{3,7},{4,0},{5,6},{6,5},{7,3},{8,12},{9,10},{10,... | collective-permute-start | bytes 196616 | tf_op jit(solution)/shard_map/ppermute | solution.py:546
  55.1 3.8 %collective-permute-start.8 = (f16[656,128]{1,0:T(8,128)(2,1)S(1)}, f16[656,128]{1,0:T(8,128)(2,1)S(1)}, u32[]{:S(2)}, u32[]{:S(2)}) collective-permute-start(f16[656,128]{1,0:T(8,128)(2,1)S(1)} %convert_element_type.55), channel_id=1, source_target_pairs={{0,4},{1,5},{2,6},{3,7},{4,0},{5,1},{6,2},{7,3},{8,12},{9,13},{10,... | collective-permute-start | bytes 503816 | tf_op jit(solution)/shard_map/ppermute | solution.py:542
  55.2 6.7 %collective-permute-start.9 = (f16[656,128]{1,0:T(8,128)(2,1)S(1)}, f16[656,128]{1,0:T(8,128)(2,1)S(1)}, u32[]{:S(2)}, u32[]{:S(2)}) collective-permute-start(f16[656,128]{1,0:T(8,128)(2,1)S(1)} %convert_element_type.55), channel_id=1, source_target_pairs={{0,1},{1,0},{2,3},{3,2},{4,8},{5,9},{6,10},{7,11},{8,4},{9,5},{10,... | collective-permute-start | bytes 503816 | tf_op jit(solution)/shard_map/ppermute | solution.py:546
  59.0 3.0 %copy-start.2 = (bf16[4,512,512]{2,1,0:T(8,128)(2,1)S(1)}, bf16[4,512,512]{2,1,0:T(8,128)(2,1)}, u32[]{:S(2)}) copy-start(bf16[4,512,512]{2,1,0:T(8,128)(2,1)} %get-tuple-element.106.refs_2_.ka_ref) | copy-start | bytes 6291460
  59.0 3.0 %copy-start.5 = (bf16[2,4,256,256]{3,2,1,0:T(8,128)(2,1)S(1)}, bf16[2,4,256,256]{3,2,1,0:T(8,128)(2,1)}, u32[]{:S(2)}) copy-start(bf16[2,4,256,256]{3,2,1,0:T(8,128)(2,1)} %get-tuple-element.108.refs_4_.xya_ref) | copy-start | bytes 3145732
  59.0 3.0 %copy-start.8 = (bf16[4,256,256]{2,1,0:T(8,128)(2,1)S(1)}, bf16[4,256,256]{2,1,0:T(8,128)(2,1)}, u32[]{:S(2)}) copy-start(bf16[4,256,256]{2,1,0:T(8,128)(2,1)} %get-tuple-element.107.refs_3_.ya_ref) | copy-start | bytes 1572868
  59.1 3.0 %copy-start.11 = (bf16[2,32,512]{2,1,0:T(8,128)(2,1)S(1)}, bf16[2,32,512]{2,1,0:T(8,128)(2,1)}, u32[]{:S(2)}) copy-start(bf16[2,32,512]{2,1,0:T(8,128)(2,1)} %get-tuple-element.109.refs_5_.za_ref) | copy-start | bytes 196612
  65.5 5.4 %collective-permute-start.11 = (f16[656,128]{1,0:T(8,128)(2,1)S(1)}, f16[656,128]{1,0:T(8,128)(2,1)S(1)}, u32[]{:S(2)}, u32[]{:S(2)}) collective-permute-start(f16[656,128]{1,0:T(8,128)(2,1)S(1)} %convert_element_type.60), channel_id=1, source_target_pairs={{0,1},{1,0},{2,3},{3,2},{4,8},{5,9},{6,10},{7,11},{8,4},{9,5},{10,... | collective-permute-start | bytes 503816 | tf_op jit(solution)/shard_map/ppermute | solution.py:546
  67.8 3.2 %collective-permute-start.10 = (f16[656,128]{1,0:T(8,128)(2,1)S(1)}, f16[656,128]{1,0:T(8,128)(2,1)S(1)}, u32[]{:S(2)}, u32[]{:S(2)}) collective-permute-start(f16[656,128]{1,0:T(8,128)(2,1)S(1)} %convert_element_type.58), channel_id=1, source_target_pairs={{0,4},{1,5},{2,6},{3,7},{4,0},{5,1},{6,2},{7,3},{8,12},{9,13},{10,... | collective-permute-start | bytes 503816 | tf_op jit(solution)/shard_map/ppermute | solution.py:542
  71.2 4.0 %collective-permute-start.12 = (f32[64,128]{1,0:T(8,128)S(1)}, f32[64,128]{1,0:T(8,128)S(1)}, u32[]{:S(2)}, u32[]{:S(2)}) collective-permute-start(f32[64,128]{1,0:T(8,128)S(1)} %get-tuple-element.163), channel_id=1, source_target_pairs={{0,1},{1,0},{2,3},{3,2},{4,5},{5,4},{6,7},{7,6},{8,9},{9,8},{10,11... | collective-permute-start | bytes 98312 | tf_op jit(solution)/shard_map/ppermute | solution.py:542
  71.6 3.6 %collective-permute-start.13 = (f32[64,128]{1,0:T(8,128)S(1)}, f32[64,128]{1,0:T(8,128)S(1)}, u32[]{:S(2)}, u32[]{:S(2)}) collective-permute-start(f32[64,128]{1,0:T(8,128)S(1)} %get-tuple-element.164), channel_id=1, source_target_pairs={{0,4},{1,2},{2,1},{3,7},{4,0},{5,6},{6,5},{7,3},{8,12},{9,10},{10,... | collective-permute-start | bytes 98312 | tf_op jit(solution)/shard_map/ppermute | solution.py:546

commit v7 on v5

--- a/solution.py
+++ b/solution.py
@@ -356,12 +356,6 @@
     copy.wait()
 
 
-def pack_edges(quotient_ref, edge_ref, shifts):
-    for v in range(V):
-        for yr in range(2):
-            edge_ref[v, yr] = pack_strip(quotient_ref[v], shifts[yr])
-
-
 def quotient_first_kernel(info_ref, arrived_ref, *refs):
     outside, (data_ref, quotient_ref, edge_ref, far_ref), held, planes_ref, sems = (
         refs[:6], refs[6:10], refs[10:16], refs[16], refs[17],
@@ -377,11 +371,12 @@
     def _():
         planes_ref[...] = dot(table_ref[...], arrived_ref[...])
 
-    for v in range(V):
-        copies[1 + v].wait()
-
-        @pl.when(shifts[0] >= 0)
-        def _():
+    for copy in copies[1 : 1 + V]:
+        copy.wait()
+
+    @pl.when(shifts[0] >= 0)
+    def _():
+        for v in range(V):
             for x in range(BX):
                 rows = slice(x * NZ, (x + 1) * NZ)
                 piece = planes_ref[v * NZ : (v + 1) * NZ, x * BY : (x + 1) * BY]
@@ -464,9 +459,10 @@
 
     def add(v, part):
         quotient_ref[v] = data_ref[v].astype(f32) / (blurred_ref[v] + part)
+        for yr in range(2):
+            edge_ref[v, yr] = pack_strip(quotient_ref[v], shifts[yr])
 
     forward_parts(read_scaled(from_far_ref), (k_ref, y_ref, xy_ref, z_ref), shifts, add)
-    pack_edges(quotient_ref, edge_ref, shifts)
     write_scaled(far_ref, *adjoint_parts(quotient_ref, edge_ref, (ka_ref, ya_ref, xya_ref, za_ref)))
 
 

time: 77.5 us -> 77.5 us (level)
  no operation moved by 1% of the time
where the time goes in v7:
time: 77.5 us; the launch traced here: 76.3 us
  Pallas kernels  44.9 us (58%)
  starting transfers between devices  20.8 us (27%)
  waiting for transfers between devices  7.61 us (10%)
  local copies, waits for them, and re-layouts  1.28 us (2%)
  other arithmetic  0.8 us (1%)
  between operations  0.79 us (1%)
    pallas_call x21, Pallas kernels, call(): pl.pallas_call(kernel, out_shape=[HBM(s, d) if where is HBM else jax.Shap...  44.9 us
    ppermute x7, starting transfers between devices, swap_far(): lax.ppermute(narrow(axis, value), ('gx', 'gy'), partner_swaps(axis)[1])  8.33 us
    ppermute x7, starting transfers between devices, swap_near(): lax.ppermute(narrow(axis, value), ('gx', 'gy'), partner_swaps(axis)[0])  7.02 us
    all_to_all x1, starting transfers between devices, shards(): lax.all_to_all(outgoing.reshape(devices, cap, plane), ('gx', 'gy'), split...  5.4 us
    ppermute x7, waiting for transfers between devices, swap_near(): lax.ppermute(narrow(axis, value), ('gx', 'gy'), partner_swaps(axis)[0])  2.94 us
    all_to_all x1, waiting for transfers between devices, shards(): lax.all_to_all(outgoing.reshape(devices, cap, plane), ('gx', 'gy'), split...  2.68 us
    ppermute x7, waiting for transfers between devices, swap_far(): lax.ppermute(narrow(axis, value), ('gx', 'gy'), partner_swaps(axis)[1])  1.98 us
  transfers between devices with their start and end apart: 15, of which 5 were waited for; matrix products, arithmetic and copies ran while one was open for 2% of the time, Pallas kernels for 41%

profile of v7, /device:TPU:0, one launch (start us, length us, event | category | flops | bytes accessed | tf_op | source)
XLA Modules:
  0.0 76.3 jit_solution(945384530104967894)
XLA Ops:
  0.1 1.8 %shard_map.55 = (f32[512,128]{1,0:T(8,128)S(1)}, f32[64,128]{1,0:T(8,128)S(1)}, f32[64,128]{1,0:T(8,128)S(1)}, s32[32,128]{1,0:T(8,128)S(1)}, bf16[128,16,128]{2,1,0:T(8,128)(2,1)S(1)}) custom-call(s32[2]{0:T(128)S(1)} %pad_add_fusion.info_ref, f32[32,16,128]{2,1,0:T(8,128)} %refs_0_.1, s32[32,128]{1,0:T(8,128)} %bitcast.9, bf16[128,16,128]{2,1,0:T(8,128)(2,1)} %refs_2_.1), custom_call_target="tpu_custom_call" | custom-call | bytes 70000 | tf_op jit(solution)/shard_map/pallas_call | solution.py:502
  1.9 3.1 %collective-permute-start = (f32[64,128]{1,0:T(8,128)S(1)}, f32[64,128]{1,0:T(8,128)S(1)}, u32[]{:S(2)}, u32[]{:S(2)}) collective-permute-start(f32[64,128]{1,0:T(8,128)S(1)} %get-tuple-element.87), channel_id=1, source_target_pairs={{0,1},{1,0},{2,3},{3,2},{4,5},{5,4},{6,7},{7,6},{8,9},{9,8},{10,11... | collective-permute-start | bytes 98312 | tf_op jit(solution)/shard_map/ppermute | solution.py:538
  5.0 1.6 %shard_map.56 = bf16[256,2048]{1,0:T(8,128)(2,1)} custom-call(s32[1]{0:T(128)} %bitcast.3.me_ref, s32[32,128]{1,0:T(8,128)S(1)} %get-tuple-element.89.slots_ref, bf16[128,16,128]{2,1,0:T(8,128)(2,1)S(1)} %get-tuple-element.90.stored_ref), custom_call_target="tpu_custom_call" | custom-call | bytes 70000 | tf_op jit(solution)/shard_map/pallas_call | solution.py:502
  6.6 5.4 %all-to-all-start = ((bf16[32,8,2048]{2,1,0:T(8,128)(2,1)}), bf16[32,8,2048]{2,1,0:T(8,128)(2,1)S(1)}, u32[]{:S(2)}, u32[]{:S(2)}) async-start(bf16[32,8,2048]{2,1,0:T(8,128)(2,1)} %bitcast.4), calls=%async_computation | async-start | bytes 2097152 | tf_op jit(solution)/shard_map/all_to_all | solution.py:619
  13.7 2.5 %shard_map.58 = (bf16[4,512,512]{2,1,0:T(8,128)(2,1)S(1)}, bf16[384,512]{1,0:T(8,128)(2,1)S(1)}, bf16[2,4,256,256]{3,2,1,0:T(8,128)(2,1)S(1)}, bf16[2,128,128]{2...) custom-call(f32[108,128]{1,0:T(8,128)S(1)} %get-tuple-element.126.ta, ...), custom_call_target="tpu_custom_call" | custom-call | bytes 10500000 | tf_op jit(solution)/shard_map/pallas_call | solution.py:502
  16.2 7.0 %shard_map.62 = (bf16[4,512,512]{2,1,0:T(8,128)(2,1)}, bf16[4,256,256]{2,1,0:T(8,128)(2,1)}, bf16[2,4,256,256]{3,2,1,0:T(8,128)(2,1)}, bf16[2,32,512]{2,1,0:T(8,...) custom-call(f32[108,128]{1,0:T(8,128)S(1)} %get-tuple-element.126.ta, ...), custom_call_target="tpu_custom_call" | custom-call | bytes 14000000 | tf_op jit(solution)/shard_map/pallas_call | solution.py:502
  23.3 1.8 %collective-permute-start.3 = (f16[640,128]{1,0:T(8,128)(2,1)S(1)}, f16[640,128]{1,0:T(8,128)(2,1)S(1)}, u32[]{:S(2)}, u32[]{:S(2)}) collective-permute-start(f16[640,128]{1,0:T(8,128)(2,1)S(1)} %convert_element_type.48), channel_id=1, source_target_pairs={{0,1},{1,0},{2,3},{3,2},{4,8},{5,9},{6,10},{7,11},{8,4},{9,5},{10,... | collective-permute-start | bytes 491528 | tf_op jit(solution)/shard_map/ppermute | solution.py:542
  25.2 1.0 %shard_map.57.refs_0_ = bf16[128,256]{1,0:T(8,128)(2,1)} custom-call(s32[1]{0:T(128)} %bitcast.3.me_ref, s32[256,128]{1,0:T(8,128)S(1)} %broadcast_bitcast_fusion.slots_ref), custom_call_target="tpu_custom_call" | custom-call | bytes 70000 | tf_op jit(solution)/shard_map/pallas_call | solution.py:502
  26.2 1.9 %shard_map.59.refs_0_ = f32[4,512,128]{2,1,0:T(8,128)S(1)} custom-call(s32[2]{0:T(128)S(1)} %pad_add_fusion.info_ref, f32[640,128]{1,0:T(8,128)S(1)} %constant_dynamic-update-slice_fusion.refs_0_.old_ref, bf16[4,512,512]{2,1,0:T(8,128)(2,1)S(1)} %get-tuple-element.95.refs_1_, bf16[384,512]{1,0:T(8,128)(2,1)S(1)} %get-tuple-element.96.refs_2_, ...), custom_call_target="tpu_custom_call" | custom-call | bytes 70000 | tf_op jit(solution)/shard_map/pallas_call | solution.py:502
  28.2 2.0 %shard_map.60.blurred_ref = f32[4,512,128]{2,1,0:T(8,128)S(1)} custom-call(s32[2]{0:T(128)S(1)} %pad_add_fusion.info_ref, f32[4,512,128]{2,1,0:T(8,128)S(1)} %shard_map.59.refs_0_, f32[640,128]{1,0:T(8,128)S(1)} %convert_element_type.49.refs_1_, bf16[4,512,512]{2,1,0:T(8,128)(2,1)S(1)} %get-tuple-element.99.refs_2_, ...), custom_call_target="tpu_custom_call" | custom-call | bytes 70000 | tf_op jit(solution)/shard_map/pallas_call | solution.py:502
  30.2 1.2 %collective-permute-done.3 = f16[640,128]{1,0:T(8,128)(2,1)S(1)} collective-permute-done((f16[640,128]{1,0:T(8,128)(2,1)S(1)}, f16[640,128]{1,0:T(8,128)(2,1)S(1)}, u32[]{:S(2)}, u32[]{:S(2)}) %collective-permute-start.3) | collective-permute-done | bytes 163872 | tf_op jit(solution)/shard_map/ppermute | solution.py:542
  31.4 2.9 %shard_map.61.refs_1_ = f32[4,512,128]{2,1,0:T(8,128)} custom-call(s32[2]{0:T(128)S(1)} %pad_add_fusion.info_ref, f32[4,512,128]{2,1,0:T(8,128)S(1)} %shard_map.60.blurred_ref, f32[640,128]{1,0:T(8,128)S(1)} %convert_element_type.50.message_ref, bf16[4,512,512]{2,1,0:T(8,128)(2,1)S(1)} %get-tuple-element.103.k_ref, ...), custom_call_target="tpu_custom_call" | custom-call | bytes 70000 | tf_op jit(solution)/shard_map/pallas_call | solution.py:502
  34.4 2.7 %all-to-all-done = bf16[32,8,2048]{2,1,0:T(8,128)(2,1)S(1)} async-done(((bf16[32,8,2048]{2,1,0:T(8,128)(2,1)}), bf16[32,8,2048]{2,1,0:T(8,128)(2,1)S(1)}, u32[]{:S(2)}, u32[]{:S(2)}) %all-to-all-start) | async-done | bytes 1048608 | tf_op jit(solution)/shard_map/all_to_all | solution.py:619
  37.1 4.8 %shard_map.63 = (bf16[4,512,128]{2,1,0:T(8,128)(2,1)S(1)}, f32[4,512,128]{2,1,0:T(8,128)S(1)}, f32[4,2,64,128]{3,2,1,0:T(8,128)S(1)}, f32[656,128]{1,0:T(8,128)S(1)}) custom-call(s32[2]{0:T(128)S(1)} %pad_add_fusion.info_ref, bf16[256,2048]{1,0:T(8,128)(2,1)S(1)} %bitcast.8, bf16[128,256]{1,0:T(8,128)(2,1)} %shard_map.57.refs_0_, ...), custom_call_target="tpu_custom_call" | custom-call | bytes 70000 | tf_op jit(solution)/shard_map/pallas_call | solution.py:502
  41.9 3.2 %collective-permute-start.5 = (f16[656,128]{1,0:T(8,128)(2,1)S(1)}, f16[656,128]{1,0:T(8,128)(2,1)S(1)}, u32[]{:S(2)}, u32[]{:S(2)}) collective-permute-start(f16[656,128]{1,0:T(8,128)(2,1)S(1)} %convert_element_type.53), channel_id=1, source_target_pairs={{0,1},{1,0},{2,3},{3,2},{4,8},{5,9},{6,10},{7,11},{8,4},{9,5},{10,... | collective-permute-start | bytes 503816 | tf_op jit(solution)/shard_map/ppermute | solution.py:542
  45.1 1.5 %shard_map.65 = f32[656,128]{1,0:T(8,128)S(1)} custom-call(f32[4,512,128]{2,1,0:T(8,128)S(1)} %get-tuple-element.111.quotient_ref, f32[4,2,64,128]{3,2,1,0:T(8,128)S(1)} %get-tuple-element.112.edge_ref, bf16[4,512,512]{2,1,0:T(8,128)(2,1)S(1)} %copy-done.1, bf16[4,256,256]{2,1,0:T(8,128)(2,1)S(1)} %copy-done.7, bf16[2,4,256,256]{3,2,1,0:T(8,128)(2,1)S(1)} %copy-done.4, ...), custom_call_target="tpu_custom_call" | custom-call | bytes 70000 | tf_op jit(solution)/shard_map/pallas_call | solution.py:502
  47.1 1.4 %shard_map.64 = (f32[512,128]{1,0:T(8,128)S(1)}, f32[2,64,128]{2,1,0:T(8,128)S(1)}) custom-call(f32[4,512,128]{2,1,0:T(8,128)S(1)} %get-tuple-element.111.quotient_ref, f32[4,2,64,128]{3,2,1,0:T(8,128)S(1)} %get-tuple-element.112.edge_ref, bf16[4,512,512]{2,1,0:T(8,128)(2,1)S(1)} %copy-done, bf16[4,256,256]{2,1,0:T(8,128)(2,1)S(1)} %copy-done.6, ...), custom_call_target="tpu_custom_call" | custom-call | bytes 70000 | tf_op jit(solution)/shard_map/pallas_call | solution.py:502
  48.5 0.8 %shard_map.66 = (f32[512,128]{1,0:T(8,128)S(1)}, f32[128,128]{1,0:T(8,128)S(1)}, f32[128,128]{1,0:T(8,128)S(1)}) custom-call(s32[2]{0:T(128)S(1)} %pad_add_fusion.info_ref, f32[512,128]{1,0:T(8,128)S(1)} %get-tuple-element.117.field_ref, f32[2,64,128]{2,1,0:T(8,128)S(1)} %get-tuple-element.118.strips_ref, f32[656,128]{1,0:T(8,128)S(1)} %convert_element_type.52.near_ref, ...), custom_call_target="tpu_custom_call" | custom-call | bytes 70000 | tf_op jit(solution)/shard_map/pallas_call | solution.py:502
  49.4 2.0 %collective-permute-start.6 = (f32[128,128]{1,0:T(8,128)S(1)}, f32[128,128]{1,0:T(8,128)S(1)}, u32[]{:S(2)}, u32[]{:S(2)}) collective-permute-start(f32[128,128]{1,0:T(8,128)S(1)} %get-tuple-element.142.up_ref), channel_id=1, source_target_pairs={{0,1},{1,0},{2,3},{3,2},{4,5},{5,4},{6,7},{7,6},{8,9},{9,8},{10,11... | collective-permute-start | bytes 196616 | tf_op jit(solution)/shard_map/ppermute | solution.py:538
  51.4 2.5 %shard_map.67 = (bf16[4,512,512]{2,1,0:T(8,128)(2,1)S(1)}, bf16[384,512]{1,0:T(8,128)(2,1)S(1)}, bf16[2,4,256,256]{3,2,1,0:T(8,128)(2,1)S(1)}, bf16[2,128,128]{2...) custom-call(f32[108,128]{1,0:T(8,128)S(1)} %get-tuple-element.126.ta, ...), custom_call_target="tpu_custom_call" | custom-call | bytes 70000 | tf_op jit(solution)/shard_map/pallas_call | solution.py:502
  54.2 0.9 %shard_map.68 = (f32[640,128]{1,0:T(8,128)S(1)}, f32[656,128]{1,0:T(8,128)S(1)}) custom-call(s32[2]{0:T(128)S(1)} %pad_add_fusion.info_ref, f32[640,128]{1,0:T(8,128)S(1)} %constant_dynamic-update-slice_fusion.refs_0_.old_ref, f32[512,128]{1,0:T(8,128)S(1)} %get-tuple-element.141.total_ref, f32[128,128]{1,0:T(8,128)S(1)} %get-tuple-element.142.up_ref, ...), custom_call_target="tpu_custom_call" | custom-call | bytes 70000 | tf_op jit(solution)/shard_map/pallas_call | solution.py:502
  55.4 1.6 %collective-permute-start.9 = (f16[656,128]{1,0:T(8,128)(2,1)S(1)}, f16[656,128]{1,0:T(8,128)(2,1)S(1)}, u32[]{:S(2)}, u32[]{:S(2)}) collective-permute-start(f16[656,128]{1,0:T(8,128)(2,1)S(1)} %convert_element_type.55), channel_id=1, source_target_pairs={{0,1},{1,0},{2,3},{3,2},{4,8},{5,9},{6,10},{7,11},{8,4},{9,5},{10,... | collective-permute-start | bytes 503816 | tf_op jit(solution)/shard_map/ppermute | solution.py:542
  57.0 1.9 %shard_map.69.blurred_ref = f32[4,512,128]{2,1,0:T(8,128)S(1)} custom-call(s32[2]{0:T(128)S(1)} %pad_add_fusion.info_ref, f32[640,128]{1,0:T(8,128)S(1)} %get-tuple-element.144.own_ref.old_ref, bf16[4,512,512]{2,1,0:T(8,128)(2,1)S(1)} %get-tuple-element.146.k_ref, bf16[384,512]{1,0:T(8,128)(2,1)S(1)} %get-tuple-element.147.y_ref, ...), custom_call_target="tpu_custom_call" | custom-call | bytes 70000 | tf_op jit(solution)/shard_map/pallas_call | solution.py:502
  59.1 2.0 %shard_map.70.blurred_ref = f32[4,512,128]{2,1,0:T(8,128)S(1)} custom-call(s32[2]{0:T(128)S(1)} %pad_add_fusion.info_ref, f32[4,512,128]{2,1,0:T(8,128)S(1)} %shard_map.69.blurred_ref, f32[656,128]{1,0:T(8,128)S(1)} %convert_element_type.56.near_ref, bf16[4,512,512]{2,1,0:T(8,128)(2,1)S(1)} %get-tuple-element.151.k_ref, ...), custom_call_target="tpu_custom_call" | custom-call | bytes 70000 | tf_op jit(solution)/shard_map/pallas_call | solution.py:502
  61.1 3.5 %shard_map.71 = (f32[4,512,128]{2,1,0:T(8,128)S(1)}, f32[4,2,64,128]{3,2,1,0:T(8,128)S(1)}, f32[656,128]{1,0:T(8,128)S(1)}) custom-call(s32[2]{0:T(128)S(1)} %pad_add_fusion.info_ref, bf16[4,512,128]{2,1,0:T(8,128)(2,1)S(1)} %get-tuple-element.145.data_ref, f32[4,512,128]{2,1,0:T(8,128)S(1)} %shard_map.70.blurred_ref, ...), custom_call_target="tpu_custom_call" | custom-call | bytes 70000 | tf_op jit(solution)/shard_map/pallas_call | solution.py:502
  64.6 1.4 %collective-permute-start.11 = (f16[656,128]{1,0:T(8,128)(2,1)S(1)}, f16[656,128]{1,0:T(8,128)(2,1)S(1)}, u32[]{:S(2)}, u32[]{:S(2)}) collective-permute-start(f16[656,128]{1,0:T(8,128)(2,1)S(1)} %convert_element_type.60), channel_id=1, source_target_pairs={{0,1},{1,0},{2,3},{3,2},{4,8},{5,9},{6,10},{7,11},{8,4},{9,5},{10,... | collective-permute-start | bytes 503816 | tf_op jit(solution)/shard_map/ppermute | solution.py:542
  66.0 1.7 %shard_map.73 = f32[656,128]{1,0:T(8,128)S(1)} custom-call(f32[4,512,128]{2,1,0:T(8,128)S(1)} %get-tuple-element.159.quotient_ref, f32[4,2,64,128]{3,2,1,0:T(8,128)S(1)} %get-tuple-element.160.edge_ref, bf16[4,512,512]{2,1,0:T(8,128)(2,1)S(1)} %copy-done.1, bf16[4,256,256]{2,1,0:T(8,128)(2,1)S(1)} %copy-done.7, bf16[2,4,256,256]{3,2,1,0:T(8,128)(2,1)S(1)} %copy-done.4, ...), custom_call_target="tpu_custom_call" | custom-call | bytes 70000 | tf_op jit(solution)/shard_map/pallas_call | solution.py:502
  67.9 1.4 %shard_map.72 = (f32[512,128]{1,0:T(8,128)S(1)}, f32[2,64,128]{2,1,0:T(8,128)S(1)}) custom-call(f32[4,512,128]{2,1,0:T(8,128)S(1)} %get-tuple-element.159.quotient_ref, f32[4,2,64,128]{3,2,1,0:T(8,128)S(1)} %get-tuple-element.160.edge_ref, bf16[4,512,512]{2,1,0:T(8,128)(2,1)S(1)} %copy-done, bf16[4,256,256]{2,1,0:T(8,128)(2,1)S(1)} %copy-done.6, ...), custom_call_target="tpu_custom_call" | custom-call | bytes 70000 | tf_op jit(solution)/shard_map/pallas_call | solution.py:502
  69.3 0.8 collective-permute-done.11
  70.2 1.4 %collective-permute-start.12 = (f32[64,128]{1,0:T(8,128)S(1)}, f32[64,128]{1,0:T(8,128)S(1)}, u32[]{:S(2)}, u32[]{:S(2)}) collective-permute-start(f32[64,128]{1,0:T(8,128)S(1)} %get-tuple-element.165), channel_id=1, source_target_pairs={{0,1},{1,0},{2,3},{3,2},{4,5},{5,4},{6,7},{7,6},{8,9},{9,8},{10,11... | collective-permute-start | bytes 98312 | tf_op jit(solution)/shard_map/ppermute | solution.py:538
  72.0 2.6 %collective-permute-done.12.up_in_ref = f32[64,128]{1,0:T(8,128)S(1)} collective-permute-done((f32[64,128]{1,0:T(8,128)S(1)}, f32[64,128]{1,0:T(8,128)S(1)}, u32[]{:S(2)}, u32[]{:S(2)}) %collective-permute-start.12) | collective-permute-done | bytes 32800 | tf_op jit(solution)/shard_map/ppermute | solution.py:538
  74.6 1.6 %shard_map.75 = f32[32,16,128]{2,1,0:T(8,128)} custom-call(s32[2]{0:T(128)S(1)} %pad_add_fusion.info_ref, f32[640,128]{1,0:T(8,128)S(1)} %get-tuple-element.144.own_ref.old_ref, f32[512,128]{1,0:T(8,128)S(1)} %get-tuple-element.164.total_ref, f32[64,128]{1,0:T(8,128)S(1)} %collective-permute-done.12.up_in_ref, f32[64,128]{1,0:T(8,128)S(1)} %collective-permute-done.13.down_in_ref), custom_call_target="tpu_custom_call" | custom-call | bytes 70000 | tf_op jit(solution)/shard_map/pallas_call | solution.py:502
  (86 shorter events, 3.6 us)
Async XLA Ops:
  0.1 12.0 %copy-start.12 = (s32[8,4,4,3]{0,2,3,1:T(4,128)S(1)}, s32[8,4,4,3]{0,2,3,1:T(4,128)}, u32[]{:S(2)}) copy-start(s32[8,4,4,3]{0,2,3,1:T(4,128)} %param.9) | copy-start | bytes 4612
  1.9 10.8 %copy-start.14 = (f32[48,31]{0,1:T(8,128)S(1)}, f32[48,31]{0,1:T(8,128)}, u32[]{:S(2)}) copy-start(f32[48,31]{0,1:T(8,128)} %param.8) | copy-start | bytes 17860
  1.9 21.3 %collective-permute-start = (f32[64,128]{1,0:T(8,128)S(1)}, f32[64,128]{1,0:T(8,128)S(1)}, u32[]{:S(2)}, u32[]{:S(2)}) collective-permute-start(f32[64,128]{1,0:T(8,128)S(1)} %get-tuple-element.87), channel_id=1, source_target_pairs={{0,1},{1,0},{2,3},{3,2},{4,5},{5,4},{6,7},{7,6},{8,9},{9,8},{10,11... | collective-permute-start | bytes 98312 | tf_op jit(solution)/shard_map/ppermute | solution.py:538
  5.0 18.2 %collective-permute-start.1 = (f32[64,128]{1,0:T(8,128)S(1)}, f32[64,128]{1,0:T(8,128)S(1)}, u32[]{:S(2)}, u32[]{:S(2)}) collective-permute-start(f32[64,128]{1,0:T(8,128)S(1)} %get-tuple-element.88), channel_id=1, source_target_pairs={{0,4},{1,2},{2,1},{3,7},{4,0},{5,6},{6,5},{7,3},{8,12},{9,10},{10,... | collective-permute-start | bytes 98312 | tf_op jit(solution)/shard_map/ppermute | solution.py:542
  6.6 30.5 %all-to-all-start = ((bf16[32,8,2048]{2,1,0:T(8,128)(2,1)}), bf16[32,8,2048]{2,1,0:T(8,128)(2,1)S(1)}, u32[]{:S(2)}, u32[]{:S(2)}) async-start(bf16[32,8,2048]{2,1,0:T(8,128)(2,1)} %bitcast.4), calls=%async_computation | async-start | bytes 2097152 | tf_op jit(solution)/shard_map/all_to_all | solution.py:619
  12.0 13.2 %copy-start.13 = (s32[4096]{0:T(1024)S(1)}, s32[4096]{0:T(1024)}, u32[]{:S(2)}) copy-start(s32[4096]{0:T(1024)} %param.7) | copy-start | bytes 49156
  23.3 8.1 %collective-permute-start.3 = (f16[640,128]{1,0:T(8,128)(2,1)S(1)}, f16[640,128]{1,0:T(8,128)(2,1)S(1)}, u32[]{:S(2)}, u32[]{:S(2)}) collective-permute-start(f16[640,128]{1,0:T(8,128)(2,1)S(1)} %convert_element_type.48), channel_id=1, source_target_pairs={{0,1},{1,0},{2,3},{3,2},{4,8},{5,9},{6,10},{7,11},{8,4},{9,5},{10,... | collective-permute-start | bytes 491528 | tf_op jit(solution)/shard_map/ppermute | solution.py:542
  25.1 3.1 %collective-permute-start.2 = (f16[640,128]{1,0:T(8,128)(2,1)S(1)}, f16[640,128]{1,0:T(8,128)(2,1)S(1)}, u32[]{:S(2)}, u32[]{:S(2)}) collective-permute-start(f16[640,128]{1,0:T(8,128)(2,1)S(1)} %convert_element_type.48), channel_id=1, source_target_pairs={{0,4},{1,5},{2,6},{3,7},{4,0},{5,1},{6,2},{7,3},{8,12},{9,13},{10,... | collective-permute-start | bytes 491528 | tf_op jit(solution)/shard_map/ppermute | solution.py:538
  37.1 8.0 %copy-start.1 = (bf16[4,512,512]{2,1,0:T(8,128)(2,1)S(1)}, bf16[4,512,512]{2,1,0:T(8,128)(2,1)}, u32[]{:S(2)}) copy-start(bf16[4,512,512]{2,1,0:T(8,128)(2,1)} %get-tuple-element.119.k_ref) | copy-start | bytes 6291460
  37.1 8.0 %copy-start.4 = (bf16[2,4,256,256]{3,2,1,0:T(8,128)(2,1)S(1)}, bf16[2,4,256,256]{3,2,1,0:T(8,128)(2,1)}, u32[]{:S(2)}) copy-start(bf16[2,4,256,256]{3,2,1,0:T(8,128)(2,1)} %get-tuple-element.121.xy_ref) | copy-start | bytes 3145732
  37.1 8.0 %copy-start.7 = (bf16[4,256,256]{2,1,0:T(8,128)(2,1)S(1)}, bf16[4,256,256]{2,1,0:T(8,128)(2,1)}, u32[]{:S(2)}) copy-start(bf16[4,256,256]{2,1,0:T(8,128)(2,1)} %get-tuple-element.120.y_ref) | copy-start | bytes 1572868
  37.1 8.0 %copy-start.10 = (bf16[2,32,512]{2,1,0:T(8,128)(2,1)S(1)}, bf16[2,32,512]{2,1,0:T(8,128)(2,1)}, u32[]{:S(2)}) copy-start(bf16[2,32,512]{2,1,0:T(8,128)(2,1)} %get-tuple-element.122.z_ref) | copy-start | bytes 196612
  41.9 6.6 %collective-permute-start.5 = (f16[656,128]{1,0:T(8,128)(2,1)S(1)}, f16[656,128]{1,0:T(8,128)(2,1)S(1)}, u32[]{:S(2)}, u32[]{:S(2)}) collective-permute-start(f16[656,128]{1,0:T(8,128)(2,1)S(1)} %convert_element_type.53), channel_id=1, source_target_pairs={{0,1},{1,0},{2,3},{3,2},{4,8},{5,9},{6,10},{7,11},{8,4},{9,5},{10,... | collective-permute-start | bytes 503816 | tf_op jit(solution)/shard_map/ppermute | solution.py:542
  45.1 1.7 %copy-start = (bf16[4,512,512]{2,1,0:T(8,128)(2,1)S(1)}, bf16[4,512,512]{2,1,0:T(8,128)(2,1)}, u32[]{:S(2)}) copy-start(bf16[4,512,512]{2,1,0:T(8,128)(2,1)} %get-tuple-element.113.k_ref) | copy-start | bytes 6291460
  45.1 1.8 %copy-start.3 = (bf16[2,4,256,256]{3,2,1,0:T(8,128)(2,1)S(1)}, bf16[2,4,256,256]{3,2,1,0:T(8,128)(2,1)}, u32[]{:S(2)}) copy-start(bf16[2,4,256,256]{3,2,1,0:T(8,128)(2,1)} %get-tuple-element.115.xy_ref) | copy-start | bytes 3145732
  45.1 2.0 %copy-start.6 = (bf16[4,256,256]{2,1,0:T(8,128)(2,1)S(1)}, bf16[4,256,256]{2,1,0:T(8,128)(2,1)}, u32[]{:S(2)}) copy-start(bf16[4,256,256]{2,1,0:T(8,128)(2,1)} %get-tuple-element.114.y_ref) | copy-start | bytes 1572868
  45.1 2.0 %copy-start.9 = (bf16[2,32,512]{2,1,0:T(8,128)(2,1)S(1)}, bf16[2,32,512]{2,1,0:T(8,128)(2,1)}, u32[]{:S(2)}) copy-start(bf16[2,32,512]{2,1,0:T(8,128)(2,1)} %get-tuple-element.116.z_ref) | copy-start | bytes 196612
  46.7 1.8 %collective-permute-start.4 = (f16[656,128]{1,0:T(8,128)(2,1)S(1)}, f16[656,128]{1,0:T(8,128)(2,1)S(1)}, u32[]{:S(2)}, u32[]{:S(2)}) collective-permute-start(f16[656,128]{1,0:T(8,128)(2,1)S(1)} %convert_element_type.51), channel_id=1, source_target_pairs={{0,4},{1,5},{2,6},{3,7},{4,0},{5,1},{6,2},{7,3},{8,12},{9,13},{10,... | collective-permute-start | bytes 503816 | tf_op jit(solution)/shard_map/ppermute | solution.py:538
  49.4 4.9 %collective-permute-start.6 = (f32[128,128]{1,0:T(8,128)S(1)}, f32[128,128]{1,0:T(8,128)S(1)}, u32[]{:S(2)}, u32[]{:S(2)}) collective-permute-start(f32[128,128]{1,0:T(8,128)S(1)} %get-tuple-element.142.up_ref), channel_id=1, source_target_pairs={{0,1},{1,0},{2,3},{3,2},{4,5},{5,4},{6,7},{7,6},{8,9},{9,8},{10,11... | collective-permute-start | bytes 196616 | tf_op jit(solution)/shard_map/ppermute | solution.py:538
  51.4 2.9 %collective-permute-start.7 = (f32[128,128]{1,0:T(8,128)S(1)}, f32[128,128]{1,0:T(8,128)S(1)}, u32[]{:S(2)}, u32[]{:S(2)}) collective-permute-start(f32[128,128]{1,0:T(8,128)S(1)} %get-tuple-element.143.down_ref), channel_id=1, source_target_pairs={{0,4},{1,2},{2,1},{3,7},{4,0},{5,6},{6,5},{7,3},{8,12},{9,10},{10,... | collective-permute-start | bytes 196616 | tf_op jit(solution)/shard_map/ppermute | solution.py:542
  55.1 3.8 %collective-permute-start.8 = (f16[656,128]{1,0:T(8,128)(2,1)S(1)}, f16[656,128]{1,0:T(8,128)(2,1)S(1)}, u32[]{:S(2)}, u32[]{:S(2)}) collective-permute-start(f16[656,128]{1,0:T(8,128)(2,1)S(1)} %convert_element_type.55), channel_id=1, source_target_pairs={{0,4},{1,5},{2,6},{3,7},{4,0},{5,1},{6,2},{7,3},{8,12},{9,13},{10,... | collective-permute-start | bytes 503816 | tf_op jit(solution)/shard_map/ppermute | solution.py:538
  55.4 5.6 %collective-permute-start.9 = (f16[656,128]{1,0:T(8,128)(2,1)S(1)}, f16[656,128]{1,0:T(8,128)(2,1)S(1)}, u32[]{:S(2)}, u32[]{:S(2)}) collective-permute-start(f16[656,128]{1,0:T(8,128)(2,1)S(1)} %convert_element_type.55), channel_id=1, source_target_pairs={{0,1},{1,0},{2,3},{3,2},{4,8},{5,9},{6,10},{7,11},{8,4},{9,5},{10,... | collective-permute-start | bytes 503816 | tf_op jit(solution)/shard_map/ppermute | solution.py:542
  59.0 2.1 %copy-start.2 = (bf16[4,512,512]{2,1,0:T(8,128)(2,1)S(1)}, bf16[4,512,512]{2,1,0:T(8,128)(2,1)}, u32[]{:S(2)}) copy-start(bf16[4,512,512]{2,1,0:T(8,128)(2,1)} %get-tuple-element.107.refs_2_.ka_ref) | copy-start | bytes 6291460
  59.0 2.1 %copy-start.5 = (bf16[2,4,256,256]{3,2,1,0:T(8,128)(2,1)S(1)}, bf16[2,4,256,256]{3,2,1,0:T(8,128)(2,1)}, u32[]{:S(2)}) copy-start(bf16[2,4,256,256]{3,2,1,0:T(8,128)(2,1)} %get-tuple-element.109.refs_4_.xya_ref) | copy-start | bytes 3145732
  59.0 2.1 %copy-start.8 = (bf16[4,256,256]{2,1,0:T(8,128)(2,1)S(1)}, bf16[4,256,256]{2,1,0:T(8,128)(2,1)}, u32[]{:S(2)}) copy-start(bf16[4,256,256]{2,1,0:T(8,128)(2,1)} %get-tuple-element.108.refs_3_.ya_ref) | copy-start | bytes 1572868
  59.1 2.1 %copy-start.11 = (bf16[2,32,512]{2,1,0:T(8,128)(2,1)S(1)}, bf16[2,32,512]{2,1,0:T(8,128)(2,1)}, u32[]{:S(2)}) copy-start(bf16[2,32,512]{2,1,0:T(8,128)(2,1)} %get-tuple-element.110.refs_5_.za_ref) | copy-start | bytes 196612
  64.6 5.4 %collective-permute-start.11 = (f16[656,128]{1,0:T(8,128)(2,1)S(1)}, f16[656,128]{1,0:T(8,128)(2,1)S(1)}, u32[]{:S(2)}, u32[]{:S(2)}) collective-permute-start(f16[656,128]{1,0:T(8,128)(2,1)S(1)} %convert_element_type.60), channel_id=1, source_target_pairs={{0,1},{1,0},{2,3},{3,2},{4,8},{5,9},{6,10},{7,11},{8,4},{9,5},{10,... | collective-permute-start | bytes 503816 | tf_op jit(solution)/shard_map/ppermute | solution.py:542
  67.8 2.3 %collective-permute-start.10 = (f16[656,128]{1,0:T(8,128)(2,1)S(1)}, f16[656,128]{1,0:T(8,128)(2,1)S(1)}, u32[]{:S(2)}, u32[]{:S(2)}) collective-permute-start(f16[656,128]{1,0:T(8,128)(2,1)S(1)} %convert_element_type.58), channel_id=1, source_target_pairs={{0,4},{1,5},{2,6},{3,7},{4,0},{5,1},{6,2},{7,3},{8,12},{9,13},{10,... | collective-permute-start | bytes 503816 | tf_op jit(solution)/shard_map/ppermute | solution.py:538
  70.2 4.3 %collective-permute-start.12 = (f32[64,128]{1,0:T(8,128)S(1)}, f32[64,128]{1,0:T(8,128)S(1)}, u32[]{:S(2)}, u32[]{:S(2)}) collective-permute-start(f32[64,128]{1,0:T(8,128)S(1)} %get-tuple-element.165), channel_id=1, source_target_pairs={{0,1},{1,0},{2,3},{3,2},{4,5},{5,4},{6,7},{7,6},{8,9},{9,8},{10,11... | collective-permute-start | bytes 98312 | tf_op jit(solution)/shard_map/ppermute | solution.py:538
  71.6 2.9 %collective-permute-start.13 = (f32[64,128]{1,0:T(8,128)S(1)}, f32[64,128]{1,0:T(8,128)S(1)}, u32[]{:S(2)}, u32[]{:S(2)}) collective-permute-start(f32[64,128]{1,0:T(8,128)S(1)} %get-tuple-element.166), channel_id=1, source_target_pairs={{0,4},{1,2},{2,1},{3,7},{4,0},{5,6},{6,5},{7,3},{8,12},{9,10},{10,... | collective-permute-start | bytes 98312 | tf_op jit(solution)/shard_map/ppermute | solution.py:542
